TPU v7x, 256 devices: a whole 4x4x8 slice. The times are simulated.
256 devices in a mesh: lat: 8 (over x, y_lo), lon: 16 (over z, core), tp: 2 (over y_hi).
Axes of the slice: x: 4, y: 4 (y_hi: 2, y_lo: 2; y = y_hi * 2 + y_lo), z: 8, core: 2. Of those that a mesh axis runs over, the one named last changes fastest.
Arguments:
- tokens: bfloat16 [2, 96, 768, 512], P('tp', 'lat', 'lon'), may hold values from -6 to 6
- labels: int32 [2, 96, 768], P(None, 'lat', 'lon'), may hold values from 0 to 2
- gain_one: float32 [512], replicated, may hold values from 0.5 to 2
- second_norm_gain: float32 [512], replicated, may hold values from 0.5 to 2
- w_qkv: bfloat16 [3, 512, 512], P(None, None, 'tp'), may hold values from -8 to 8
- w_out: bfloat16 [512, 512], P('tp'), may hold values from -0.25 to 0.25
- w_fc1: bfloat16 [512, 2048], P(None, 'tp'), may hold values from -0.25 to 0.25
- w_fc2: bfloat16 [2048, 512], P('tp'), may hold values from -0.125 to 0.125
- cotangent: bfloat16 [2, 96, 768, 512], P('tp', 'lat', 'lon'), may hold values from -0.119628906 to 0.119628906
Outputs:
- output: bfloat16 [2, 96, 768, 512], P('tp', 'lat', 'lon')
- grad_qkv: bfloat16 [3, 512, 512], P(None, None, 'tp')
- grad_out: bfloat16 [512, 512], P('tp')
- grad_fc1: bfloat16 [512, 2048], P(None, 'tp')
- grad_fc2: bfloat16 [2048, 512], P('tp')
All inputs are finite; a program needn't handle non-finite values.
Results may differ from a plain program's by a relative error of at most 0.024.
Values may be sent and summed in bfloat16 or wider, within the bound.
No kernel may reach another device: no remote copies, remote signals or barrier semaphores. Data moves between devices by JAX's collectives and lax.ppermute only.
A program may use at most 128 MiB of HBM per device.

v0:
```python
import functools

import jax
import jax.numpy as jnp
from jax import lax
from jax.experimental import pallas as pl
from jax.experimental.pallas import tpu as pltpu
from jax.sharding import Mesh
from jax.sharding import PartitionSpec as P

D = 512
FF = 2048
WLAT = 6
WLON = 12
SEATS = 144
WINS = 4
TOK = SEATS * WINS
EPS = 1e-05
GELU_C = 0.7978845608028654
BF = jnp.bfloat16
F32 = jnp.float32
AXES = ("x", "yl", "z", "c", "tp")
VMEM_LIMIT = 48 * 1024 * 1024


def pairs_of(move):
    pairs = []
    for x in range(4):
        for yl in range(2):
            for z in range(8):
                for c in range(2):
                    for t in range(2):
                        dest = move(x, yl, z, c, t)
                        if dest is not None:
                            pairs.append((rank(x, yl, z, c, t), rank(*dest)))
    return pairs


def rank(x, yl, z, c, t):
    return ((2 * x + yl) * 16 + 2 * z + c) * 2 + t


def send(value, move):
    return lax.ppermute(value, AXES, pairs_of(move))


def flip(value, x=0, yl=0, z=0, c=0, t=0):
    return send(value, lambda a, b, d, e, f: (a ^ x, b ^ yl, d ^ z, e ^ c, f ^ t))


def shift_lat(x, yl, step):
    lat = (2 * x + yl + step) % 8
    return lat // 2, lat % 2


def shift_lon(z, c, step):
    lon = (2 * z + c + step) % 16
    return lon // 2, lon % 2


def lon_move(step):
    def move(x, yl, z, c, t):
        zz, cc = shift_lon(z, c, step)
        return x, yl, zz, cc, t

    return move


def far_move(x, yl, z, c, t):
    if t == 1:
        return x, yl, z, c, 0
    xx, yy = shift_lat(x, yl, -1)
    return xx, yy, z, c, 1


def far_back(x, yl, z, c, t):
    if t == 0:
        return x, yl, z, c, 1
    xx, yy = shift_lat(x, yl, 1)
    return xx, yy, z, c, 0


def lat_move(step):
    def move(x, yl, z, c, t):
        if t == 0:
            return None
        xx, yy = shift_lat(x, yl, step)
        return xx, yy, z, c, t

    return move


def fence(values, after):
    n = len(values)
    anywhere = pl.BlockSpec(memory_space=pl.ANY)
    return pl.pallas_call(
        lambda *refs: None,
        out_shape=tuple(jax.ShapeDtypeStruct(v.shape, v.dtype) for v in values),
        in_specs=[anywhere] * (n + len(after)),
        out_specs=tuple([anywhere] * n),
        input_output_aliases={i: i for i in range(n)},
        name="fence",
    )(*values, *after)


def band_pieces(tile, t):
    first = t == 0
    return (
        jnp.where(first, tile[9:12], tile[3:6]),
        jnp.where(first, tile[0:3], tile[6:9]),
        tile[0:3],
    )


def exchange_rows(pieces):
    near, far, below = pieces
    return flip(near, t=1), send(far, far_move), send(below, lat_move(-1))


def first_columns(tile, near, far, below, t):
    edge = tile[:, :6]
    own = jnp.where(t == 0, edge[3:9], jnp.concatenate([edge[9:12], below[:, :6]], 0))
    return jnp.concatenate([own, near[:, :6], far[:, :6]], 0)


def to_windows(band):
    width = band.shape[-1]
    return band.reshape(12, WINS, WLON, width).transpose(1, 0, 2, 3).reshape(TOK, width)


def load_windows(t, tile, near, far, below, moved, stage, wins):
    for row in range(12):
        if row < 3:
            value = tile[3 + row + 6 * t].astype(F32)
        elif row < 6:
            value = jnp.where(t == 0, tile[3 + row].astype(F32), below[row - 3].astype(F32))
        elif row < 9:
            value = near[row - 6].astype(F32)
        else:
            value = far[row - 9].astype(F32)
        stage[row, 0:48] = value
        stage[row, 48:54] = moved[row].astype(F32)
        for w in range(WINS):
            start = w * SEATS + row * WLON
            wins[start : start + WLON, :] = stage[row, 6 + 12 * w : 18 + 12 * w]


def store_windows(wins, stage, band, tail):
    for row in range(12):
        for w in range(WINS):
            start = w * SEATS + row * WLON
            stage[row, 6 + 12 * w : 18 + 12 * w] = wins[start : start + WLON, :]
        band[row] = stage[row, 0:48].astype(BF)
        tail[row] = stage[row, 48:54].astype(BF)


def norm(value, gain):
    centered = value - jnp.mean(value, -1, keepdims=True)
    rstd = lax.rsqrt(jnp.mean(centered * centered, -1, keepdims=True) + EPS)
    xhat = centered * rstd
    return xhat * gain, xhat, rstd


def dot(a, b):
    return lax.dot_general(a, b, (((1,), (0,)), ((), ())), preferred_element_type=F32)


def dot_nt(a, b):
    return lax.dot_general(a, b, (((1,), (1,)), ((), ())), preferred_element_type=F32)


def dot_tn(a, b):
    return lax.dot_general(a, b, (((0,), (0,)), ((), ())), preferred_element_type=F32)


def head_mask(h):
    lane = lax.broadcasted_iota(jnp.int32, (1, 128), 1)
    return (lane < 64) if h == 0 else (lane >= 64)


def attend_kernel(
    place, tile, near, far, below, moved, labc, labr, g1, wq_own, wo_own, wqo_m, wqo_s,
    n1t_ref, qkv_ref, prob_ref, heads_ref, wo_full, mixed_ref, n1_scr, stage, wins,
):
    c = place[3]
    mine = pl.ds(pl.multiple_of(c * 256, 256), 256)
    sibs = pl.ds(pl.multiple_of((1 - c) * 256, 256), 256)
    load_windows(place[4], tile, near, far, below, moved, stage, wins)
    x = wins[...]
    normed = norm(x, g1[...])[0]
    n1_scr[...] = normed.astype(BF)
    n1t_ref[...] = normed.T.astype(BF)
    n1 = n1_scr[...]
    for i in range(3):
        scale = 0.125 if i == 0 else 1.0
        own = dot(n1, wq_own[i]).astype(BF)
        other = (dot(n1_scr[:, mine], wqo_m[i]) + dot(n1_scr[:, sibs], wqo_s[i])).astype(BF)
        qkv_ref[:, i * 512 : i * 512 + 256] = own * BF(scale)
        qkv_ref[:, i * 512 + 256 : i * 512 + 512] = other * BF(scale)

    def window(w, carry):
        rows = pl.ds(pl.multiple_of(w * SEATS, 16), SEATS)
        same = labc[rows, 0:1] == labr[w, 0:1, :]
        for p in range(4):
            q2 = qkv_ref[rows, p * 128 : p * 128 + 128]
            k2 = qkv_ref[rows, 512 + p * 128 : 640 + p * 128]
            v2 = qkv_ref[rows, 1024 + p * 128 : 1152 + p * 128]
            total = None
            for h in range(2):
                keep = head_mask(h)
                scores = dot_nt(jnp.where(keep, q2, BF(0)), k2)
                scores = jnp.where(same, scores, -1e30)
                expo = jnp.exp(scores - jnp.max(scores, -1, keepdims=True))
                prob = (expo * (1.0 / jnp.sum(expo, -1, keepdims=True))).astype(BF)
                prob_ref[w * 8 + p * 2 + h] = prob
                part = dot(prob, jnp.where(keep, v2, BF(0)))
                total = part if total is None else total + part
            heads_ref[rows, p * 128 : p * 128 + 128] = total.astype(BF)
        return carry

    lax.fori_loop(0, WINS, window, 0)
    wo_full[0:256, :] = wo_own[...]
    wo_full[256:512, mine] = wqo_m[3]
    wo_full[256:512, sibs] = wqo_s[3]
    attn = dot(heads_ref[...], wo_full[...]).astype(BF).astype(F32)
    mixed_ref[...] = (x + attn).astype(BF)


def gelu_parts(v):
    square = v * v
    tanh_v = jnp.tanh(GELU_C * v * (1.0 + 0.044715 * square))
    half = 0.5 * (1.0 + tanh_v)
    slope = half + 0.5 * v * (1.0 - tanh_v * tanh_v) * (GELU_C + (3.0 * 0.044715 * GELU_C) * square)
    return v * half, slope


def store_rows(out, block, lead, cols):
    for yl in range(2):
        for z in range(8):
            rows = slice(z * 32 + yl * 16, z * 32 + yl * 16 + 16)
            out[lead + (yl, z, slice(None), cols)] = block[rows].astype(BF)


def mlp_kernel(
    place, mixed_ref, tile, near, far, below, moved, g2, w1_own, w2_own, w12_m, w12_s,
    band, tail, dm_ref, keep, away,
    n2t, cott, hid_scr, dpre_scr, stage, wins,
):
    mx, c, mt = place[0], place[3], place[4]
    mine = pl.ds(pl.multiple_of(c * 256, 256), 256)
    sibs = pl.ds(pl.multiple_of((1 - c) * 256, 256), 256)
    load_windows(mt, tile, near, far, below, moved, stage, wins)
    gain = g2[...]
    mixed = mixed_ref[...].astype(F32)
    normed, xhat, rstd = norm(mixed, gain)
    n2 = normed.astype(BF)
    n2t[...] = normed.T.astype(BF)
    cott[...] = wins[...].T.astype(BF)
    cot = wins[...].astype(BF)
    blocks = [(0, x, w1_own, w2_own, x) for x in range(4)]
    for pair, half in ((w12_m, c), (w12_s, 1 - c)):
        blocks += [(1, 2 * half + i, pair.at[0], pair.at[1], i) for i in range(2)]
    for n, (t, x, w1, w2, i) in enumerate(blocks):
        cols = slice(i * 256, i * 256 + 256)
        place_cols = slice(n * 256, n * 256 + 256)
        hidden, slope = gelu_parts(dot(n2, w1[:, cols]))
        hidden = hidden.astype(BF)
        dpre = (dot_nt(cot, w2[cols, :]) * slope).astype(BF)
        hid_scr[:, place_cols] = hidden
        dpre_scr[:, place_cols] = dpre
        lead = (x ^ mx, t ^ mt)
        for rows, out in ((sibs, away), (mine, keep)):
            store_rows(out, dot(n2t[rows, :], dpre), lead, slice(0, 256))
            store_rows(out, dot(cott[rows, :], hidden), lead, slice(256, 512))
    d_norm = (
        dot_nt(dpre_scr[:, :1024], w1_own[...])
        + dot_nt(dpre_scr[:, 1024:1536], w12_m[0])
        + dot_nt(dpre_scr[:, 1536:], w12_s[0])
    )
    scaled = d_norm * gain
    dm = wins[...] + rstd * (
        scaled
        - jnp.mean(scaled, -1, keepdims=True)
        - xhat * jnp.mean(scaled * xhat, -1, keepdims=True)
    )
    dm_ref[...] = dm.astype(BF)
    wins[...] = mixed + (
        dot(hid_scr[:, :1024], w2_own[...])
        + dot(hid_scr[:, 1024:1536], w12_m[1])
        + dot(hid_scr[:, 1536:], w12_s[1])
    )
    store_windows(wins, stage, band, tail)


def attend_back_kernel(
    place, dm_ref, heads_ref, prob_ref, qkv_ref, n1t_ref, wo_full, first, second,
    keep, away,
    dmt, dheads, dqkv,
):
    mx, c, mt = place[0], place[3], place[4]
    mine = pl.ds(pl.multiple_of(c * 256, 256), 256)
    sibs = pl.ds(pl.multiple_of((1 - c) * 256, 256), 256)
    dm = dm_ref[...]
    dmt[...] = dm.astype(F32).T.astype(BF)
    dheads[...] = dot_nt(dm, wo_full[...]).astype(BF)

    def window(w, carry):
        rows = pl.ds(pl.multiple_of(w * SEATS, 16), SEATS)
        for p in range(4):
            pc = slice(p * 128, p * 128 + 128)
            q2 = qkv_ref[rows, p * 128 : p * 128 + 128]
            k2 = qkv_ref[rows, 512 + p * 128 : 640 + p * 128]
            v2 = qkv_ref[rows, 1024 + p * 128 : 1152 + p * 128]
            do2 = dheads[rows, pc]
            dq = dk = dv = None
            for h in range(2):
                keep = head_mask(h)
                prob_b = prob_ref[w * 8 + p * 2 + h]
                prob = prob_b.astype(F32)
                do_h = jnp.where(keep, do2, BF(0))
                d_prob = dot_nt(do_h, v2)
                moment = jnp.sum(prob * d_prob, -1, keepdims=True)
                d_scores = (prob * (d_prob - moment)).astype(BF)
                pq = dot(d_scores, jnp.where(keep, k2, BF(0)))
                pk = dot_tn(d_scores, jnp.where(keep, q2, BF(0)))
                pv = dot_tn(prob_b, do_h)
                dq = pq if dq is None else dq + pq
                dk = pk if dk is None else dk + pk
                dv = pv if dv is None else dv + pv
            dqkv[rows, p * 128 : p * 128 + 128] = (dq * 0.125).astype(BF)
            dqkv[rows, 512 + p * 128 : 640 + p * 128] = dk.astype(BF)
            dqkv[rows, 1024 + p * 128 : 1152 + p * 128] = dv.astype(BF)
        return carry

    lax.fori_loop(0, WINS, window, 0)
    for rows, out in ((sibs, away), (mine, keep)):
        for t in range(2):
            for half in range(2):
                for which in range(2):
                    if which == 0 or half == 0:
                        start = (2 * which + half) * 512 + t * 256
                        grad = dot(n1t_ref[rows, :], dqkv[:, start : start + 256])
                    else:
                        grad = dot(dmt[rows, :], heads_ref[:, t * 256 : t * 256 + 256])
                    for sub in range(2):
                        lead = ((half * 2 + sub) ^ mx, t ^ mt)
                        cols = slice(which * 128, which * 128 + 128)
                        store_rows(out, grad[:, sub * 128 : sub * 128 + 128], lead, cols)


def whole(shape, dtype=BF):
    return jax.ShapeDtypeStruct(shape, dtype)


def call(kernel, args, outs, scratch=(), place=None, flops=0, name=None, after=()):
    spec = pl.BlockSpec(memory_space=pltpu.VMEM)
    specs = [spec] * len(args) + [pl.BlockSpec(memory_space=pl.ANY)] * len(after)
    args = tuple(args) + tuple(after)
    if place is not None:
        args = (place,) + args
        specs = [pl.BlockSpec(memory_space=pltpu.SMEM)] + specs
    size = sum(a.size * a.dtype.itemsize for a in list(args) + list(outs))
    return pl.pallas_call(
        kernel,
        out_shape=tuple(outs),
        in_specs=specs,
        out_specs=tuple([spec] * len(outs)),
        scratch_shapes=list(scratch),
        compiler_params=pltpu.CompilerParams(vmem_limit_bytes=VMEM_LIMIT),
        cost_estimate=pl.CostEstimate(flops=flops, bytes_accessed=size, transcendentals=0),
        name=name,
    )(*args)


def add(*values):
    total = values[0].astype(F32)
    for value in values[1:]:
        total = total + value.astype(F32)
    return total.astype(BF)


def core_sum_kernel(keep, arrived, *outs):
    for x in range(4):
        outs[x][...] = add(keep[x], arrived[x])


def x_sum_kernel(*refs):
    fc, at, out = refs[0:4], refs[4:8], refs[-1]
    out[:, :, :, :, :512] = add(*[r[...] for r in fc])
    out[:, :, :, :, 512:] = add(*[r[...] for r in at])


def last_sum_kernel(parts, out):
    total = parts[0].astype(F32)
    for i in range(1, 32):
        total = total + parts[i].astype(F32)
    for z in range(8):
        out[z] = total.astype(BF)


def copies_kernel(part, out):
    for i in range(8):
        out[i] = part[...]


def place_kernel(place, mine, sib, gq, go, g1, g2, scr2, scro):
    c = place[3]
    for src, cc in ((mine, c), (sib, 1 - c)):
        base = cc * 256
        for yl in range(2):
            for x in range(4):
                for z in range(8):
                    rows = pl.ds(pl.multiple_of(base + z * 32 + yl * 16, 16), 16)
                    chunk = src[2 * x + yl, z]
                    lo = (x % 2) * 128
                    g1[rows, x * 256 : x * 256 + 256] = chunk[:, :256]
                    scr2[rows, x * 256 : x * 256 + 256] = chunk[:, 256:512]
                    gq[x // 2, rows, lo : lo + 128] = chunk[:, 512:640]
                    if x < 2:
                        gq[2, rows, lo : lo + 128] = chunk[:, 640:]
                    else:
                        scro[rows, lo : lo + 128] = chunk[:, 640:]
    for i in range(4):
        g2[i * 256 : i * 256 + 256, :] = scr2[:, i * 256 : i * 256 + 256].astype(F32).T.astype(BF)
    go[...] = scro[...].astype(F32).T.astype(BF)


def core_phase(keep, away, width):
    outs = [whole((2, 2, 8, 16, width))] * 4
    return call(core_sum_kernel, (keep, flip(away, c=1)), outs, name="core_sum")


def x_phase(cut):
    return [cut[0]] + [flip(cut[k], x=k) for k in (1, 2, 3)]


def reduce_and_gather(place, fc, at, after):
    (total,) = call(x_sum_kernel, (*fc, *at), [whole((2, 2, 8, 16, 768))], name="x_sum", after=after)
    parts = lax.all_to_all(total.reshape(32, 16, 768), ("tp", "yl", "z"), 0, 0)
    (chunks,) = call(last_sum_kernel, (parts,), [whole((8, 16, 768))], name="last_sum")
    column = lax.all_to_all(chunks, "z", 0, 0)
    (columns,) = call(copies_kernel, (column,), [whole((8, 8, 16, 768))], name="copies")
    mine = lax.all_to_all(columns, ("x", "yl"), 0, 0)
    sib = flip(mine, c=1)
    outs = [whole((3, 512, 256)), whole((256, 512)), whole((512, 1024)), whole((1024, 512))]
    scratch = [pltpu.VMEM((512, 1024), BF), pltpu.VMEM((512, 256), BF)]
    return call(place_kernel, (mine, sib), outs, scratch, place, name="place")


def per_device(tokens, labels, gain_one, second_norm_gain, w_qkv, w_out, w_fc1, w_fc2, cotangent):
    x, yl, z, c, t = [lax.axis_index(name) for name in AXES]
    place = jnp.stack([x, yl, z, c, t]).astype(jnp.int32)
    tile, cot = tokens[0], cotangent[0]

    rows = exchange_rows(band_pieces(tile, t))
    wqo = jnp.concatenate(
        [
            lax.dynamic_slice_in_dim(w_qkv, c * 256, 256, 1),
            lax.dynamic_slice_in_dim(w_out, c * 256, 256, 1)[None],
        ],
        0,
    )
    wqo = flip(wqo, yl=1, t=1)
    edge = first_columns(tile, *rows, t)
    moved = send(edge, lon_move(-1))

    w12 = jnp.stack(
        [
            lax.dynamic_slice_in_dim(w_fc1, c * 512, 512, 1),
            lax.dynamic_slice_in_dim(w_fc2, c * 512, 512, 0),
        ]
    )
    *pieces, w12 = fence((*band_pieces(cot, t), w12), (edge,))
    cot_rows = exchange_rows(pieces)
    w12 = flip(w12, yl=1, t=1)
    cot_edge = first_columns(cot, *cot_rows, t)
    cot_moved = send(cot_edge, lon_move(-1))
    wqo_sib = flip(wqo, c=1)

    band = lax.dynamic_slice_in_dim(labels, t * 6, 6, 1)
    band = jnp.where(t == 0, band, band[::-1]).reshape(12, 48, 1)
    lab = to_windows(band).reshape(TOK)
    labc = jnp.broadcast_to(lab[:, None], (TOK, 128))
    labr = jnp.broadcast_to(lab.reshape(WINS, 1, SEATS), (WINS, 8, SEATS))

    stage = [pltpu.VMEM((12, 56, D), F32), pltpu.VMEM((TOK, D), F32)]
    n1t, qkv, prob, heads, wo_full, mixed = call(
        without(attend_kernel, 13, 1),
        (tile, *rows, moved, labc, labr, gain_one[None], w_qkv, w_out, wqo, wqo_sib),
        [
            whole((D, TOK)), whole((TOK, 3 * D)), whole((WINS * 8, SEATS, SEATS)),
            whole((TOK, D)), whole((D, D)), whole((TOK, D)),
        ],
        [pltpu.VMEM((TOK, D), BF)] + stage,
        place,
        flops=3 * 10**9,
        name="attend",
        after=(cot_edge,),
    )
    w12_sib = flip(w12, c=1)
    grads = [whole((4, 2, 2, 8, 16, 512))] * 2
    out_band, tail, dm, *fc = call(
        mlp_kernel,
        (mixed, cot, *cot_rows, cot_moved, second_norm_gain[None], w_fc1, w_fc2, w12, w12_sib),
        [whole((12, 48, D)), whole((12, 6, D)), whole((TOK, D))] + grads,
        [
            pltpu.VMEM((D, TOK), BF), pltpu.VMEM((D, TOK), BF),
            pltpu.VMEM((TOK, FF), BF), pltpu.VMEM((TOK, FF), BF),
        ]
        + stage,
        place,
        flops=8 * 10**9,
        name="mlp",
    )
    fc_cut = core_phase(*fc, 512)
    out_moved = send(tail, lon_move(1))
    fc_parts = x_phase(fc_cut)
    grads = [whole((4, 2, 2, 8, 16, 256))] * 2
    at = call(
        attend_back_kernel,
        (dm, heads, prob, qkv, n1t, wo_full),
        grads,
        [pltpu.VMEM((D, TOK), BF), pltpu.VMEM((TOK, D), BF), pltpu.VMEM((TOK, 3 * D), BF)],
        place,
        flops=5 * 10**9,
        name="attend_back",
        after=(fc_cut[0], out_moved),
    )
    at_cut = core_phase(*at, 256)
    at_parts = x_phase(at_cut)

    out = jnp.concatenate([out_moved, out_band[:, 6:]], 1)
    near, far, above = fence((out[6:9], out[9:12], out[3:6]), (at_cut[0],))
    near, far, above = flip(near, t=1), send(far, far_back), send(above, lat_move(1))
    gq, go, g1, g2 = reduce_and_gather(place, fc_parts, at_parts, (near, far, above))
    out = jnp.where(
        t == 0,
        jnp.concatenate([far, out[0:6], near], 0),
        jnp.concatenate([above, near, far, out[0:3]], 0),
    )
    return out[None], gq, go, g1, g2


def without(kernel, start, count):
    return lambda *refs: kernel(*refs[:start], *refs[start + count :])


def solution(mesh):
    fine = Mesh(mesh.devices.reshape(4, 2, 8, 2, 2), AXES)
    lat, lon = ("x", "yl"), ("z", "c")
    return jax.shard_map(
        per_device,
        mesh=fine,
        in_specs=(
            P("tp", lat, lon, None),
            P(None, lat, lon),
            P(),
            P(),
            P(None, None, "tp"),
            P("tp", None),
            P(None, "tp"),
            P("tp", None),
            P("tp", lat, lon, None),
        ),
        out_specs=(
            P("tp", lat, lon, None),
            P(None, None, "tp"),
            P("tp", None),
            P(None, "tp"),
            P("tp", None),
        ),
        check_vma=False,
    )
```

profile of v0, /device:TPU:1, one launch (start us, length us, event | category | flops | bytes accessed | tf_op | source)
XLA Modules:
  0.0 241.7 jit_solution(17845559026855286074)
XLA Ops:
  1.8 5.8 %collective-permute-start.1 = (bf16[3,48,512]{2,1,0:T(8,128)(2,1)S(1)}, bf16[3,48,512]{2,1,0:T(8,128)(2,1)S(1)}, u32[]{:S(2)}, u32[]{:S(2)}) collective-permute-start(bf16[3,48,512]{2,1,0:T(8,128)(2,1)S(1)} %bitcast_select_fusion.1), channel_id=1, source_target_pairs={{0,225},{1,0},{2,227},{3,2},{4,229},{5,4},{6,231},{7,6},{8,233},{9... | collective-permute-start | bytes 442376 | tf_op jit(solution)/shard_map/ppermute | solution.py:44
  10.1 3.5 %collective-permute-start = (bf16[3,48,512]{2,1,0:T(8,128)(2,1)}, bf16[3,48,512]{2,1,0:T(8,128)(2,1)}, u32[]{:S(2)}, u32[]{:S(2)}) collective-permute-start(bf16[3,48,512]{2,1,0:T(8,128)(2,1)} %get-tuple-element.76), channel_id=1, source_target_pairs={{0,1},{1,0},{2,3},{3,2},{4,5},{5,4},{6,7},{7,6},{8,9},{9,8},{10,11... | collective-permute-start | bytes 442376 | tf_op jit(solution)/shard_map/ppermute | solution.py:44
  23.0 2.7 %collective-permute-start.4 = (bf16[4,256,256]{2,1,0:T(8,128)(2,1)}, bf16[4,256,256]{2,1,0:T(8,128)(2,1)}, u32[]{:S(2)}, u32[]{:S(2)}) collective-permute-start(bf16[4,256,256]{2,1,0:T(8,128)(2,1)} %pad_maximum_fusion.1), channel_id=1, source_target_pairs={{0,33},{1,32},{2,35},{3,34},{4,37},{5,36},{6,39},{7,38},{8,41},{9,... | collective-permute-start | bytes 1572872 | tf_op jit(solution)/shard_map/ppermute | solution.py:44
  25.7 20.2 %collective-permute-done.10.w12_m = bf16[2,512,512]{2,1,0:T(8,128)(2,1)} collective-permute-done((bf16[2,512,512]{2,1,0:T(8,128)(2,1)}, bf16[2,512,512]{2,1,0:T(8,128)(2,1)}, u32[]{:S(2)}, u32[]{:S(2)}) %collective-permute-start.10) | collective-permute-done | bytes 1048608 | tf_op jit(solution)/shard_map/ppermute | solution.py:44
  45.9 4.3 %collective-permute-start.11 = (bf16[2,512,512]{2,1,0:T(8,128)(2,1)}, bf16[2,512,512]{2,1,0:T(8,128)(2,1)}, u32[]{:S(2)}, u32[]{:S(2)}) collective-permute-start(bf16[2,512,512]{2,1,0:T(8,128)(2,1)} %collective-permute-done.10.w12_m), channel_id=1, source_target_pairs={{0,2},{1,3},{2,0},{3,1},{4,6},{5,7},{6,4},{7,5},{8,10},{9,11},{10,... | collective-permute-start | bytes 3145736 | tf_op jit(solution)/shard_map/ppermute | solution.py:44
  53.5 2.5 %collective-permute-start.7 = (bf16[3,48,512]{2,1,0:T(8,128)(2,1)}, bf16[3,48,512]{2,1,0:T(8,128)(2,1)}, u32[]{:S(2)}, u32[]{:S(2)}) collective-permute-start(bf16[3,48,512]{2,1,0:T(8,128)(2,1)} %get-tuple-element.38), channel_id=1, source_target_pairs={{0,1},{1,0},{2,3},{3,2},{4,5},{5,4},{6,7},{7,6},{8,9},{9,8},{10,11... | collective-permute-start | bytes 442376 | tf_op jit(solution)/shard_map/ppermute | solution.py:44
  57.1 5.3 %collective-permute-start.5 = (bf16[4,256,256]{2,1,0:T(8,128)(2,1)}, bf16[4,256,256]{2,1,0:T(8,128)(2,1)}, u32[]{:S(2)}, u32[]{:S(2)}) collective-permute-start(bf16[4,256,256]{2,1,0:T(8,128)(2,1)} %collective-permute-done.4.refs_11_), channel_id=1, source_target_pairs={{0,2},{1,3},{2,0},{3,1},{4,6},{5,7},{6,4},{7,5},{8,10},{9,11},{10,... | collective-permute-start | bytes 1572872 | tf_op jit(solution)/shard_map/ppermute | solution.py:44
  70.6 6.0 %collective-permute-start.9 = (bf16[12,6,512]{2,1,0:T(8,128)(2,1)S(1)}, bf16[12,6,512]{2,1,0:T(8,128)(2,1)S(1)}, u32[]{:S(2)}, u32[]{:S(2)}) collective-permute-start(bf16[12,6,512]{2,1,0:T(8,128)(2,1)S(1)} %pad_maximum_fusion.4.refs_13_), channel_id=1, source_target_pairs={{0,30},{1,31},{2,0},{3,1},{4,2},{5,3},{6,4},{7,5},{8,6},{9,7},{10,... | collective-permute-start | bytes 221192 | tf_op jit(solution)/shard_map/ppermute | solution.py:44
  79.7 9.0 %attend.1 = (bf16[512,576]{1,0:T(8,128)(2,1)S(1)}, bf16[576,1536]{1,0:T(8,128)(2,1)}, bf16[32,144,144]{2,1,0:T(8,128)(2,1)}, bf16[576,512]{1,0:T(8,128)(2,1)S(1)...) custom-call(s32[5]{0:T(128)S(1)} %stack.32.refs_0_.place, bf16[12,48,512]{2,1,0:T(8,128)(2,1)S(1)} %bitcast.47, ...), custom_call_target="tpu_custom_call" | custom-call | flops 3000000000 | bytes 8982548 | tf_op jit(solution)/shard_map/attend/pallas_call | solution.py:363
  88.7 13.1 %mlp.1 = (bf16[12,48,512]{2,1,0:T(8,128)(2,1)S(1)}, bf16[12,6,512]{2,1,0:T(8,128)(2,1)S(1)}, bf16[576,512]{1,0:T(8,128)(2,1)S(1)}, bf16[4,2,2,8,16,512]{5,4,3,2,...) custom-call(s32[5]{0:T(128)S(1)} %stack.32.refs_0_.place, bf16[576,512]{1,0:T(8,128)(2,1)S(1)} %get-tuple-element.40.mixed_ref, ...), custom_call_target="tpu_custom_call" | custom-call | flops 8000000000 | bytes 11339796 | tf_op jit(solution)/shard_map/mlp/pallas_call | solution.py:363
  102.2 4.5 %collective-permute-done.13.arrived = bf16[4,2,2,8,16,512]{5,4,3,2,1,0:T(8,128)(2,1)S(1)} collective-permute-done((bf16[4,2,2,8,16,512]{5,4,3,2,1,0:T(8,128)(2,1)}, bf16[4,2,2,8,16,512]{5,4,3,2,1,0:T(8,128)(2,1)S(1)}, u32[]{:S(2)}, u32[]{:S(2)}) %collective-permute-start.13) | collective-permute-done | bytes 2097184 | tf_op jit(solution)/shard_map/ppermute | solution.py:44
  109.6 2.8 %core_sum.2 = (bf16[2,2,8,16,512]{4,3,2,1,0:T(8,128)(2,1)S(1)}, bf16[2,2,8,16,512]{4,3,2,1,0:T(8,128)(2,1)}, bf16[2,2,8,16,512]{4,3,2,1,0:T(8,128)(2,1)}, bf16[2,2,8,16,512]{4,3,2,1,0:T(8,128)(2,1)}) custom-call(bf16[4,2,2,8,16,512]{5,4,3,2,1,0:T(8,128)(2,1)S(1)} %copy-done, bf16[4,2,2,8,16,512]{5,4,3,2,1,0:T(8,128)(2,1)} %copy-done.17), custom_call_target="tpu_custom_call" | custom-call | bytes 6291456 | tf_op jit(solution)/shard_map/core_sum/pallas_call | solution.py:363
  112.5 12.2 %attend_back.1 = (bf16[4,2,2,8,16,256]{5,4,3,2,1,0:T(8,128)(2,1)S(1)}, bf16[4,2,2,8,16,256]{5,4,3,2,1,0:T(8,128)(2,1)S(1)}) custom-call(s32[5]{0:T(128)S(1)} %stack.32.refs_0_.place, bf16[576,512]{1,0:T(8,128)(2,1)S(1)} %get-tuple-element.44.dm_ref, bf16[576,512]{1,0:T(8,128)(2,1)S(1)} %get-tuple-element.45.heads_ref, ...), custom_call_target="tpu_custom_call" | custom-call | flops 5000000000 | bytes 8085524 | tf_op jit(solution)/shard_map/attend_back/pallas_call | solution.py:363
  126.5 2.4 collective-permute-start.20
  130.9 7.4 %collective-permute-done.18.refs_1_ = bf16[2,2,8,16,512]{4,3,2,1,0:T(8,128)(2,1)S(1)} collective-permute-done((bf16[2,2,8,16,512]{4,3,2,1,0:T(8,128)(2,1)}, bf16[2,2,8,16,512]{4,3,2,1,0:T(8,128)(2,1)S(1)}, u32[]{:S(2)}, u32[]{:S(2)}) %collective-permute-start.18) | collective-permute-done | bytes 524320 | tf_op jit(solution)/shard_map/ppermute | solution.py:44
  139.8 10.1 %collective-permute-done.19.refs_2_ = bf16[2,2,8,16,512]{4,3,2,1,0:T(8,128)(2,1)S(1)} collective-permute-done((bf16[2,2,8,16,512]{4,3,2,1,0:T(8,128)(2,1)}, bf16[2,2,8,16,512]{4,3,2,1,0:T(8,128)(2,1)S(1)}, u32[]{:S(2)}, u32[]{:S(2)}) %collective-permute-start.19) | collective-permute-done | bytes 524320 | tf_op jit(solution)/shard_map/ppermute | solution.py:44
  149.9 2.1 collective-permute-start.23
  152.0 6.8 %collective-permute-done.15.refs_9_ = bf16[3,48,512]{2,1,0:T(8,128)(2,1)S(1)} collective-permute-done((bf16[3,48,512]{2,1,0:T(8,128)(2,1)}, bf16[3,48,512]{2,1,0:T(8,128)(2,1)S(1)}, u32[]{:S(2)}, u32[]{:S(2)}) %collective-permute-start.15) | collective-permute-done | bytes 147488 | tf_op jit(solution)/shard_map/ppermute | solution.py:44
  161.2 2.0 collective-permute-done.23.refs_7_
  164.6 32.7 %all_to_all.15.parts = bf16[32,16,768]{2,1,0:T(8,128)(2,1)S(1)} all-to-all(bf16[32,16,768]{2,1,0:T(8,128)(2,1)S(1)} %bitcast.44), channel_id=1, replica_groups=mesh['x'=4,'yl'=2,'z'=8,'c'=2,'tp'=2] {'tp','yl','z'}, dimensions={0} | all-to-all | bytes 1572864 | tf_op jit(solution)/shard_map/all_to_all | solution.py:439
  197.4 13.6 %all_to_all.16.part = bf16[8,16,768]{2,1,0:T(8,128)(2,1)S(1)} all-to-all(bf16[8,16,768]{2,1,0:T(8,128)(2,1)S(1)} %last_sum.1), channel_id=1, replica_groups=mesh['x'=4,'yl'=2,'z'=8,'c'=2,'tp'=2] {'z'}, dimensions={0} | all-to-all | bytes 393216 | tf_op jit(solution)/shard_map/all_to_all | solution.py:441
  211.2 18.3 %all_to_all.17.mine = bf16[8,8,16,768]{3,2,1,0:T(8,128)(2,1)S(1)} all-to-all(bf16[8,8,16,768]{3,2,1,0:T(8,128)(2,1)S(1)} %copies.1), channel_id=1, replica_groups=mesh['x'=4,'yl'=2,'z'=8,'c'=2,'tp'=2] {'x','yl'}, dimensions={0} | all-to-all | bytes 3145728 | tf_op jit(solution)/shard_map/all_to_all | solution.py:443
  229.5 6.3 %collective-permute-start.24 = (bf16[8,8,16,768]{3,2,1,0:T(8,128)(2,1)S(1)}, bf16[8,8,16,768]{3,2,1,0:T(8,128)(2,1)S(1)}, u32[]{:S(2)}, u32[]{:S(2)}) collective-permute-start(bf16[8,8,16,768]{3,2,1,0:T(8,128)(2,1)S(1)} %all_to_all.17.mine), channel_id=1, source_target_pairs={{0,2},{1,3},{2,0},{3,1},{4,6},{5,7},{6,4},{7,5},{8,10},{9,11},{10,... | collective-permute-start | bytes 4718600 | tf_op jit(solution)/shard_map/ppermute | solution.py:44
  238.8 2.8 %place.1 = (bf16[3,512,256]{2,1,0:T(8,128)(2,1)}, bf16[256,512]{1,0:T(8,128)(2,1)}, bf16[512,1024]{1,0:T(8,128)(2,1)}, bf16[1024,512]{1,0:T(8,128)(2,1)}) custom-call(s32[5]{0:T(128)S(1)} %stack.32.refs_0_.place, bf16[8,8,16,768]{3,2,1,0:T(8,128)(2,1)S(1)} %all_to_all.17.mine, bf16[8,8,16,768]{3,2,1,0:T(8,128)(2,1)S(1)} %collective-permute-done.24.sib), custom_call_target="tpu_custom_call" | custom-call | bytes 6291476 | tf_op jit(solution)/shard_map/place/pallas_call | solution.py:363
  (112 shorter events, 44.2 us)
Async XLA Ops:
  1.8 16.4 %collective-permute-start.1 = (bf16[3,48,512]{2,1,0:T(8,128)(2,1)S(1)}, bf16[3,48,512]{2,1,0:T(8,128)(2,1)S(1)}, u32[]{:S(2)}, u32[]{:S(2)}) collective-permute-start(bf16[3,48,512]{2,1,0:T(8,128)(2,1)S(1)} %bitcast_select_fusion.1), channel_id=1, source_target_pairs={{0,225},{1,0},{2,227},{3,2},{4,229},{5,4},{6,231},{7,6},{8,233},{9... | collective-permute-start | bytes 442376 | tf_op jit(solution)/shard_map/ppermute | solution.py:44
  9.4 9.5 %collective-permute-start.2 = (bf16[3,48,512]{2,1,0:T(8,128)(2,1)S(1)}, bf16[3,48,512]{2,1,0:T(8,128)(2,1)S(1)}, u32[]{:S(2)}, u32[]{:S(2)}) collective-permute-start(bf16[3,48,512]{2,1,0:T(8,128)(2,1)S(1)} %get-tuple-element.75), channel_id=1, source_target_pairs={{1,225},{3,227},{5,229},{7,231},{9,233},{11,235},{13,237},{15,239}... | collective-permute-start | bytes 442376 | tf_op jit(solution)/shard_map/ppermute | solution.py:44
  10.1 9.6 %collective-permute-start = (bf16[3,48,512]{2,1,0:T(8,128)(2,1)}, bf16[3,48,512]{2,1,0:T(8,128)(2,1)}, u32[]{:S(2)}, u32[]{:S(2)}) collective-permute-start(bf16[3,48,512]{2,1,0:T(8,128)(2,1)} %get-tuple-element.76), channel_id=1, source_target_pairs={{0,1},{1,0},{2,3},{3,2},{4,5},{5,4},{6,7},{7,6},{8,9},{9,8},{10,11... | collective-permute-start | bytes 442376 | tf_op jit(solution)/shard_map/ppermute | solution.py:44
  21.1 24.8 %collective-permute-start.10 = (bf16[2,512,512]{2,1,0:T(8,128)(2,1)}, bf16[2,512,512]{2,1,0:T(8,128)(2,1)}, u32[]{:S(2)}, u32[]{:S(2)}) collective-permute-start(bf16[2,512,512]{2,1,0:T(8,128)(2,1)} %get-tuple-element.41), channel_id=1, source_target_pairs={{0,33},{1,32},{2,35},{3,34},{4,37},{5,36},{6,39},{7,38},{8,41},{9,... | collective-permute-start | bytes 3145736 | tf_op jit(solution)/shard_map/ppermute | solution.py:44
  23.0 34.1 %collective-permute-start.4 = (bf16[4,256,256]{2,1,0:T(8,128)(2,1)}, bf16[4,256,256]{2,1,0:T(8,128)(2,1)}, u32[]{:S(2)}, u32[]{:S(2)}) collective-permute-start(bf16[4,256,256]{2,1,0:T(8,128)(2,1)} %pad_maximum_fusion.1), channel_id=1, source_target_pairs={{0,33},{1,32},{2,35},{3,34},{4,37},{5,36},{6,39},{7,38},{8,41},{9,... | collective-permute-start | bytes 1572872 | tf_op jit(solution)/shard_map/ppermute | solution.py:44
  45.9 42.8 %collective-permute-start.11 = (bf16[2,512,512]{2,1,0:T(8,128)(2,1)}, bf16[2,512,512]{2,1,0:T(8,128)(2,1)}, u32[]{:S(2)}, u32[]{:S(2)}) collective-permute-start(bf16[2,512,512]{2,1,0:T(8,128)(2,1)} %collective-permute-done.10.w12_m), channel_id=1, source_target_pairs={{0,2},{1,3},{2,0},{3,1},{4,6},{5,7},{6,4},{7,5},{8,10},{9,11},{10,... | collective-permute-start | bytes 3145736 | tf_op jit(solution)/shard_map/ppermute | solution.py:44
  52.2 15.4 %collective-permute-start.6 = (bf16[3,48,512]{2,1,0:T(8,128)(2,1)}, bf16[3,48,512]{2,1,0:T(8,128)(2,1)}, u32[]{:S(2)}, u32[]{:S(2)}) collective-permute-start(bf16[3,48,512]{2,1,0:T(8,128)(2,1)} %get-tuple-element.37), channel_id=1, source_target_pairs={{1,225},{3,227},{5,229},{7,231},{9,233},{11,235},{13,237},{15,239}... | collective-permute-start | bytes 442376 | tf_op jit(solution)/shard_map/ppermute | solution.py:44
  53.5 14.9 %collective-permute-start.7 = (bf16[3,48,512]{2,1,0:T(8,128)(2,1)}, bf16[3,48,512]{2,1,0:T(8,128)(2,1)}, u32[]{:S(2)}, u32[]{:S(2)}) collective-permute-start(bf16[3,48,512]{2,1,0:T(8,128)(2,1)} %get-tuple-element.38), channel_id=1, source_target_pairs={{0,1},{1,0},{2,3},{3,2},{4,5},{5,4},{6,7},{7,6},{8,9},{9,8},{10,11... | collective-permute-start | bytes 442376 | tf_op jit(solution)/shard_map/ppermute | solution.py:44
  56.0 13.1 %collective-permute-start.8 = (bf16[3,48,512]{2,1,0:T(8,128)(2,1)}, bf16[3,48,512]{2,1,0:T(8,128)(2,1)}, u32[]{:S(2)}, u32[]{:S(2)}) collective-permute-start(bf16[3,48,512]{2,1,0:T(8,128)(2,1)} %get-tuple-element.39), channel_id=1, source_target_pairs={{0,225},{1,0},{2,227},{3,2},{4,229},{5,4},{6,231},{7,6},{8,233},{9... | collective-permute-start | bytes 442376 | tf_op jit(solution)/shard_map/ppermute | solution.py:44
  57.1 19.5 %collective-permute-start.5 = (bf16[4,256,256]{2,1,0:T(8,128)(2,1)}, bf16[4,256,256]{2,1,0:T(8,128)(2,1)}, u32[]{:S(2)}, u32[]{:S(2)}) collective-permute-start(bf16[4,256,256]{2,1,0:T(8,128)(2,1)} %collective-permute-done.4.refs_11_), channel_id=1, source_target_pairs={{0,2},{1,3},{2,0},{3,1},{4,6},{5,7},{6,4},{7,5},{8,10},{9,11},{10,... | collective-permute-start | bytes 1572872 | tf_op jit(solution)/shard_map/ppermute | solution.py:44
  67.6 9.0 %collective-permute-start.3 = (bf16[12,6,512]{2,1,0:T(8,128)(2,1)}, bf16[12,6,512]{2,1,0:T(8,128)(2,1)S(1)}, u32[]{:S(2)}, u32[]{:S(2)}) collective-permute-start(bf16[12,6,512]{2,1,0:T(8,128)(2,1)} %pad_maximum_fusion.3.refs_4_), channel_id=1, source_target_pairs={{0,30},{1,31},{2,0},{3,1},{4,2},{5,3},{6,4},{7,5},{8,6},{9,7},{10,... | collective-permute-start | bytes 221192 | tf_op jit(solution)/shard_map/ppermute | solution.py:44
  70.6 18.1 %collective-permute-start.9 = (bf16[12,6,512]{2,1,0:T(8,128)(2,1)S(1)}, bf16[12,6,512]{2,1,0:T(8,128)(2,1)S(1)}, u32[]{:S(2)}, u32[]{:S(2)}) collective-permute-start(bf16[12,6,512]{2,1,0:T(8,128)(2,1)S(1)} %pad_maximum_fusion.4.refs_13_), channel_id=1, source_target_pairs={{0,30},{1,31},{2,0},{3,1},{4,2},{5,3},{6,4},{7,5},{8,6},{9,7},{10,... | collective-permute-start | bytes 221192 | tf_op jit(solution)/shard_map/ppermute | solution.py:44
  101.9 4.8 %collective-permute-start.13 = (bf16[4,2,2,8,16,512]{5,4,3,2,1,0:T(8,128)(2,1)}, bf16[4,2,2,8,16,512]{5,4,3,2,1,0:T(8,128)(2,1)S(1)}, u32[]{:S(2)}, u32[]{:S(2)}) collective-permute-start(bf16[4,2,2,8,16,512]{5,4,3,2,1,0:T(8,128)(2,1)} %get-tuple-element.51), channel_id=1, source_target_pairs={{0,2},{1,3},{2,0},{3,1},{4,6},{5,7},{6,4},{7,5},{8,10},{9,11},{10,... | collective-permute-start | bytes 6291464 | tf_op jit(solution)/shard_map/ppermute | solution.py:44
  102.2 10.3 %collective-permute-start.12 = (bf16[12,6,512]{2,1,0:T(8,128)(2,1)S(1)}, bf16[12,6,512]{2,1,0:T(8,128)(2,1)S(1)}, u32[]{:S(2)}, u32[]{:S(2)}) collective-permute-start(bf16[12,6,512]{2,1,0:T(8,128)(2,1)S(1)} %get-tuple-element.42), channel_id=1, source_target_pairs={{0,2},{1,3},{2,4},{3,5},{4,6},{5,7},{6,8},{7,9},{8,10},{9,11},{10,... | collective-permute-start | bytes 221192 | tf_op jit(solution)/shard_map/ppermute | solution.py:44
  124.7 5.2 %collective-permute-start.14 = (bf16[4,2,2,8,16,256]{5,4,3,2,1,0:T(8,128)(2,1)S(1)}, bf16[4,2,2,8,16,256]{5,4,3,2,1,0:T(8,128)(2,1)S(1)}, u32[]{:S(2)}, u32[]{:S(2)}) collective-permute-start(bf16[4,2,2,8,16,256]{5,4,3,2,1,0:T(8,128)(2,1)S(1)} %get-tuple-element.54), channel_id=1, source_target_pairs={{0,2},{1,3},{2,0},{3,1},{4,6},{5,7},{6,4},{7,5},{8,10},{9,11},{10,... | collective-permute-start | bytes 3145736 | tf_op jit(solution)/shard_map/ppermute | solution.py:44
  125.0 13.4 %collective-permute-start.18 = (bf16[2,2,8,16,512]{4,3,2,1,0:T(8,128)(2,1)}, bf16[2,2,8,16,512]{4,3,2,1,0:T(8,128)(2,1)S(1)}, u32[]{:S(2)}, u32[]{:S(2)}) collective-permute-start(bf16[2,2,8,16,512]{4,3,2,1,0:T(8,128)(2,1)} %get-tuple-element.59), channel_id=1, source_target_pairs={{0,64},{1,65},{2,66},{3,67},{4,68},{5,69},{6,70},{7,71},{8,72},{9,... | collective-permute-start | bytes 1572872 | tf_op jit(solution)/shard_map/ppermute | solution.py:44
  125.0 24.9 %collective-permute-start.19 = (bf16[2,2,8,16,512]{4,3,2,1,0:T(8,128)(2,1)}, bf16[2,2,8,16,512]{4,3,2,1,0:T(8,128)(2,1)S(1)}, u32[]{:S(2)}, u32[]{:S(2)}) collective-permute-start(bf16[2,2,8,16,512]{4,3,2,1,0:T(8,128)(2,1)} %get-tuple-element.60), channel_id=1, source_target_pairs={{0,128},{1,129},{2,130},{3,131},{4,132},{5,133},{6,134},{7,135},{8... | collective-permute-start | bytes 1572872 | tf_op jit(solution)/shard_map/ppermute | solution.py:44
  126.5 25.5 %collective-permute-start.20 = (bf16[2,2,8,16,512]{4,3,2,1,0:T(8,128)(2,1)}, bf16[2,2,8,16,512]{4,3,2,1,0:T(8,128)(2,1)S(1)}, u32[]{:S(2)}, u32[]{:S(2)}) collective-permute-start(bf16[2,2,8,16,512]{4,3,2,1,0:T(8,128)(2,1)} %get-tuple-element.61), channel_id=1, source_target_pairs={{0,192},{1,193},{2,194},{3,195},{4,196},{5,197},{6,198},{7,199},{8... | collective-permute-start | bytes 1572872 | tf_op jit(solution)/shard_map/ppermute | solution.py:44
  130.9 27.9 %collective-permute-start.15 = (bf16[3,48,512]{2,1,0:T(8,128)(2,1)}, bf16[3,48,512]{2,1,0:T(8,128)(2,1)S(1)}, u32[]{:S(2)}, u32[]{:S(2)}) collective-permute-start(bf16[3,48,512]{2,1,0:T(8,128)(2,1)} %get-tuple-element.56), channel_id=1, source_target_pairs={{0,1},{1,32},{2,3},{3,34},{4,5},{5,36},{6,7},{7,38},{8,9},{9,40},{... | collective-permute-start | bytes 442376 | tf_op jit(solution)/shard_map/ppermute | solution.py:44
  130.9 28.6 %collective-permute-start.21 = (bf16[2,2,8,16,256]{4,3,2,1,0:T(8,128)(2,1)S(1)}, bf16[2,2,8,16,256]{4,3,2,1,0:T(8,128)(2,1)S(1)}, u32[]{:S(2)}, u32[]{:S(2)}) collective-permute-start(bf16[2,2,8,16,256]{4,3,2,1,0:T(8,128)(2,1)S(1)} %get-tuple-element.62), channel_id=1, source_target_pairs={{0,64},{1,65},{2,66},{3,67},{4,68},{5,69},{6,70},{7,71},{8,72},{9,... | collective-permute-start | bytes 786440 | tf_op jit(solution)/shard_map/ppermute | solution.py:44
  138.3 22.9 %collective-permute-start.22 = (bf16[2,2,8,16,256]{4,3,2,1,0:T(8,128)(2,1)S(1)}, bf16[2,2,8,16,256]{4,3,2,1,0:T(8,128)(2,1)S(1)}, u32[]{:S(2)}, u32[]{:S(2)}) collective-permute-start(bf16[2,2,8,16,256]{4,3,2,1,0:T(8,128)(2,1)S(1)} %get-tuple-element.63), channel_id=1, source_target_pairs={{0,128},{1,129},{2,130},{3,131},{4,132},{5,133},{6,134},{7,135},{8... | collective-permute-start | bytes 786440 | tf_op jit(solution)/shard_map/ppermute | solution.py:44
  149.9 13.3 %collective-permute-start.23 = (bf16[2,2,8,16,256]{4,3,2,1,0:T(8,128)(2,1)S(1)}, bf16[2,2,8,16,256]{4,3,2,1,0:T(8,128)(2,1)S(1)}, u32[]{:S(2)}, u32[]{:S(2)}) collective-permute-start(bf16[2,2,8,16,256]{4,3,2,1,0:T(8,128)(2,1)S(1)} %get-tuple-element.64), channel_id=1, source_target_pairs={{0,192},{1,193},{2,194},{3,195},{4,196},{5,197},{6,198},{7,199},{8... | collective-permute-start | bytes 786440 | tf_op jit(solution)/shard_map/ppermute | solution.py:44
  152.0 7.5 %collective-permute-start.16 = (bf16[3,48,512]{2,1,0:T(8,128)(2,1)}, bf16[3,48,512]{2,1,0:T(8,128)(2,1)S(1)}, u32[]{:S(2)}, u32[]{:S(2)}) collective-permute-start(bf16[3,48,512]{2,1,0:T(8,128)(2,1)} %get-tuple-element.57), channel_id=1, source_target_pairs={{0,1},{1,0},{2,3},{3,2},{4,5},{5,4},{6,7},{7,6},{8,9},{9,8},{10,11... | collective-permute-start | bytes 442376 | tf_op jit(solution)/shard_map/ppermute | solution.py:44
  229.5 9.4 %collective-permute-start.24 = (bf16[8,8,16,768]{3,2,1,0:T(8,128)(2,1)S(1)}, bf16[8,8,16,768]{3,2,1,0:T(8,128)(2,1)S(1)}, u32[]{:S(2)}, u32[]{:S(2)}) collective-permute-start(bf16[8,8,16,768]{3,2,1,0:T(8,128)(2,1)S(1)} %all_to_all.17.mine), channel_id=1, source_target_pairs={{0,2},{1,3},{2,0},{3,1},{4,6},{5,7},{6,4},{7,5},{8,10},{9,11},{10,... | collective-permute-start | bytes 4718600 | tf_op jit(solution)/shard_map/ppermute | solution.py:44
  (19 other events, 199.2 us)
where the time goes:
time: 243 us; the launch traced here: 242 us
  blocking collectives  64.7 us (27%)
  waiting for transfers between devices  56.1 us (23%)
  starting transfers between devices  46.9 us (19%)
  Pallas kernels  40.9 us (17%)
  local copies, waits for them, and re-layouts  19.8 us (8%)
  other arithmetic  12.4 us (5%)
    ppermute x25, waiting for transfers between devices, send(): return lax.ppermute(value, AXES, pairs_of(move))  56.1 us
    ppermute x25, starting transfers between devices, send(): return lax.ppermute(value, AXES, pairs_of(move))  46.9 us
    pallas_call x9, Pallas kernels, call(): pl.pallas_call(kernel, out_shape=tuple(outs), in_specs=specs, out_specs=t...  40.9 us
    all_to_all x1, blocking collectives, reduce_and_gather(): parts = lax.all_to_all(total.reshape(32, 16, 768), ('tp', 'yl', 'z'), 0, 0)  32.7 us
    all_to_all x1, blocking collectives, reduce_and_gather(): mine = lax.all_to_all(columns, ('x', 'yl'), 0, 0)  18.3 us
    all_to_all x1, blocking collectives, reduce_and_gather(): column = lax.all_to_all(chunks, 'z', 0, 0)  13.6 us
    unnamed x36, local copies, waits for them, and re-layouts  8.91 us
  transfers between devices with their start and end apart: 25, of which 10 were waited for; matrix products, arithmetic and copies ran while one was open for 9% of the time, Pallas kernels for 5%

commit v1 on v0

--- a/solution.py
+++ b/solution.py
@@ -103,13 +103,16 @@
     )(*values, *after)
 
 
-def band_pieces(tile, t):
-    first = t == 0
-    return (
-        jnp.where(first, tile[9:12], tile[3:6]),
-        jnp.where(first, tile[0:3], tile[6:9]),
-        tile[0:3],
-    )
+def pieces_kernel(place, tile, near, far, below):
+    t = place[4]
+    for i in range(3):
+        near[i] = tile[9 + i - 6 * t]
+        far[i] = tile[i + 6 * t]
+        below[i] = tile[i]
+
+
+def band_pieces(place, tile, name):
+    return call(pieces_kernel, (tile,), [whole((3, 48, D))] * 3, place=place, name=name)
 
 
 def exchange_rows(pieces):
@@ -117,10 +120,56 @@
     return flip(near, t=1), send(far, far_move), send(below, lat_move(-1))
 
 
-def first_columns(tile, near, far, below, t):
-    edge = tile[:, :6]
-    own = jnp.where(t == 0, edge[3:9], jnp.concatenate([edge[9:12], below[:, :6]], 0))
-    return jnp.concatenate([own, near[:, :6], far[:, :6]], 0)
+def edge_kernel(place, tile, near, far, below, edge):
+    t = place[4]
+    for i in range(3):
+        edge[i] = tile[3 + i + 6 * t, :6]
+        edge[3 + i] = jnp.where(t == 0, tile[6 + i, :6].astype(F32), below[i, :6].astype(F32)).astype(BF)
+        edge[6 + i] = near[i, :6]
+        edge[9 + i] = far[i, :6]
+
+
+def first_columns(place, tile, rows, name, after=()):
+    kernel = without(edge_kernel, 5, len(after))
+    (edge,) = call(kernel, (tile, *rows), [whole((12, 6, D))], place=place, name=name, after=after)
+    return edge
+
+
+def half_of_attend_weights(place, w_qkv, w_out):
+    def kernel(place, wq, wo, out):
+        out[0:3] = wq[...]
+        out[3] = wo[...]
+
+    return halves(
+        kernel, place, (w_qkv, w_out), (4, 256, 256),
+        [((3, 256, 256), lambda i, p: (0, p[3], 0)), ((256, 256), lambda i, p: (0, p[3]))], "half_attend",
+    )
+
+
+def half_of_mlp_weights(place, w_fc1, w_fc2):
+    def kernel(place, w1, w2, out):
+        out[0] = w1[...]
+        out[1] = w2[...]
+
+    return halves(
+        kernel, place, (w_fc1, w_fc2), (2, 512, 512),
+        [((512, 512), lambda i, p: (0, p[3])), ((512, 512), lambda i, p: (p[3], 0))], "half_mlp",
+    )
+
+
+def halves(kernel, place, args, shape, specs, name):
+    return pl.pallas_call(
+        kernel,
+        out_shape=whole(shape),
+        grid_spec=pltpu.PrefetchScalarGridSpec(
+            num_scalar_prefetch=1,
+            grid=(1,),
+            in_specs=[pl.BlockSpec(block, index) for block, index in specs],
+            out_specs=pl.BlockSpec(shape, lambda i, p: (0,) * len(shape)),
+        ),
+        compiler_params=pltpu.CompilerParams(vmem_limit_bytes=VMEM_LIMIT),
+        name=name,
+    )(place, *args)
 
 
 def to_windows(band):
@@ -241,65 +290,78 @@
             out[lead + (yl, z, slice(None), cols)] = block[rows].astype(BF)
 
 
-def mlp_kernel(
-    place, mixed_ref, tile, near, far, below, moved, g2, w1_own, w2_own, w12_m, w12_s,
-    band, tail, dm_ref, keep, away,
-    n2t, cott, hid_scr, dpre_scr, stage, wins,
-):
-    mx, c, mt = place[0], place[3], place[4]
+def mlp_block(w1, w2, cols, n2, cot):
+    hidden, slope = gelu_parts(dot(n2, w1[:, cols]))
+    return hidden.astype(BF), (dot_nt(cot, w2[cols, :]) * slope).astype(BF)
+
+
+def store_grads(n2t, cott, hidden, dpre, lead, c, keep, away):
     mine = pl.ds(pl.multiple_of(c * 256, 256), 256)
     sibs = pl.ds(pl.multiple_of((1 - c) * 256, 256), 256)
-    load_windows(mt, tile, near, far, below, moved, stage, wins)
-    gain = g2[...]
+    for rows, out in ((sibs, away), (mine, keep)):
+        store_rows(out, dot(n2t[rows, :], dpre), lead, slice(0, 256))
+        store_rows(out, dot(cott[rows, :], hidden), lead, slice(256, 512))
+
+
+def mlp_own_kernel(
+    place, mixed_ref, tile, near, far, below, moved, g2, w1_own, w2_own,
+    n2_ref, n2t, cot_ref, cott, out_acc, norm_acc, keep, away,
+    hid_scr, dpre_scr, stage, wins,
+):
+    mx, c = place[0], place[3]
+    load_windows(place[4], tile, near, far, below, moved, stage, wins)
     mixed = mixed_ref[...].astype(F32)
-    normed, xhat, rstd = norm(mixed, gain)
-    n2 = normed.astype(BF)
+    normed = norm(mixed, g2[...])[0]
+    n2_ref[...] = normed.astype(BF)
     n2t[...] = normed.T.astype(BF)
     cott[...] = wins[...].T.astype(BF)
-    cot = wins[...].astype(BF)
-    blocks = [(0, x, w1_own, w2_own, x) for x in range(4)]
-    for pair, half in ((w12_m, c), (w12_s, 1 - c)):
-        blocks += [(1, 2 * half + i, pair.at[0], pair.at[1], i) for i in range(2)]
-    for n, (t, x, w1, w2, i) in enumerate(blocks):
-        cols = slice(i * 256, i * 256 + 256)
-        place_cols = slice(n * 256, n * 256 + 256)
-        hidden, slope = gelu_parts(dot(n2, w1[:, cols]))
-        hidden = hidden.astype(BF)
-        dpre = (dot_nt(cot, w2[cols, :]) * slope).astype(BF)
-        hid_scr[:, place_cols] = hidden
-        dpre_scr[:, place_cols] = dpre
-        lead = (x ^ mx, t ^ mt)
-        for rows, out in ((sibs, away), (mine, keep)):
-            store_rows(out, dot(n2t[rows, :], dpre), lead, slice(0, 256))
-            store_rows(out, dot(cott[rows, :], hidden), lead, slice(256, 512))
-    d_norm = (
-        dot_nt(dpre_scr[:, :1024], w1_own[...])
-        + dot_nt(dpre_scr[:, 1024:1536], w12_m[0])
-        + dot_nt(dpre_scr[:, 1536:], w12_s[0])
-    )
+    cot_ref[...] = wins[...].astype(BF)
+    n2, cot = n2_ref[...], cot_ref[...]
+    for x in range(4):
+        cols = slice(x * 256, x * 256 + 256)
+        hidden, dpre = mlp_block(w1_own, w2_own, cols, n2, cot)
+        hid_scr[:, cols] = hidden
+        dpre_scr[:, cols] = dpre
+        store_grads(n2t, cott, hidden, dpre, (x ^ mx,), c, keep, away)
+    out_acc[...] = mixed + dot(hid_scr[...], w2_own[...])
+    norm_acc[...] = dot_nt(dpre_scr[...], w1_own[...])
+
+
+def mlp_other_kernel(
+    place, mixed_ref, n2_ref, n2t, cot_ref, cott, out_acc, norm_acc, g2, w12_m, w12_s,
+    band, tail, dm_ref, keep, away,
+    hid_scr, dpre_scr, stage, wins,
+):
+    mx, c = place[0], place[3]
+    n2, cot = n2_ref[...], cot_ref[...]
+    for n, (pair, half) in enumerate(((w12_m, c), (w12_s, 1 - c))):
+        for i in range(2):
+            cols = slice(i * 256, i * 256 + 256)
+            hidden, dpre = mlp_block(pair.at[0], pair.at[1], cols, n2, cot)
+            hid_scr[:, n * 512 + i * 256 : n * 512 + i * 256 + 256] = hidden
+            dpre_scr[:, n * 512 + i * 256 : n * 512 + i * 256 + 256] = dpre
+            store_grads(n2t, cott, hidden, dpre, ((2 * half + i) ^ mx,), c, keep, away)
+    d_norm = norm_acc[...] + (
+        dot_nt(dpre_scr[:, :512], w12_m[0]) + dot_nt(dpre_scr[:, 512:], w12_s[0])
+    )
+    gain = g2[...]
+    xhat, rstd = norm(mixed_ref[...].astype(F32), gain)[1:]
     scaled = d_norm * gain
-    dm = wins[...] + rstd * (
+    dm = cot.astype(F32) + rstd * (
         scaled
         - jnp.mean(scaled, -1, keepdims=True)
         - xhat * jnp.mean(scaled * xhat, -1, keepdims=True)
     )
     dm_ref[...] = dm.astype(BF)
-    wins[...] = mixed + (
-        dot(hid_scr[:, :1024], w2_own[...])
-        + dot(hid_scr[:, 1024:1536], w12_m[1])
-        + dot(hid_scr[:, 1536:], w12_s[1])
-    )
+    wins[...] = out_acc[...] + (dot(hid_scr[:, :512], w12_m[1]) + dot(hid_scr[:, 512:], w12_s[1]))
     store_windows(wins, stage, band, tail)
 
 
 def attend_back_kernel(
-    place, dm_ref, heads_ref, prob_ref, qkv_ref, n1t_ref, wo_full, first, second,
-    keep, away,
-    dmt, dheads, dqkv,
+    dm_ref, prob_ref, qkv_ref, wo_full, first, second,
+    dqkv, dmt,
+    dheads,
 ):
-    mx, c, mt = place[0], place[3], place[4]
-    mine = pl.ds(pl.multiple_of(c * 256, 256), 256)
-    sibs = pl.ds(pl.multiple_of((1 - c) * 256, 256), 256)
     dm = dm_ref[...]
     dmt[...] = dm.astype(F32).T.astype(BF)
     dheads[...] = dot_nt(dm, wo_full[...]).astype(BF)
@@ -333,6 +395,15 @@
         return carry
 
     lax.fori_loop(0, WINS, window, 0)
+
+
+def attend_grads_kernel(
+    place, dqkv, dmt, heads_ref, n1t_ref, first, second, third,
+    keep, away,
+):
+    mx, c, mt = place[0], place[3], place[4]
+    mine = pl.ds(pl.multiple_of(c * 256, 256), 256)
+    sibs = pl.ds(pl.multiple_of((1 - c) * 256, 256), 256)
     for rows, out in ((sibs, away), (mine, keep)):
         for t in range(2):
             for half in range(2):
@@ -384,9 +455,11 @@
         outs[x][...] = add(keep[x], arrived[x])
 
 
-def x_sum_kernel(*refs):
-    fc, at, out = refs[0:4], refs[4:8], refs[-1]
-    out[:, :, :, :, :512] = add(*[r[...] for r in fc])
+def x_sum_kernel(place, *refs):
+    own, other, at, out = refs[0:4], refs[4:8], refs[8:12], refs[-1]
+    t = place[4]
+    out[t, :, :, :, :512] = add(*[r[...] for r in own])
+    out[1 - t, :, :, :, :512] = add(*[r[...] for r in other])
     out[:, :, :, :, 512:] = add(*[r[...] for r in at])
 
 
@@ -425,8 +498,8 @@
     go[...] = scro[...].astype(F32).T.astype(BF)
 
 
-def core_phase(keep, away, width):
-    outs = [whole((2, 2, 8, 16, width))] * 4
+def core_phase(keep, away):
+    outs = [whole(keep.shape[1:])] * 4
     return call(core_sum_kernel, (keep, flip(away, c=1)), outs, name="core_sum")
 
 
@@ -434,8 +507,10 @@
     return [cut[0]] + [flip(cut[k], x=k) for k in (1, 2, 3)]
 
 
-def reduce_and_gather(place, fc, at, after):
-    (total,) = call(x_sum_kernel, (*fc, *at), [whole((2, 2, 8, 16, 768))], name="x_sum", after=after)
+def reduce_and_gather(place, own, other, at, after):
+    (total,) = call(
+        x_sum_kernel, (*own, *other, *at), [whole((2, 2, 8, 16, 768))], (), place, name="x_sum", after=after
+    )
     parts = lax.all_to_all(total.reshape(32, 16, 768), ("tp", "yl", "z"), 0, 0)
     (chunks,) = call(last_sum_kernel, (parts,), [whole((8, 16, 768))], name="last_sum")
     column = lax.all_to_all(chunks, "z", 0, 0)
@@ -452,30 +527,20 @@
     place = jnp.stack([x, yl, z, c, t]).astype(jnp.int32)
     tile, cot = tokens[0], cotangent[0]
 
-    rows = exchange_rows(band_pieces(tile, t))
-    wqo = jnp.concatenate(
-        [
-            lax.dynamic_slice_in_dim(w_qkv, c * 256, 256, 1),
-            lax.dynamic_slice_in_dim(w_out, c * 256, 256, 1)[None],
-        ],
-        0,
-    )
+    pieces = band_pieces(place, tile, "pieces")
+    rows = exchange_rows(pieces)
+    (wqo,) = fence((half_of_attend_weights(place, w_qkv, w_out),), (pieces[0],))
     wqo = flip(wqo, yl=1, t=1)
-    edge = first_columns(tile, *rows, t)
+    edge = first_columns(place, tile, rows, "edge")
     moved = send(edge, lon_move(-1))
-
-    w12 = jnp.stack(
-        [
-            lax.dynamic_slice_in_dim(w_fc1, c * 512, 512, 1),
-            lax.dynamic_slice_in_dim(w_fc2, c * 512, 512, 0),
-        ]
-    )
-    *pieces, w12 = fence((*band_pieces(cot, t), w12), (edge,))
-    cot_rows = exchange_rows(pieces)
+    (wqo,) = fence((wqo,), (edge,))
+
+    cot_rows = exchange_rows(fence(band_pieces(place, cot, "cot_pieces"), (edge,)))
+    wqo_sib = flip(wqo, c=1)
+    (w12,) = fence((half_of_mlp_weights(place, w_fc1, w_fc2),), (wqo, moved))
     w12 = flip(w12, yl=1, t=1)
-    cot_edge = first_columns(cot, *cot_rows, t)
+    cot_edge = first_columns(place, cot, cot_rows, "cot_edge", (moved,))
     cot_moved = send(cot_edge, lon_move(-1))
-    wqo_sib = flip(wqo, c=1)
 
     band = lax.dynamic_slice_in_dim(labels, t * 6, 6, 1)
     band = jnp.where(t == 0, band, band[::-1]).reshape(12, 48, 1)
@@ -497,42 +562,61 @@
         name="attend",
         after=(cot_edge,),
     )
+    grads = [whole((4, 2, 8, 16, 512))] * 2
+    scratch = [pltpu.VMEM((TOK, 1024), BF), pltpu.VMEM((TOK, 1024), BF)] + stage
+    tokens_like = [whole((TOK, D)), whole((D, TOK))] * 2 + [whole((TOK, D), F32)] * 2
+    *carried, keep, away = call(
+        mlp_own_kernel,
+        (mixed, cot, *cot_rows, cot_moved, second_norm_gain[None], w_fc1, w_fc2),
+        tokens_like + grads,
+        scratch,
+        place,
+        flops=4 * 10**9,
+        name="mlp_own",
+    )
+    own = (keep, away)
+    (w12,) = fence((w12,), (keep,))
     w12_sib = flip(w12, c=1)
-    grads = [whole((4, 2, 2, 8, 16, 512))] * 2
-    out_band, tail, dm, *fc = call(
-        mlp_kernel,
-        (mixed, cot, *cot_rows, cot_moved, second_norm_gain[None], w_fc1, w_fc2, w12, w12_sib),
+    out_band, tail, dm, *other = call(
+        mlp_other_kernel,
+        (mixed, *carried, second_norm_gain[None], w12, w12_sib),
         [whole((12, 48, D)), whole((12, 6, D)), whole((TOK, D))] + grads,
-        [
-            pltpu.VMEM((D, TOK), BF), pltpu.VMEM((D, TOK), BF),
-            pltpu.VMEM((TOK, FF), BF), pltpu.VMEM((TOK, FF), BF),
-        ]
-        + stage,
+        scratch,
         place,
-        flops=8 * 10**9,
-        name="mlp",
-    )
-    fc_cut = core_phase(*fc, 512)
+        flops=4 * 10**9,
+        name="mlp_other",
+    )
+    own_cut = core_phase(*own)
+    own_parts = x_phase(own_cut)
+    other_cut = core_phase(*other)
+    other_parts = x_phase(other_cut)
     out_moved = send(tail, lon_move(1))
-    fc_parts = x_phase(fc_cut)
-    grads = [whole((4, 2, 2, 8, 16, 256))] * 2
+    dqkv, dmt = call(
+        attend_back_kernel,
+        (dm, prob, qkv, wo_full),
+        [whole((TOK, 3 * D)), whole((D, TOK))],
+        [pltpu.VMEM((TOK, D), BF)],
+        flops=4 * 10**9,
+        name="attend_back",
+        after=(other_cut[0], out_moved),
+    )
     at = call(
-        attend_back_kernel,
-        (dm, heads, prob, qkv, n1t, wo_full),
-        grads,
-        [pltpu.VMEM((D, TOK), BF), pltpu.VMEM((TOK, D), BF), pltpu.VMEM((TOK, 3 * D), BF)],
+        attend_grads_kernel,
+        (dqkv, dmt, heads, n1t),
+        [whole((4, 2, 2, 8, 16, 256))] * 2,
+        (),
         place,
-        flops=5 * 10**9,
-        name="attend_back",
-        after=(fc_cut[0], out_moved),
-    )
-    at_cut = core_phase(*at, 256)
-    at_parts = x_phase(at_cut)
+        flops=1 * 10**9,
+        name="attend_grads",
+        after=own_parts[1:],
+    )
+    at_cut = core_phase(*at)
+    at_parts = x_phase((at_cut[0], *fence(at_cut[1:], other_parts[1:])))
 
     out = jnp.concatenate([out_moved, out_band[:, 6:]], 1)
     near, far, above = fence((out[6:9], out[9:12], out[3:6]), (at_cut[0],))
     near, far, above = flip(near, t=1), send(far, far_back), send(above, lat_move(1))
-    gq, go, g1, g2 = reduce_and_gather(place, fc_parts, at_parts, (near, far, above))
+    gq, go, g1, g2 = reduce_and_gather(place, own_parts, other_parts, at_parts, (near, far, above))
     out = jnp.where(
         t == 0,
         jnp.concatenate([far, out[0:6], near], 0),

time: 243 us -> 247 us (1.016)
  waiting for transfers between devices: 56.1 us -> 20.5 us
  starting transfers between devices: 46.9 us -> 78.5 us
  local copies, waits for them, and re-layouts: 19.8 us -> 33.3 us
  other arithmetic: 12.4 us -> 1.98 us
  Pallas kernels: 40.9 us -> 48.9 us
  blocking collectives: 64.7 us -> 61.9 us
    ppermute x25 -> x29, waiting for transfers between devices: 56.1 us -> 20.5 us  [send(): return lax.ppermute(value, AXES, pairs_of(move))]
    ppermute x25 -> x29, starting transfers between devices: 46.9 us -> 78.5 us  [send(): return lax.ppermute(value, AXES, pairs_of(move))]
    unnamed x36 -> x140, local copies, waits for them, and re-layouts: 8.91 us -> 32.6 us
    pallas_call x9 -> x16, Pallas kernels: 40.9 us -> 47.7 us  [call(): pl.pallas_call(kernel, out_shape=tuple(outs), in_specs=specs, out_specs=t...]
    slice x8 -> x0, local copies, waits for them, and re-layouts: 3.61 us -> none  [the longest x4 2.26 us: first_columns(): return jnp.concatenate([own, near[:, :6], far[:, :6]], 0)]
    select_n x4 -> x0, other arithmetic: 3.58 us -> none  [the longest x2 2.81 us: band_pieces(): jnp.where(first, tile[0:3], tile[6:9])]
    slice x2 -> x0, other arithmetic: 3.53 us -> none  [band_pieces(): tile[0:3]]
  transfers between devices with their start and end apart: 25 -> 29, of which waited for: 10 -> 9; matrix products, arithmetic and copies ran while one was open for 9% -> 1% of each run, Pallas kernels for 5% -> 16%
where the time goes in v1:
time: 247 us; the launch traced here: 246 us
  starting transfers between devices  78.5 us (32%)
  blocking collectives  61.9 us (25%)
  Pallas kernels  48.9 us (20%)
  local copies, waits for them, and re-layouts  33.3 us (13%)
  waiting for transfers between devices  20.5 us (8%)
    ppermute x29, starting transfers between devices, send(): return lax.ppermute(value, AXES, pairs_of(move))  78.5 us
    pallas_call x16, Pallas kernels, call(): pl.pallas_call(kernel, out_shape=tuple(outs), in_specs=specs, out_specs=t...  47.7 us
    unnamed x140, local copies, waits for them, and re-layouts  32.6 us
    all_to_all x1, blocking collectives, reduce_and_gather(): parts = lax.all_to_all(total.reshape(32, 16, 768), ('tp', 'yl', 'z'), 0, 0)  30.4 us
    ppermute x29, waiting for transfers between devices, send(): return lax.ppermute(value, AXES, pairs_of(move))  20.5 us
    all_to_all x1, blocking collectives, reduce_and_gather(): mine = lax.all_to_all(columns, ('x', 'yl'), 0, 0)  17.7 us
    all_to_all x1, blocking collectives, reduce_and_gather(): column = lax.all_to_all(chunks, 'z', 0, 0)  13.7 us
  transfers between devices with their start and end apart: 29, of which 9 were waited for; matrix products, arithmetic and copies ran while one was open for 1% of the time, Pallas kernels for 16%

profile of v1, /device:TPU:1, one launch (start us, length us, event | category | flops | bytes accessed | tf_op | source)
XLA Modules:
  0.0 246.2 jit_solution(2269480137808110226)
XLA Ops:
  6.5 3.6 %collective-permute-start.4 = (bf16[4,256,256]{2,1,0:T(8,128)(2,1)}, bf16[4,256,256]{2,1,0:T(8,128)(2,1)S(1)}, u32[]{:S(2)}, u32[]{:S(2)}) collective-permute-start(bf16[4,256,256]{2,1,0:T(8,128)(2,1)} %fence.7), channel_id=1, source_target_pairs={{0,33},{1,32},{2,35},{3,34},{4,37},{5,36},{6,39},{7,38},{8,41},{9,... | collective-permute-start | bytes 1572872 | tf_op jit(solution)/shard_map/ppermute | solution.py:44
  10.1 2.2 collective-permute-start.1
  12.9 4.8 %collective-permute-start = (bf16[3,48,512]{2,1,0:T(8,128)(2,1)}, bf16[3,48,512]{2,1,0:T(8,128)(2,1)S(1)}, u32[]{:S(2)}, u32[]{:S(2)}) collective-permute-start(bf16[3,48,512]{2,1,0:T(8,128)(2,1)} %copy-done.41), channel_id=1, source_target_pairs={{0,1},{1,0},{2,3},{3,2},{4,5},{5,4},{6,7},{7,6},{8,9},{9,8},{10,11... | collective-permute-start | bytes 442376 | tf_op jit(solution)/shard_map/ppermute | solution.py:44
  17.7 6.0 %collective-permute-done.refs_2_ = bf16[3,48,512]{2,1,0:T(8,128)(2,1)S(1)} collective-permute-done((bf16[3,48,512]{2,1,0:T(8,128)(2,1)}, bf16[3,48,512]{2,1,0:T(8,128)(2,1)S(1)}, u32[]{:S(2)}, u32[]{:S(2)}) %collective-permute-start) | collective-permute-done | bytes 147488 | tf_op jit(solution)/shard_map/ppermute | solution.py:44
  25.1 2.6 %collective-permute-done.4.refs_0_ = bf16[4,256,256]{2,1,0:T(8,128)(2,1)S(1)} collective-permute-done((bf16[4,256,256]{2,1,0:T(8,128)(2,1)}, bf16[4,256,256]{2,1,0:T(8,128)(2,1)S(1)}, u32[]{:S(2)}, u32[]{:S(2)}) %collective-permute-start.4) | collective-permute-done | bytes 524320 | tf_op jit(solution)/shard_map/ppermute | solution.py:44
  35.2 2.8 %collective-permute-start.10 = (bf16[2,512,512]{2,1,0:T(8,128)(2,1)}, bf16[2,512,512]{2,1,0:T(8,128)(2,1)}, u32[]{:S(2)}, u32[]{:S(2)}) collective-permute-start(bf16[2,512,512]{2,1,0:T(8,128)(2,1)} %fence.10), channel_id=1, source_target_pairs={{0,33},{1,32},{2,35},{3,34},{4,37},{5,36},{6,39},{7,38},{8,41},{9,... | collective-permute-start | bytes 3145736 | tf_op jit(solution)/shard_map/ppermute | solution.py:44
  41.0 4.2 %collective-permute-start.7 = (bf16[3,48,512]{2,1,0:T(8,128)(2,1)}, bf16[3,48,512]{2,1,0:T(8,128)(2,1)S(1)}, u32[]{:S(2)}, u32[]{:S(2)}) collective-permute-start(bf16[3,48,512]{2,1,0:T(8,128)(2,1)} %get-tuple-element.66), channel_id=1, source_target_pairs={{0,225},{1,0},{2,227},{3,2},{4,229},{5,4},{6,231},{7,6},{8,233},{9... | collective-permute-start | bytes 442376 | tf_op jit(solution)/shard_map/ppermute | solution.py:44
  49.5 6.3 %collective-permute-start.9 = (bf16[12,6,512]{2,1,0:T(8,128)(2,1)S(1)}, bf16[12,6,512]{2,1,0:T(8,128)(2,1)S(1)}, u32[]{:S(2)}, u32[]{:S(2)}) collective-permute-start(bf16[12,6,512]{2,1,0:T(8,128)(2,1)S(1)} %cot_edge.1.refs_13_), channel_id=1, source_target_pairs={{0,30},{1,31},{2,0},{3,1},{4,2},{5,3},{6,4},{7,5},{8,6},{9,7},{10,... | collective-permute-start | bytes 221192 | tf_op jit(solution)/shard_map/ppermute | solution.py:44
  59.6 8.9 %attend.1 = (bf16[512,576]{1,0:T(8,128)(2,1)S(1)}, bf16[576,1536]{1,0:T(8,128)(2,1)}, bf16[32,144,144]{2,1,0:T(8,128)(2,1)}, bf16[576,512]{1,0:T(8,128)(2,1)S(1)...) custom-call(s32[5]{0:T(128)S(1)} %stack.23.place.refs_0_, bf16[12,48,512]{2,1,0:T(8,128)(2,1)S(1)} %bitcast.28, ...), custom_call_target="tpu_custom_call" | custom-call | flops 3000000000 | bytes 8982548 | tf_op jit(solution)/shard_map/attend/pallas_call | solution.py:434
  69.3 9.3 %mlp_own.1 = (bf16[576,512]{1,0:T(8,128)(2,1)S(1)}, bf16[512,576]{1,0:T(8,128)(2,1)S(1)}, bf16[576,512]{1,0:T(8,128)(2,1)S(1)}, bf16[512,576]{1,0:T(8,128)(2,1)S...) custom-call(s32[5]{0:T(128)S(1)} %stack.23.place.refs_0_, ...), custom_call_target="tpu_custom_call" | custom-call | flops 4000000000 | bytes 10610708 | tf_op jit(solution)/shard_map/mlp_own/pallas_call | solution.py:434
  83.0 6.6 %collective-permute-start.11 = (bf16[2,512,512]{2,1,0:T(8,128)(2,1)}, bf16[2,512,512]{2,1,0:T(8,128)(2,1)S(1)}, u32[]{:S(2)}, u32[]{:S(2)}) collective-permute-start(bf16[2,512,512]{2,1,0:T(8,128)(2,1)} %fence.11.w12_m), channel_id=1, source_target_pairs={{0,2},{1,3},{2,0},{3,1},{4,6},{5,7},{6,4},{7,5},{8,10},{9,11},{10,... | collective-permute-start | bytes 3145736 | tf_op jit(solution)/shard_map/ppermute | solution.py:44
  96.3 8.5 %mlp_other.1 = (bf16[12,48,512]{2,1,0:T(8,128)(2,1)S(1)}, bf16[12,6,512]{2,1,0:T(8,128)(2,1)S(1)}, bf16[576,512]{1,0:T(8,128)(2,1)S(1)}, bf16[4,2,8,16,512]{4,3,...) custom-call(s32[5]{0:T(128)S(1)} %stack.23.place.refs_0_, bf16[576,512]{1,0:T(8,128)(2,1)S(1)} %copy-done.59, ...), custom_call_target="tpu_custom_call" | custom-call | flops 4000000000 | bytes 10758164 | tf_op jit(solution)/shard_map/mlp_other/pallas_call | solution.py:434
  106.8 2.4 collective-permute-start.16
  110.4 9.8 %attend_back.1 = (bf16[576,1536]{1,0:T(8,128)(2,1)S(1)}, bf16[512,576]{1,0:T(8,128)(2,1)S(1)}) custom-call(bf16[576,512]{1,0:T(8,128)(2,1)S(1)} %get-tuple-element.78.dm_ref, bf16[32,144,144]{2,1,0:T(8,128)(2,1)} %get-tuple-element.79.prob_ref, bf16[576,1536]{1,0:T(8,128)(2,1)S(1)} %copy-done.53, bf16[512,512]{1,0:T(8,128)(2,1)S(1)} %copy-done.65, ...), custom_call_target="tpu_custom_call" | custom-call | flops 4000000000 | bytes 6905856 | tf_op jit(solution)/shard_map/attend_back/pallas_call | solution.py:434
  122.8 3.5 %attend_grads.1 = (bf16[4,2,2,8,16,256]{5,4,3,2,1,0:T(8,128)(2,1)S(1)}, bf16[4,2,2,8,16,256]{5,4,3,2,1,0:T(8,128)(2,1)S(1)}) custom-call(s32[5]{0:T(128)S(1)} %stack.23.place.refs_0_, bf16[576,1536]{1,0:T(8,128)(2,1)} %copy-done.9, bf16[512,576]{1,0:T(8,128)(2,1)S(1)} %get-tuple-element.86.dmt, bf16[576,512]{1,0:T(8,128)(2,1)S(1)} %copy-done.24, ...), custom_call_target="tpu_custom_call" | custom-call | flops 1000000000 | bytes 6422548 | tf_op jit(solution)/shard_map/attend_grads/pallas_call | solution.py:434
  130.1 2.2 collective-permute-start.24
  136.4 15.1 %collective-permute-start.19 = (bf16[3,48,512]{2,1,0:T(8,128)(2,1)}, bf16[3,48,512]{2,1,0:T(8,128)(2,1)S(1)}, u32[]{:S(2)}, u32[]{:S(2)}) collective-permute-start(bf16[3,48,512]{2,1,0:T(8,128)(2,1)} %get-tuple-element.96), channel_id=1, source_target_pairs={{0,1},{1,32},{2,3},{3,34},{4,5},{5,36},{6,7},{7,38},{8,9},{9,40},{... | collective-permute-start | bytes 442376 | tf_op jit(solution)/shard_map/ppermute | solution.py:44
  154.1 2.2 collective-permute-start.27
  156.3 7.4 %collective-permute-start.20 = (bf16[3,48,512]{2,1,0:T(8,128)(2,1)S(1)}, bf16[3,48,512]{2,1,0:T(8,128)(2,1)S(1)}, u32[]{:S(2)}, u32[]{:S(2)}) collective-permute-start(bf16[3,48,512]{2,1,0:T(8,128)(2,1)S(1)} %copy-done.67), channel_id=1, source_target_pairs={{0,1},{1,0},{2,3},{3,2},{4,5},{5,4},{6,7},{7,6},{8,9},{9,8},{10,11... | collective-permute-start | bytes 442376 | tf_op jit(solution)/shard_map/ppermute | solution.py:44
  171.5 30.4 %all_to_all.15.parts = bf16[32,16,768]{2,1,0:T(8,128)(2,1)S(1)} all-to-all(bf16[32,16,768]{2,1,0:T(8,128)(2,1)S(1)} %bitcast.22), channel_id=1, replica_groups=mesh['x'=4,'yl'=2,'z'=8,'c'=2,'tp'=2] {'tp','yl','z'}, dimensions={0} | all-to-all | bytes 1572864 | tf_op jit(solution)/shard_map/all_to_all | solution.py:514
  202.1 13.7 %all_to_all.16.part = bf16[8,16,768]{2,1,0:T(8,128)(2,1)S(1)} all-to-all(bf16[8,16,768]{2,1,0:T(8,128)(2,1)S(1)} %last_sum.1), channel_id=1, replica_groups=mesh['x'=4,'yl'=2,'z'=8,'c'=2,'tp'=2] {'z'}, dimensions={0} | all-to-all | bytes 393216 | tf_op jit(solution)/shard_map/all_to_all | solution.py:516
  215.8 17.7 %all_to_all.17.mine = bf16[8,8,16,768]{3,2,1,0:T(8,128)(2,1)S(1)} all-to-all(bf16[8,8,16,768]{3,2,1,0:T(8,128)(2,1)S(1)} %copies.1), channel_id=1, replica_groups=mesh['x'=4,'yl'=2,'z'=8,'c'=2,'tp'=2] {'x','yl'}, dimensions={0} | all-to-all | bytes 3145728 | tf_op jit(solution)/shard_map/all_to_all | solution.py:518
  233.6 6.8 %collective-permute-start.28 = (bf16[8,8,16,768]{3,2,1,0:T(8,128)(2,1)S(1)}, bf16[8,8,16,768]{3,2,1,0:T(8,128)(2,1)S(1)}, u32[]{:S(2)}, u32[]{:S(2)}) collective-permute-start(bf16[8,8,16,768]{3,2,1,0:T(8,128)(2,1)S(1)} %all_to_all.17.mine), channel_id=1, source_target_pairs={{0,2},{1,3},{2,0},{3,1},{4,6},{5,7},{6,4},{7,5},{8,10},{9,11},{10,... | collective-permute-start | bytes 4718600 | tf_op jit(solution)/shard_map/ppermute | solution.py:44
  243.4 2.8 %place.1 = (bf16[3,512,256]{2,1,0:T(8,128)(2,1)}, bf16[256,512]{1,0:T(8,128)(2,1)}, bf16[512,1024]{1,0:T(8,128)(2,1)}, bf16[1024,512]{1,0:T(8,128)(2,1)}) custom-call(s32[5]{0:T(128)S(1)} %stack.23.place.refs_0_, bf16[8,8,16,768]{3,2,1,0:T(8,128)(2,1)S(1)} %all_to_all.17.mine, bf16[8,8,16,768]{3,2,1,0:T(8,128)(2,1)S(1)} %collective-permute-done.28.sib), custom_call_target="tpu_custom_call" | custom-call | bytes 6291476 | tf_op jit(solution)/shard_map/place/pallas_call | solution.py:434
  (217 shorter events, 65.3 us)
Async XLA Ops:
  6.5 21.1 %collective-permute-start.4 = (bf16[4,256,256]{2,1,0:T(8,128)(2,1)}, bf16[4,256,256]{2,1,0:T(8,128)(2,1)S(1)}, u32[]{:S(2)}, u32[]{:S(2)}) collective-permute-start(bf16[4,256,256]{2,1,0:T(8,128)(2,1)} %fence.7), channel_id=1, source_target_pairs={{0,33},{1,32},{2,35},{3,34},{4,37},{5,36},{6,39},{7,38},{8,41},{9,... | collective-permute-start | bytes 1572872 | tf_op jit(solution)/shard_map/ppermute | solution.py:44
  10.1 7.6 %collective-permute-start.1 = (bf16[3,48,512]{2,1,0:T(8,128)(2,1)S(1)}, bf16[3,48,512]{2,1,0:T(8,128)(2,1)S(1)}, u32[]{:S(2)}, u32[]{:S(2)}) collective-permute-start(bf16[3,48,512]{2,1,0:T(8,128)(2,1)S(1)} %get-tuple-element.60), channel_id=1, source_target_pairs={{0,225},{1,0},{2,227},{3,2},{4,229},{5,4},{6,231},{7,6},{8,233},{9... | collective-permute-start | bytes 442376 | tf_op jit(solution)/shard_map/ppermute | solution.py:44
  12.3 5.4 %collective-permute-start.2 = (bf16[3,48,512]{2,1,0:T(8,128)(2,1)S(1)}, bf16[3,48,512]{2,1,0:T(8,128)(2,1)S(1)}, u32[]{:S(2)}, u32[]{:S(2)}) collective-permute-start(bf16[3,48,512]{2,1,0:T(8,128)(2,1)S(1)} %get-tuple-element.61), channel_id=1, source_target_pairs={{1,225},{3,227},{5,229},{7,231},{9,233},{11,235},{13,237},{15,239}... | collective-permute-start | bytes 442376 | tf_op jit(solution)/shard_map/ppermute | solution.py:44
  12.9 10.8 %collective-permute-start = (bf16[3,48,512]{2,1,0:T(8,128)(2,1)}, bf16[3,48,512]{2,1,0:T(8,128)(2,1)S(1)}, u32[]{:S(2)}, u32[]{:S(2)}) collective-permute-start(bf16[3,48,512]{2,1,0:T(8,128)(2,1)} %copy-done.41), channel_id=1, source_target_pairs={{0,1},{1,0},{2,3},{3,2},{4,5},{5,4},{6,7},{7,6},{8,9},{9,8},{10,11... | collective-permute-start | bytes 442376 | tf_op jit(solution)/shard_map/ppermute | solution.py:44
  28.4 27.4 %collective-permute-start.5 = (bf16[4,256,256]{2,1,0:T(8,128)(2,1)}, bf16[4,256,256]{2,1,0:T(8,128)(2,1)}, u32[]{:S(2)}, u32[]{:S(2)}) collective-permute-start(bf16[4,256,256]{2,1,0:T(8,128)(2,1)} %fence.8.refs_11_.refs_1_), channel_id=1, source_target_pairs={{0,2},{1,3},{2,0},{3,1},{4,6},{5,7},{6,4},{7,5},{8,10},{9,11},{10,... | collective-permute-start | bytes 1572872 | tf_op jit(solution)/shard_map/ppermute | solution.py:44
  35.2 47.8 %collective-permute-start.10 = (bf16[2,512,512]{2,1,0:T(8,128)(2,1)}, bf16[2,512,512]{2,1,0:T(8,128)(2,1)}, u32[]{:S(2)}, u32[]{:S(2)}) collective-permute-start(bf16[2,512,512]{2,1,0:T(8,128)(2,1)} %fence.10), channel_id=1, source_target_pairs={{0,33},{1,32},{2,35},{3,34},{4,37},{5,36},{6,39},{7,38},{8,41},{9,... | collective-permute-start | bytes 3145736 | tf_op jit(solution)/shard_map/ppermute | solution.py:44
  40.6 5.8 %collective-permute-start.6 = (bf16[3,48,512]{2,1,0:T(8,128)(2,1)}, bf16[3,48,512]{2,1,0:T(8,128)(2,1)S(1)}, u32[]{:S(2)}, u32[]{:S(2)}) collective-permute-start(bf16[3,48,512]{2,1,0:T(8,128)(2,1)} %get-tuple-element.65), channel_id=1, source_target_pairs={{0,1},{1,0},{2,3},{3,2},{4,5},{5,4},{6,7},{7,6},{8,9},{9,8},{10,11... | collective-permute-start | bytes 442376 | tf_op jit(solution)/shard_map/ppermute | solution.py:44
  41.0 7.0 %collective-permute-start.7 = (bf16[3,48,512]{2,1,0:T(8,128)(2,1)}, bf16[3,48,512]{2,1,0:T(8,128)(2,1)S(1)}, u32[]{:S(2)}, u32[]{:S(2)}) collective-permute-start(bf16[3,48,512]{2,1,0:T(8,128)(2,1)} %get-tuple-element.66), channel_id=1, source_target_pairs={{0,225},{1,0},{2,227},{3,2},{4,229},{5,4},{6,231},{7,6},{8,233},{9... | collective-permute-start | bytes 442376 | tf_op jit(solution)/shard_map/ppermute | solution.py:44
  49.5 19.8 %collective-permute-start.9 = (bf16[12,6,512]{2,1,0:T(8,128)(2,1)S(1)}, bf16[12,6,512]{2,1,0:T(8,128)(2,1)S(1)}, u32[]{:S(2)}, u32[]{:S(2)}) collective-permute-start(bf16[12,6,512]{2,1,0:T(8,128)(2,1)S(1)} %cot_edge.1.refs_13_), channel_id=1, source_target_pairs={{0,30},{1,31},{2,0},{3,1},{4,2},{5,3},{6,4},{7,5},{8,6},{9,7},{10,... | collective-permute-start | bytes 221192 | tf_op jit(solution)/shard_map/ppermute | solution.py:44
  83.0 9.1 %collective-permute-start.11 = (bf16[2,512,512]{2,1,0:T(8,128)(2,1)}, bf16[2,512,512]{2,1,0:T(8,128)(2,1)S(1)}, u32[]{:S(2)}, u32[]{:S(2)}) collective-permute-start(bf16[2,512,512]{2,1,0:T(8,128)(2,1)} %fence.11.w12_m), channel_id=1, source_target_pairs={{0,2},{1,3},{2,0},{3,1},{4,6},{5,7},{6,4},{7,5},{8,10},{9,11},{10,... | collective-permute-start | bytes 3145736 | tf_op jit(solution)/shard_map/ppermute | solution.py:44
  89.6 15.6 %collective-permute-start.14 = (bf16[4,2,8,16,512]{4,3,2,1,0:T(8,128)(2,1)}, bf16[4,2,8,16,512]{4,3,2,1,0:T(8,128)(2,1)S(1)}, u32[]{:S(2)}, u32[]{:S(2)}) collective-permute-start(bf16[4,2,8,16,512]{4,3,2,1,0:T(8,128)(2,1)} %get-tuple-element.89), channel_id=1, source_target_pairs={{0,2},{1,3},{2,0},{3,1},{4,6},{5,7},{6,4},{7,5},{8,10},{9,11},{10,... | collective-permute-start | bytes 3145736 | tf_op jit(solution)/shard_map/ppermute | solution.py:44
  105.5 16.0 %collective-permute-start.15 = (bf16[2,8,16,512]{3,2,1,0:T(8,128)(2,1)S(1)}, bf16[2,8,16,512]{3,2,1,0:T(8,128)(2,1)S(1)}, u32[]{:S(2)}, u32[]{:S(2)}) collective-permute-start(bf16[2,8,16,512]{3,2,1,0:T(8,128)(2,1)S(1)} %get-tuple-element.90), channel_id=1, source_target_pairs={{0,64},{1,65},{2,66},{3,67},{4,68},{5,69},{6,70},{7,71},{8,72},{9,... | collective-permute-start | bytes 786440 | tf_op jit(solution)/shard_map/ppermute | solution.py:44
  106.8 14.6 %collective-permute-start.16 = (bf16[2,8,16,512]{3,2,1,0:T(8,128)(2,1)S(1)}, bf16[2,8,16,512]{3,2,1,0:T(8,128)(2,1)S(1)}, u32[]{:S(2)}, u32[]{:S(2)}) collective-permute-start(bf16[2,8,16,512]{3,2,1,0:T(8,128)(2,1)S(1)} %get-tuple-element.91), channel_id=1, source_target_pairs={{0,128},{1,129},{2,130},{3,131},{4,132},{5,133},{6,134},{7,135},{8... | collective-permute-start | bytes 786440 | tf_op jit(solution)/shard_map/ppermute | solution.py:44
  109.2 13.6 %collective-permute-start.17 = (bf16[2,8,16,512]{3,2,1,0:T(8,128)(2,1)S(1)}, bf16[2,8,16,512]{3,2,1,0:T(8,128)(2,1)S(1)}, u32[]{:S(2)}, u32[]{:S(2)}) collective-permute-start(bf16[2,8,16,512]{3,2,1,0:T(8,128)(2,1)S(1)} %get-tuple-element.92), channel_id=1, source_target_pairs={{0,192},{1,193},{2,194},{3,195},{4,196},{5,197},{6,198},{7,199},{8... | collective-permute-start | bytes 786440 | tf_op jit(solution)/shard_map/ppermute | solution.py:44
  126.3 7.0 %collective-permute-start.18 = (bf16[4,2,2,8,16,256]{5,4,3,2,1,0:T(8,128)(2,1)S(1)}, bf16[4,2,2,8,16,256]{5,4,3,2,1,0:T(8,128)(2,1)S(1)}, u32[]{:S(2)}, u32[]{:S(2)}) collective-permute-start(bf16[4,2,2,8,16,256]{5,4,3,2,1,0:T(8,128)(2,1)S(1)} %get-tuple-element.94), channel_id=1, source_target_pairs={{0,2},{1,3},{2,0},{3,1},{4,6},{5,7},{6,4},{7,5},{8,10},{9,11},{10,... | collective-permute-start | bytes 3145736 | tf_op jit(solution)/shard_map/ppermute | solution.py:44
  128.4 23.2 %collective-permute-start.22 = (bf16[2,8,16,512]{3,2,1,0:T(8,128)(2,1)}, bf16[2,8,16,512]{3,2,1,0:T(8,128)(2,1)S(1)}, u32[]{:S(2)}, u32[]{:S(2)}) collective-permute-start(bf16[2,8,16,512]{3,2,1,0:T(8,128)(2,1)} %get-tuple-element.100), channel_id=1, source_target_pairs={{0,64},{1,65},{2,66},{3,67},{4,68},{5,69},{6,70},{7,71},{8,72},{9,... | collective-permute-start | bytes 786440 | tf_op jit(solution)/shard_map/ppermute | solution.py:44
  128.4 23.2 %collective-permute-start.23 = (bf16[2,8,16,512]{3,2,1,0:T(8,128)(2,1)}, bf16[2,8,16,512]{3,2,1,0:T(8,128)(2,1)S(1)}, u32[]{:S(2)}, u32[]{:S(2)}) collective-permute-start(bf16[2,8,16,512]{3,2,1,0:T(8,128)(2,1)} %get-tuple-element.101), channel_id=1, source_target_pairs={{0,128},{1,129},{2,130},{3,131},{4,132},{5,133},{6,134},{7,135},{8... | collective-permute-start | bytes 786440 | tf_op jit(solution)/shard_map/ppermute | solution.py:44
  130.1 21.5 %collective-permute-start.24 = (bf16[2,8,16,512]{3,2,1,0:T(8,128)(2,1)}, bf16[2,8,16,512]{3,2,1,0:T(8,128)(2,1)S(1)}, u32[]{:S(2)}, u32[]{:S(2)}) collective-permute-start(bf16[2,8,16,512]{3,2,1,0:T(8,128)(2,1)} %get-tuple-element.102), channel_id=1, source_target_pairs={{0,192},{1,193},{2,194},{3,195},{4,196},{5,197},{6,198},{7,199},{8... | collective-permute-start | bytes 786440 | tf_op jit(solution)/shard_map/ppermute | solution.py:44
  136.4 27.3 %collective-permute-start.19 = (bf16[3,48,512]{2,1,0:T(8,128)(2,1)}, bf16[3,48,512]{2,1,0:T(8,128)(2,1)S(1)}, u32[]{:S(2)}, u32[]{:S(2)}) collective-permute-start(bf16[3,48,512]{2,1,0:T(8,128)(2,1)} %get-tuple-element.96), channel_id=1, source_target_pairs={{0,1},{1,32},{2,3},{3,34},{4,5},{5,36},{6,7},{7,38},{8,9},{9,40},{... | collective-permute-start | bytes 442376 | tf_op jit(solution)/shard_map/ppermute | solution.py:44
  152.4 14.1 %collective-permute-start.25 = (bf16[2,2,8,16,256]{4,3,2,1,0:T(8,128)(2,1)}, bf16[2,2,8,16,256]{4,3,2,1,0:T(8,128)(2,1)S(1)}, u32[]{:S(2)}, u32[]{:S(2)}) collective-permute-start(bf16[2,2,8,16,256]{4,3,2,1,0:T(8,128)(2,1)} %get-tuple-element.106), channel_id=1, source_target_pairs={{0,64},{1,65},{2,66},{3,67},{4,68},{5,69},{6,70},{7,71},{8,72},{9,... | collective-permute-start | bytes 786440 | tf_op jit(solution)/shard_map/ppermute | solution.py:44
  152.4 14.1 %collective-permute-start.26 = (bf16[2,2,8,16,256]{4,3,2,1,0:T(8,128)(2,1)}, bf16[2,2,8,16,256]{4,3,2,1,0:T(8,128)(2,1)S(1)}, u32[]{:S(2)}, u32[]{:S(2)}) collective-permute-start(bf16[2,2,8,16,256]{4,3,2,1,0:T(8,128)(2,1)} %get-tuple-element.107), channel_id=1, source_target_pairs={{0,128},{1,129},{2,130},{3,131},{4,132},{5,133},{6,134},{7,135},{8... | collective-permute-start | bytes 786440 | tf_op jit(solution)/shard_map/ppermute | solution.py:44
  154.1 13.6 %collective-permute-start.27 = (bf16[2,2,8,16,256]{4,3,2,1,0:T(8,128)(2,1)}, bf16[2,2,8,16,256]{4,3,2,1,0:T(8,128)(2,1)S(1)}, u32[]{:S(2)}, u32[]{:S(2)}) collective-permute-start(bf16[2,2,8,16,256]{4,3,2,1,0:T(8,128)(2,1)} %get-tuple-element.108), channel_id=1, source_target_pairs={{0,192},{1,193},{2,194},{3,195},{4,196},{5,197},{6,198},{7,199},{8... | collective-permute-start | bytes 786440 | tf_op jit(solution)/shard_map/ppermute | solution.py:44
  156.3 10.2 %collective-permute-start.20 = (bf16[3,48,512]{2,1,0:T(8,128)(2,1)S(1)}, bf16[3,48,512]{2,1,0:T(8,128)(2,1)S(1)}, u32[]{:S(2)}, u32[]{:S(2)}) collective-permute-start(bf16[3,48,512]{2,1,0:T(8,128)(2,1)S(1)} %copy-done.67), channel_id=1, source_target_pairs={{0,1},{1,0},{2,3},{3,2},{4,5},{5,4},{6,7},{7,6},{8,9},{9,8},{10,11... | collective-permute-start | bytes 442376 | tf_op jit(solution)/shard_map/ppermute | solution.py:44
  233.6 9.8 %collective-permute-start.28 = (bf16[8,8,16,768]{3,2,1,0:T(8,128)(2,1)S(1)}, bf16[8,8,16,768]{3,2,1,0:T(8,128)(2,1)S(1)}, u32[]{:S(2)}, u32[]{:S(2)}) collective-permute-start(bf16[8,8,16,768]{3,2,1,0:T(8,128)(2,1)S(1)} %all_to_all.17.mine), channel_id=1, source_target_pairs={{0,2},{1,3},{2,0},{3,1},{4,6},{5,7},{6,4},{7,5},{8,10},{9,11},{10,... | collective-permute-start | bytes 4718600 | tf_op jit(solution)/shard_map/ppermute | solution.py:44
  (75 other events, 463.6 us)

commit v2 on v1

--- a/solution.py
+++ b/solution.py
@@ -20,7 +20,7 @@
 BF = jnp.bfloat16
 F32 = jnp.float32
 AXES = ("x", "yl", "z", "c", "tp")
-VMEM_LIMIT = 48 * 1024 * 1024
+MIB = 1024 * 1024
 
 
 def pairs_of(move):
@@ -99,77 +99,65 @@
         in_specs=[anywhere] * (n + len(after)),
         out_specs=tuple([anywhere] * n),
         input_output_aliases={i: i for i in range(n)},
+        compiler_params=pltpu.CompilerParams(vmem_limit_bytes=MIB),
         name="fence",
     )(*values, *after)
 
 
-def pieces_kernel(place, tile, near, far, below):
+def pieces_kernel(place, tile, cot, near, far, below):
     t = place[4]
-    for i in range(3):
-        near[i] = tile[9 + i - 6 * t]
-        far[i] = tile[i + 6 * t]
-        below[i] = tile[i]
-
-
-def band_pieces(place, tile, name):
-    return call(pieces_kernel, (tile,), [whole((3, 48, D))] * 3, place=place, name=name)
-
-
-def exchange_rows(pieces):
-    near, far, below = pieces
-    return flip(near, t=1), send(far, far_move), send(below, lat_move(-1))
-
-
-def edge_kernel(place, tile, near, far, below, edge):
+    for n, ref in enumerate((tile, cot)):
+        for i in range(3):
+            near[n, i] = ref[9 + i - 6 * t]
+            far[n, i] = ref[i + 6 * t]
+            below[n, i] = ref[i]
+
+
+def edge_kernel(place, tile, cot, near, far, below, edge):
     t = place[4]
-    for i in range(3):
-        edge[i] = tile[3 + i + 6 * t, :6]
-        edge[3 + i] = jnp.where(t == 0, tile[6 + i, :6].astype(F32), below[i, :6].astype(F32)).astype(BF)
-        edge[6 + i] = near[i, :6]
-        edge[9 + i] = far[i, :6]
-
-
-def first_columns(place, tile, rows, name, after=()):
-    kernel = without(edge_kernel, 5, len(after))
-    (edge,) = call(kernel, (tile, *rows), [whole((12, 6, D))], place=place, name=name, after=after)
-    return edge
-
-
-def half_of_attend_weights(place, w_qkv, w_out):
-    def kernel(place, wq, wo, out):
-        out[0:3] = wq[...]
-        out[3] = wo[...]
-
-    return halves(
-        kernel, place, (w_qkv, w_out), (4, 256, 256),
-        [((3, 256, 256), lambda i, p: (0, p[3], 0)), ((256, 256), lambda i, p: (0, p[3]))], "half_attend",
-    )
-
-
-def half_of_mlp_weights(place, w_fc1, w_fc2):
-    def kernel(place, w1, w2, out):
-        out[0] = w1[...]
-        out[1] = w2[...]
-
-    return halves(
-        kernel, place, (w_fc1, w_fc2), (2, 512, 512),
-        [((512, 512), lambda i, p: (0, p[3])), ((512, 512), lambda i, p: (p[3], 0))], "half_mlp",
-    )
-
-
-def halves(kernel, place, args, shape, specs, name):
+    for n, ref in enumerate((tile, cot)):
+        for i in range(3):
+            edge[n, i] = ref[3 + i + 6 * t, :6]
+            row = jnp.where(t == 0, ref[6 + i, :6].astype(F32), below[n, i, :6].astype(F32))
+            edge[n, 3 + i] = row.astype(BF)
+            edge[n, 6 + i] = near[n, i, :6]
+            edge[n, 9 + i] = far[n, i, :6]
+
+
+def weight_parts(place, w_qkv, w_out, w_fc1, w_fc2):
+    def kernel(place, wq, wo, w1, w2, attend, mlp):
+        attend[0:3] = wq[...]
+        attend[3] = wo[...]
+        mlp[0] = w1[...]
+        mlp[1, :, :512] = w2[:32]
+        mlp[1, :, 512:] = w2[32:]
+
+    specs = [
+        ((3, 64, 256), lambda i, p: (0, p[3] * 4 + p[0], 0)),
+        ((64, 256), lambda i, p: (p[0], p[3])),
+        ((32, 1024), lambda i, p: (p[2] * 2 + p[3], 0)),
+        ((64, 512), lambda i, p: (p[2] * 2 + p[3], 0)),
+    ]
+    shapes = ((4, 64, 256), (2, 32, 1024))
     return pl.pallas_call(
         kernel,
-        out_shape=whole(shape),
+        out_shape=tuple(whole(shape) for shape in shapes),
         grid_spec=pltpu.PrefetchScalarGridSpec(
             num_scalar_prefetch=1,
             grid=(1,),
             in_specs=[pl.BlockSpec(block, index) for block, index in specs],
-            out_specs=pl.BlockSpec(shape, lambda i, p: (0,) * len(shape)),
+            out_specs=tuple(pl.BlockSpec(shape, lambda i, p: (0, 0, 0)) for shape in shapes),
         ),
-        compiler_params=pltpu.CompilerParams(vmem_limit_bytes=VMEM_LIMIT),
-        name=name,
-    )(place, *args)
+        compiler_params=pltpu.CompilerParams(vmem_limit_bytes=4 * MIB),
+        name="weight_parts",
+    )(place, w_qkv, w_out, w_fc1, w_fc2)
+
+
+def join_kernel(place, *refs):
+    out = refs[4]
+    rows = refs[0].shape[1]
+    for k in range(4):
+        out[:, pl.ds(pl.multiple_of((place[0] ^ k) * rows, rows), rows), :] = refs[k][...]
 
 
 def to_windows(band):
@@ -177,18 +165,18 @@
     return band.reshape(12, WINS, WLON, width).transpose(1, 0, 2, 3).reshape(TOK, width)
 
 
-def load_windows(t, tile, near, far, below, moved, stage, wins):
+def load_windows(t, n, tile, near, far, below, moved, stage, wins):
     for row in range(12):
         if row < 3:
             value = tile[3 + row + 6 * t].astype(F32)
         elif row < 6:
-            value = jnp.where(t == 0, tile[3 + row].astype(F32), below[row - 3].astype(F32))
+            value = jnp.where(t == 0, tile[3 + row].astype(F32), below[n, row - 3].astype(F32))
         elif row < 9:
-            value = near[row - 6].astype(F32)
+            value = near[n, row - 6].astype(F32)
         else:
-            value = far[row - 9].astype(F32)
+            value = far[n, row - 9].astype(F32)
         stage[row, 0:48] = value
-        stage[row, 48:54] = moved[row].astype(F32)
+        stage[row, 48:54] = moved[n, row].astype(F32)
         for w in range(WINS):
             start = w * SEATS + row * WLON
             wins[start : start + WLON, :] = stage[row, 6 + 12 * w : 18 + 12 * w]
@@ -234,7 +222,7 @@
     c = place[3]
     mine = pl.ds(pl.multiple_of(c * 256, 256), 256)
     sibs = pl.ds(pl.multiple_of((1 - c) * 256, 256), 256)
-    load_windows(place[4], tile, near, far, below, moved, stage, wins)
+    load_windows(place[4], 0, tile, near, far, below, moved, stage, wins)
     x = wins[...]
     normed = norm(x, g1[...])[0]
     n1_scr[...] = normed.astype(BF)
@@ -309,7 +297,7 @@
     hid_scr, dpre_scr, stage, wins,
 ):
     mx, c = place[0], place[3]
-    load_windows(place[4], tile, near, far, below, moved, stage, wins)
+    load_windows(place[4], 1, tile, near, far, below, moved, stage, wins)
     mixed = mixed_ref[...].astype(F32)
     normed = norm(mixed, g2[...])[0]
     n2_ref[...] = normed.astype(BF)
@@ -328,22 +316,23 @@
 
 
 def mlp_other_kernel(
-    place, mixed_ref, n2_ref, n2t, cot_ref, cott, out_acc, norm_acc, g2, w12_m, w12_s,
+    place, mixed_ref, n2_ref, n2t, cot_ref, cott, out_acc, norm_acc, g2, gathered,
     band, tail, dm_ref, keep, away,
-    hid_scr, dpre_scr, stage, wins,
+    hid_scr, dpre_scr, stage, wins, w1, w2,
 ):
     mx, c = place[0], place[3]
     n2, cot = n2_ref[...], cot_ref[...]
-    for n, (pair, half) in enumerate(((w12_m, c), (w12_s, 1 - c))):
-        for i in range(2):
-            cols = slice(i * 256, i * 256 + 256)
-            hidden, dpre = mlp_block(pair.at[0], pair.at[1], cols, n2, cot)
-            hid_scr[:, n * 512 + i * 256 : n * 512 + i * 256 + 256] = hidden
-            dpre_scr[:, n * 512 + i * 256 : n * 512 + i * 256 + 256] = dpre
-            store_grads(n2t, cott, hidden, dpre, ((2 * half + i) ^ mx,), c, keep, away)
-    d_norm = norm_acc[...] + (
-        dot_nt(dpre_scr[:, :512], w12_m[0]) + dot_nt(dpre_scr[:, 512:], w12_s[0])
-    )
+    for p in range(16):
+        w1[32 * p : 32 * p + 32, :] = gathered[p, 0]
+        w2[64 * p : 64 * p + 32, :] = gathered[p, 1, :, :512]
+        w2[64 * p + 32 : 64 * p + 64, :] = gathered[p, 1, :, 512:]
+    for x in range(4):
+        cols = slice(x * 256, x * 256 + 256)
+        hidden, dpre = mlp_block(w1, w2, cols, n2, cot)
+        hid_scr[:, cols] = hidden
+        dpre_scr[:, cols] = dpre
+        store_grads(n2t, cott, hidden, dpre, (x ^ mx,), c, keep, away)
+    d_norm = norm_acc[...] + dot_nt(dpre_scr[...], w1[...])
     gain = g2[...]
     xhat, rstd = norm(mixed_ref[...].astype(F32), gain)[1:]
     scaled = d_norm * gain
@@ -353,7 +342,7 @@
         - xhat * jnp.mean(scaled * xhat, -1, keepdims=True)
     )
     dm_ref[...] = dm.astype(BF)
-    wins[...] = out_acc[...] + (dot(hid_scr[:, :512], w12_m[1]) + dot(hid_scr[:, 512:], w12_s[1]))
+    wins[...] = out_acc[...] + dot(hid_scr[...], w2[...])
     store_windows(wins, stage, band, tail)
 
 
@@ -398,7 +387,7 @@
 
 
 def attend_grads_kernel(
-    place, dqkv, dmt, heads_ref, n1t_ref, first, second, third,
+    place, dqkv, dmt, heads_ref, n1t_ref, first, second, third, fourth, fifth,
     keep, away,
 ):
     mx, c, mt = place[0], place[3], place[4]
@@ -423,7 +412,7 @@
     return jax.ShapeDtypeStruct(shape, dtype)
 
 
-def call(kernel, args, outs, scratch=(), place=None, flops=0, name=None, after=()):
+def call(kernel, args, outs, scratch=(), place=None, flops=0, name=None, after=(), limit=8):
     spec = pl.BlockSpec(memory_space=pltpu.VMEM)
     specs = [spec] * len(args) + [pl.BlockSpec(memory_space=pl.ANY)] * len(after)
     args = tuple(args) + tuple(after)
@@ -437,7 +426,7 @@
         in_specs=specs,
         out_specs=tuple([spec] * len(outs)),
         scratch_shapes=list(scratch),
-        compiler_params=pltpu.CompilerParams(vmem_limit_bytes=VMEM_LIMIT),
+        compiler_params=pltpu.CompilerParams(vmem_limit_bytes=limit * MIB),
         cost_estimate=pl.CostEstimate(flops=flops, bytes_accessed=size, transcendentals=0),
         name=name,
     )(*args)
@@ -455,11 +444,17 @@
         outs[x][...] = add(keep[x], arrived[x])
 
 
+def core_sum_two_kernel(keep, arrived, keep_two, arrived_two, *outs):
+    for x in range(4):
+        outs[x][0] = add(keep[x], arrived[x])
+        outs[x][1] = add(keep_two[x], arrived_two[x])
+
+
 def x_sum_kernel(place, *refs):
-    own, other, at, out = refs[0:4], refs[4:8], refs[8:12], refs[-1]
+    fc, at, out = refs[0:4], refs[4:8], refs[-1]
     t = place[4]
-    out[t, :, :, :, :512] = add(*[r[...] for r in own])
-    out[1 - t, :, :, :, :512] = add(*[r[...] for r in other])
+    out[t, :, :, :, :512] = add(*[r[0] for r in fc])
+    out[1 - t, :, :, :, :512] = add(*[r[1] for r in fc])
     out[:, :, :, :, 512:] = add(*[r[...] for r in at])
 
 
@@ -498,18 +493,24 @@
     go[...] = scro[...].astype(F32).T.astype(BF)
 
 
-def core_phase(keep, away):
+def core_phase(keep, away, after):
     outs = [whole(keep.shape[1:])] * 4
-    return call(core_sum_kernel, (keep, flip(away, c=1)), outs, name="core_sum")
+    kernel = without(core_sum_kernel, 2, len(after))
+    return call(kernel, (keep, flip(away, c=1)), outs, name="core_sum", after=after)
+
+
+def core_phase_two(keep, arrived, keep_two, arrived_two):
+    outs = [whole((2,) + keep.shape[1:])] * 4
+    return call(core_sum_two_kernel, (keep, arrived, keep_two, arrived_two), outs, name="core_sum_two")
 
 
 def x_phase(cut):
     return [cut[0]] + [flip(cut[k], x=k) for k in (1, 2, 3)]
 
 
-def reduce_and_gather(place, own, other, at, after):
+def reduce_and_gather(place, fc, at, after):
     (total,) = call(
-        x_sum_kernel, (*own, *other, *at), [whole((2, 2, 8, 16, 768))], (), place, name="x_sum", after=after
+        x_sum_kernel, (*fc, *at), [whole((2, 2, 8, 16, 768))], (), place, name="x_sum", after=after
     )
     parts = lax.all_to_all(total.reshape(32, 16, 768), ("tp", "yl", "z"), 0, 0)
     (chunks,) = call(last_sum_kernel, (parts,), [whole((8, 16, 768))], name="last_sum")
@@ -527,20 +528,24 @@
     place = jnp.stack([x, yl, z, c, t]).astype(jnp.int32)
     tile, cot = tokens[0], cotangent[0]
 
-    pieces = band_pieces(place, tile, "pieces")
-    rows = exchange_rows(pieces)
-    (wqo,) = fence((half_of_attend_weights(place, w_qkv, w_out),), (pieces[0],))
-    wqo = flip(wqo, yl=1, t=1)
-    edge = first_columns(place, tile, rows, "edge")
+    part_attend, part_mlp = weight_parts(place, w_qkv, w_out, w_fc1, w_fc2)
+    wqo = flip(part_attend, yl=1, t=1)
+    pieces = call(pieces_kernel, (tile, cot), [whole((2, 3, 48, D))] * 3, (), place, name="pieces")
+    rows = (flip(pieces[0], t=1), send(pieces[1], far_move), send(pieces[2], lat_move(-1)))
+    (edge,) = call(edge_kernel, (tile, cot, *rows), [whole((2, 12, 6, D))], (), place, name="edge")
     moved = send(edge, lon_move(-1))
-    (wqo,) = fence((wqo,), (edge,))
-
-    cot_rows = exchange_rows(fence(band_pieces(place, cot, "cot_pieces"), (edge,)))
+    wqo, w12 = fence((wqo, flip(part_mlp, yl=1, t=1)), (edge,))
+    w12 = lax.all_gather(w12, ("z", "c"), axis=0)
+    (wqo,) = call(
+        without(join_kernel, 5, 1),
+        [wqo] + [flip(wqo, x=k) for k in (1, 2, 3)],
+        [whole((4, 256, 256))],
+        (),
+        place,
+        name="join",
+        after=(moved,),
+    )
     wqo_sib = flip(wqo, c=1)
-    (w12,) = fence((half_of_mlp_weights(place, w_fc1, w_fc2),), (wqo, moved))
-    w12 = flip(w12, yl=1, t=1)
-    cot_edge = first_columns(place, cot, cot_rows, "cot_edge", (moved,))
-    cot_moved = send(cot_edge, lon_move(-1))
 
     band = lax.dynamic_slice_in_dim(labels, t * 6, 6, 1)
     band = jnp.where(t == 0, band, band[::-1]).reshape(12, 48, 1)
@@ -550,7 +555,7 @@
 
     stage = [pltpu.VMEM((12, 56, D), F32), pltpu.VMEM((TOK, D), F32)]
     n1t, qkv, prob, heads, wo_full, mixed = call(
-        without(attend_kernel, 13, 1),
+        attend_kernel,
         (tile, *rows, moved, labc, labr, gain_one[None], w_qkv, w_out, wqo, wqo_sib),
         [
             whole((D, TOK)), whole((TOK, 3 * D)), whole((WINS * 8, SEATS, SEATS)),
@@ -560,37 +565,37 @@
         place,
         flops=3 * 10**9,
         name="attend",
-        after=(cot_edge,),
+        limit=12,
     )
     grads = [whole((4, 2, 8, 16, 512))] * 2
     scratch = [pltpu.VMEM((TOK, 1024), BF), pltpu.VMEM((TOK, 1024), BF)] + stage
     tokens_like = [whole((TOK, D)), whole((D, TOK))] * 2 + [whole((TOK, D), F32)] * 2
     *carried, keep, away = call(
         mlp_own_kernel,
-        (mixed, cot, *cot_rows, cot_moved, second_norm_gain[None], w_fc1, w_fc2),
+        (mixed, cot, *rows, moved, second_norm_gain[None], w_fc1, w_fc2),
         tokens_like + grads,
         scratch,
         place,
         flops=4 * 10**9,
         name="mlp_own",
-    )
-    own = (keep, away)
-    (w12,) = fence((w12,), (keep,))
-    w12_sib = flip(w12, c=1)
-    out_band, tail, dm, *other = call(
+        limit=12,
+    )
+    arrived = flip(away, c=1)
+    out_band, tail, dm, keep_two, away_two = call(
         mlp_other_kernel,
-        (mixed, *carried, second_norm_gain[None], w12, w12_sib),
+        (mixed, *carried, second_norm_gain[None], w12),
         [whole((12, 48, D)), whole((12, 6, D)), whole((TOK, D))] + grads,
-        scratch,
+        scratch + [pltpu.VMEM((D, 1024), BF), pltpu.VMEM((1024, D), BF)],
         place,
         flops=4 * 10**9,
         name="mlp_other",
-    )
-    own_cut = core_phase(*own)
-    own_parts = x_phase(own_cut)
-    other_cut = core_phase(*other)
-    other_parts = x_phase(other_cut)
+        limit=12,
+    )
+    fc_cut = core_phase_two(keep, arrived, keep_two, flip(away_two, c=1))
+    fc_parts = x_phase(fc_cut)
     out_moved = send(tail, lon_move(1))
+    out = jnp.concatenate([out_moved, out_band[:, 6:]], 1)
+    near, far, above = flip(out[6:9], t=1), send(out[9:12], far_back), send(out[3:6], lat_move(1))
     dqkv, dmt = call(
         attend_back_kernel,
         (dm, prob, qkv, wo_full),
@@ -598,7 +603,8 @@
         [pltpu.VMEM((TOK, D), BF)],
         flops=4 * 10**9,
         name="attend_back",
-        after=(other_cut[0], out_moved),
+        limit=12,
+        after=(fc_cut[0], out_moved),
     )
     at = call(
         attend_grads_kernel,
@@ -608,15 +614,12 @@
         place,
         flops=1 * 10**9,
         name="attend_grads",
-        after=own_parts[1:],
-    )
-    at_cut = core_phase(*at)
-    at_parts = x_phase((at_cut[0], *fence(at_cut[1:], other_parts[1:])))
-
-    out = jnp.concatenate([out_moved, out_band[:, 6:]], 1)
-    near, far, above = fence((out[6:9], out[9:12], out[3:6]), (at_cut[0],))
-    near, far, above = flip(near, t=1), send(far, far_back), send(above, lat_move(1))
-    gq, go, g1, g2 = reduce_and_gather(place, own_parts, other_parts, at_parts, (near, far, above))
+        limit=12,
+        after=(fc_parts[1], fc_parts[3], near, far, above),
+    )
+    at_cut = core_phase(*at, ())
+    at_parts = x_phase(at_cut)
+    gq, go, g1, g2 = reduce_and_gather(place, fc_parts, at_parts, (above,))
     out = jnp.where(
         t == 0,
         jnp.concatenate([far, out[0:6], near], 0),

time: 247 us -> 231 us (0.935)
  starting transfers between devices: 78.5 us -> 40.9 us
  waiting for transfers between devices: 20.5 us -> 45.9 us
  between operations: 1.17 us -> 14.4 us
  Pallas kernels: 48.9 us -> 38 us
  blocking collectives: 61.9 us -> 58.4 us
    ppermute x29 -> x24, starting transfers between devices: 78.5 us -> 40.9 us  [send(): return lax.ppermute(value, AXES, pairs_of(move))]
    ppermute x29 -> x24, waiting for transfers between devices: 20.5 us -> 45.9 us  [send(): return lax.ppermute(value, AXES, pairs_of(move))]
    pallas_call x16 -> x14, Pallas kernels: 47.7 us -> 37.4 us  [call(): pl.pallas_call(kernel, out_shape=tuple(outs), in_specs=specs, out_specs=t...]
    all_to_all x1, blocking collectives: 30.4 us -> 24.7 us  [reduce_and_gather(): parts = lax.all_to_all(total.reshape(32, 16, 768), ('tp', 'yl', 'z'), 0, 0)]
    unnamed x140 -> x92, local copies, waits for them, and re-layouts: 32.6 us -> 30.3 us
  transfers between devices with their start and end apart: 29 -> 25, of which waited for: 9 -> 13; matrix products, arithmetic and copies ran while one was open for 1% -> 1% of each run, Pallas kernels for 16% -> 13%
where the time goes in v2:
time: 231 us; the launch traced here: 230 us
  blocking collectives  58.4 us (25%)
  waiting for transfers between devices  45.9 us (20%)
  starting transfers between devices  40.9 us (18%)
  Pallas kernels  38 us (16%)
  local copies, waits for them, and re-layouts  30.9 us (13%)
  between operations  14.4 us (6%)
    ppermute x24, waiting for transfers between devices, send(): return lax.ppermute(value, AXES, pairs_of(move))  45.9 us
    ppermute x24, starting transfers between devices, send(): return lax.ppermute(value, AXES, pairs_of(move))  40.9 us
    pallas_call x14, Pallas kernels, call(): pl.pallas_call(kernel, out_shape=tuple(outs), in_specs=specs, out_specs=t...  37.4 us
    unnamed x92, local copies, waits for them, and re-layouts  30.3 us
    all_to_all x1, blocking collectives, reduce_and_gather(): parts = lax.all_to_all(total.reshape(32, 16, 768), ('tp', 'yl', 'z'), 0, 0)  24.7 us
    all_to_all x1, blocking collectives, reduce_and_gather(): mine = lax.all_to_all(columns, ('x', 'yl'), 0, 0)  19.8 us
    all_to_all x1, blocking collectives, reduce_and_gather(): column = lax.all_to_all(chunks, 'z', 0, 0)  13.9 us
  transfers between devices with their start and end apart: 25, of which 13 were waited for; matrix products, arithmetic and copies ran while one was open for 1% of the time, Pallas kernels for 13%

profile of v2, /device:TPU:1, one launch (start us, length us, event | category | flops | bytes accessed | tf_op | source)
XLA Modules:
  0.0 229.8 jit_solution(8062174084470350829)
XLA Ops:
  10.0 3.8 %collective-permute-start = (bf16[2,3,48,512]{3,2,1,0:T(8,128)(2,1)S(1)}, bf16[2,3,48,512]{3,2,1,0:T(8,128)(2,1)S(1)}, u32[]{:S(2)}, u32[]{:S(2)}) collective-permute-start(bf16[2,3,48,512]{3,2,1,0:T(8,128)(2,1)S(1)} %get-tuple-element.47), channel_id=1, source_target_pairs={{0,1},{1,0},{2,3},{3,2},{4,5},{5,4},{6,7},{7,6},{8,9},{9,8},{10,11... | collective-permute-start | bytes 884744 | tf_op jit(solution)/shard_map/ppermute | solution.py:44
  13.9 3.0 %collective-permute-start.1 = (bf16[2,3,48,512]{3,2,1,0:T(8,128)(2,1)S(1)}, bf16[2,3,48,512]{3,2,1,0:T(8,128)(2,1)S(1)}, u32[]{:S(2)}, u32[]{:S(2)}) collective-permute-start(bf16[2,3,48,512]{3,2,1,0:T(8,128)(2,1)S(1)} %get-tuple-element.48), channel_id=1, source_target_pairs={{0,225},{1,0},{2,227},{3,2},{4,229},{5,4},{6,231},{7,6},{8,233},{9... | collective-permute-start | bytes 884744 | tf_op jit(solution)/shard_map/ppermute | solution.py:44
  24.2 7.0 %collective-permute-done.1.far = bf16[2,3,48,512]{3,2,1,0:T(8,128)(2,1)S(1)} collective-permute-done((bf16[2,3,48,512]{3,2,1,0:T(8,128)(2,1)S(1)}, bf16[2,3,48,512]{3,2,1,0:T(8,128)(2,1)S(1)}, u32[]{:S(2)}, u32[]{:S(2)}) %collective-permute-start.1) | collective-permute-done | bytes 294944 | tf_op jit(solution)/shard_map/ppermute | solution.py:44
  32.4 2.9 %collective-permute-done.5.refs_1_ = bf16[2,32,1024]{2,1,0:T(8,128)(2,1)} collective-permute-done((bf16[2,32,1024]{2,1,0:T(8,128)(2,1)S(1)}, bf16[2,32,1024]{2,1,0:T(8,128)(2,1)}, u32[]{:S(2)}, u32[]{:S(2)}) %collective-permute-start.5) | collective-permute-done | bytes 131104 | tf_op jit(solution)/shard_map/ppermute | solution.py:44
  35.4 2.1 collective-permute-start.3
  45.1 5.6 %collective-permute-start.9 = (bf16[4,256,256]{2,1,0:T(8,128)(2,1)S(1)}, bf16[4,256,256]{2,1,0:T(8,128)(2,1)}, u32[]{:S(2)}, u32[]{:S(2)}) collective-permute-start(bf16[4,256,256]{2,1,0:T(8,128)(2,1)S(1)} %join.1.wqo_m), channel_id=1, source_target_pairs={{0,2},{1,3},{2,0},{3,1},{4,6},{5,7},{6,4},{7,5},{8,10},{9,11},{10,... | collective-permute-start | bytes 1572872 | tf_op jit(solution)/shard_map/ppermute | solution.py:44
  57.5 7.4 %attend.1 = (bf16[512,576]{1,0:T(8,128)(2,1)S(1)}, bf16[576,1536]{1,0:T(8,128)(2,1)S(1)}, bf16[32,144,144]{2,1,0:T(8,128)(2,1)S(1)}, bf16[576,512]{1,0:T(8,128)(...) custom-call(s32[5]{0:T(128)S(1)} %stack.23.place.refs_0_, bf16[12,48,512]{2,1,0:T(8,128)(2,1)S(1)} %bitcast.26, ...), custom_call_target="tpu_custom_call" | custom-call | flops 3000000000 | bytes 9424916 | tf_op jit(solution)/shard_map/attend/pallas_call | solution.py:423
  68.3 6.7 %mlp_own.1 = (bf16[576,512]{1,0:T(8,128)(2,1)S(1)}, bf16[512,576]{1,0:T(8,128)(2,1)S(1)}, bf16[576,512]{1,0:T(8,128)(2,1)S(1)}, bf16[512,576]{1,0:T(8,128)(2,1)S...) custom-call(s32[5]{0:T(128)S(1)} %stack.23.place.refs_0_, ...), custom_call_target="tpu_custom_call" | custom-call | flops 4000000000 | bytes 11126804 | tf_op jit(solution)/shard_map/mlp_own/pallas_call | solution.py:423
  90.5 6.2 %mlp_other.1 = (bf16[12,48,512]{2,1,0:T(8,128)(2,1)S(1)}, bf16[12,6,512]{2,1,0:T(8,128)(2,1)S(1)}, bf16[576,512]{1,0:T(8,128)(2,1)S(1)}, bf16[4,2,8,16,512]{4,3,...) custom-call(s32[5]{0:T(128)S(1)} %stack.23.place.refs_0_, bf16[576,512]{1,0:T(8,128)(2,1)S(1)} %copy-done.38, ...), custom_call_target="tpu_custom_call" | custom-call | flops 4000000000 | bytes 10758164 | tf_op jit(solution)/shard_map/mlp_other/pallas_call | solution.py:423
  97.1 2.4 %collective-permute-done.15.arrived_two = bf16[4,2,8,16,512]{4,3,2,1,0:T(8,128)(2,1)S(1)} collective-permute-done((bf16[4,2,8,16,512]{4,3,2,1,0:T(8,128)(2,1)S(1)}, bf16[4,2,8,16,512]{4,3,2,1,0:T(8,128)(2,1)S(1)}, u32[]{:S(2)}, u32[]{:S(2)}) %collective-permute-start.15) | collective-permute-done | bytes 1048608 | tf_op jit(solution)/shard_map/ppermute | solution.py:44
  103.7 3.6 %collective-permute-start.11 = (bf16[3,48,512]{2,1,0:T(8,128)(2,1)S(1)}, bf16[3,48,512]{2,1,0:T(8,128)(2,1)S(1)}, u32[]{:S(2)}, u32[]{:S(2)}) collective-permute-start(bf16[3,48,512]{2,1,0:T(8,128)(2,1)S(1)} %get-tuple-element.90), channel_id=1, source_target_pairs={{0,1},{1,32},{2,3},{3,34},{4,5},{5,36},{6,7},{7,38},{8,9},{9,40},{... | collective-permute-start | bytes 442376 | tf_op jit(solution)/shard_map/ppermute | solution.py:44
  107.7 8.0 %attend_back.1 = (bf16[576,1536]{1,0:T(8,128)(2,1)S(1)}, bf16[512,576]{1,0:T(8,128)(2,1)S(1)}) custom-call(bf16[576,512]{1,0:T(8,128)(2,1)S(1)} %get-tuple-element.71.dm_ref, bf16[32,144,144]{2,1,0:T(8,128)(2,1)S(1)} %copy-done.26, bf16[576,1536]{1,0:T(8,128)(2,1)S(1)} %copy-done.28, bf16[512,512]{1,0:T(8,128)(2,1)S(1)} %copy-done.44, ...), custom_call_target="tpu_custom_call" | custom-call | flops 4000000000 | bytes 7168000 | tf_op jit(solution)/shard_map/attend_back/pallas_call | solution.py:423
  115.7 6.6 %collective-permute-done.11.fourth = bf16[3,48,512]{2,1,0:T(8,128)(2,1)S(1)} collective-permute-done((bf16[3,48,512]{2,1,0:T(8,128)(2,1)S(1)}, bf16[3,48,512]{2,1,0:T(8,128)(2,1)S(1)}, u32[]{:S(2)}, u32[]{:S(2)}) %collective-permute-start.11) | collective-permute-done | bytes 147488 | tf_op jit(solution)/shard_map/ppermute | solution.py:44
  122.3 2.6 %attend_grads.1 = (bf16[4,2,2,8,16,256]{5,4,3,2,1,0:T(8,128)(2,1)S(1)}, bf16[4,2,2,8,16,256]{5,4,3,2,1,0:T(8,128)(2,1)S(1)}) custom-call(s32[5]{0:T(128)S(1)} %stack.23.place.refs_0_, bf16[576,1536]{1,0:T(8,128)(2,1)S(1)} %get-tuple-element.75.dqkv, bf16[512,576]{1,0:T(8,128)(2,1)S(1)} %get-tuple-element.76.dmt, bf16[576,512]{1,0:T(8,128)(2,1)S(1)} %copy-done.10, ...), custom_call_target="tpu_custom_call" | custom-call | flops 1000000000 | bytes 7127060 | tf_op jit(solution)/shard_map/attend_grads/pallas_call | solution.py:423
  130.3 2.5 %collective-permute-start.22 = (bf16[2,2,8,16,256]{4,3,2,1,0:T(8,128)(2,1)S(1)}, bf16[2,2,8,16,256]{4,3,2,1,0:T(8,128)(2,1)S(1)}, u32[]{:S(2)}, u32[]{:S(2)}) collective-permute-start(bf16[2,2,8,16,256]{4,3,2,1,0:T(8,128)(2,1)S(1)} %get-tuple-element.84), channel_id=1, source_target_pairs={{0,192},{1,193},{2,194},{3,195},{4,196},{5,197},{6,198},{7,199},{8... | collective-permute-start | bytes 786440 | tf_op jit(solution)/shard_map/ppermute | solution.py:44
  132.8 8.5 %collective-permute-done.17.refs_2_ = bf16[2,2,8,16,512]{4,3,2,1,0:T(8,128)(2,1)S(1)} collective-permute-done((bf16[2,2,8,16,512]{4,3,2,1,0:T(8,128)(2,1)S(1)}, bf16[2,2,8,16,512]{4,3,2,1,0:T(8,128)(2,1)S(1)}, u32[]{:S(2)}, u32[]{:S(2)}) %collective-permute-start.17) | collective-permute-done | bytes 524320 | tf_op jit(solution)/shard_map/ppermute | solution.py:44
  141.3 3.3 %collective-permute-done.20.refs_5_ = bf16[2,2,8,16,256]{4,3,2,1,0:T(8,128)(2,1)S(1)} collective-permute-done((bf16[2,2,8,16,256]{4,3,2,1,0:T(8,128)(2,1)S(1)}, bf16[2,2,8,16,256]{4,3,2,1,0:T(8,128)(2,1)S(1)}, u32[]{:S(2)}, u32[]{:S(2)}) %collective-permute-start.20) | collective-permute-done | bytes 262176 | tf_op jit(solution)/shard_map/ppermute | solution.py:44
  144.6 8.0 %collective-permute-done.21.refs_6_ = bf16[2,2,8,16,256]{4,3,2,1,0:T(8,128)(2,1)S(1)} collective-permute-done((bf16[2,2,8,16,256]{4,3,2,1,0:T(8,128)(2,1)S(1)}, bf16[2,2,8,16,256]{4,3,2,1,0:T(8,128)(2,1)S(1)}, u32[]{:S(2)}, u32[]{:S(2)}) %collective-permute-start.21) | collective-permute-done | bytes 262176 | tf_op jit(solution)/shard_map/ppermute | solution.py:44
  153.5 24.7 %all_to_all.15.parts = bf16[32,16,768]{2,1,0:T(8,128)(2,1)S(1)} all-to-all(bf16[32,16,768]{2,1,0:T(8,128)(2,1)S(1)} %bitcast.23), channel_id=1, replica_groups=mesh['x'=4,'yl'=2,'z'=8,'c'=2,'tp'=2] {'tp','yl','z'}, dimensions={0} | all-to-all | bytes 1572864 | tf_op jit(solution)/shard_map/all_to_all | solution.py:515
  178.3 13.9 %all_to_all.16.part = bf16[8,16,768]{2,1,0:T(8,128)(2,1)S(1)} all-to-all(bf16[8,16,768]{2,1,0:T(8,128)(2,1)S(1)} %last_sum.1), channel_id=1, replica_groups=mesh['x'=4,'yl'=2,'z'=8,'c'=2,'tp'=2] {'z'}, dimensions={0} | all-to-all | bytes 393216 | tf_op jit(solution)/shard_map/all_to_all | solution.py:517
  192.3 19.8 %all_to_all.17.mine = bf16[8,8,16,768]{3,2,1,0:T(8,128)(2,1)S(1)} all-to-all(bf16[8,8,16,768]{3,2,1,0:T(8,128)(2,1)S(1)} %copies.1), channel_id=1, replica_groups=mesh['x'=4,'yl'=2,'z'=8,'c'=2,'tp'=2] {'x','yl'}, dimensions={0} | all-to-all | bytes 3145728 | tf_op jit(solution)/shard_map/all_to_all | solution.py:519
  212.1 5.0 %collective-permute-start.23 = (bf16[8,8,16,768]{3,2,1,0:T(8,128)(2,1)S(1)}, bf16[8,8,16,768]{3,2,1,0:T(8,128)(2,1)S(1)}, u32[]{:S(2)}, u32[]{:S(2)}) collective-permute-start(bf16[8,8,16,768]{3,2,1,0:T(8,128)(2,1)S(1)} %all_to_all.17.mine), channel_id=1, source_target_pairs={{0,2},{1,3},{2,0},{3,1},{4,6},{5,7},{6,4},{7,5},{8,10},{9,11},{10,... | collective-permute-start | bytes 4718600 | tf_op jit(solution)/shard_map/ppermute | solution.py:44
  218.1 2.0 collective-permute-done.23.sib
  220.1 2.8 %place.1 = (bf16[3,512,256]{2,1,0:T(8,128)(2,1)}, bf16[256,512]{1,0:T(8,128)(2,1)}, bf16[512,1024]{1,0:T(8,128)(2,1)}, bf16[1024,512]{1,0:T(8,128)(2,1)}) custom-call(s32[5]{0:T(128)S(1)} %stack.23.place.refs_0_, bf16[8,8,16,768]{3,2,1,0:T(8,128)(2,1)S(1)} %all_to_all.17.mine, bf16[8,8,16,768]{3,2,1,0:T(8,128)(2,1)S(1)} %collective-permute-done.23.sib), custom_call_target="tpu_custom_call" | custom-call | bytes 6291476 | tf_op jit(solution)/shard_map/place/pallas_call | solution.py:423
  (153 shorter events, 57.0 us)
Async XLA Ops:
  7.2 73.8 %all-gather.3.cloned.1.call-start = ((), (), s32[]{:S(2)}) async-start(), calls=%async_computation.3 | async-start | bytes 2228224 | tf_op jit(solution)/shard_map/all_gather | solution.py:538
  10.0 14.1 %collective-permute-start = (bf16[2,3,48,512]{3,2,1,0:T(8,128)(2,1)S(1)}, bf16[2,3,48,512]{3,2,1,0:T(8,128)(2,1)S(1)}, u32[]{:S(2)}, u32[]{:S(2)}) collective-permute-start(bf16[2,3,48,512]{3,2,1,0:T(8,128)(2,1)S(1)} %get-tuple-element.47), channel_id=1, source_target_pairs={{0,1},{1,0},{2,3},{3,2},{4,5},{5,4},{6,7},{7,6},{8,9},{9,8},{10,11... | collective-permute-start | bytes 884744 | tf_op jit(solution)/shard_map/ppermute | solution.py:44
  13.9 17.3 %collective-permute-start.1 = (bf16[2,3,48,512]{3,2,1,0:T(8,128)(2,1)S(1)}, bf16[2,3,48,512]{3,2,1,0:T(8,128)(2,1)S(1)}, u32[]{:S(2)}, u32[]{:S(2)}) collective-permute-start(bf16[2,3,48,512]{3,2,1,0:T(8,128)(2,1)S(1)} %get-tuple-element.48), channel_id=1, source_target_pairs={{0,225},{1,0},{2,227},{3,2},{4,229},{5,4},{6,231},{7,6},{8,233},{9... | collective-permute-start | bytes 884744 | tf_op jit(solution)/shard_map/ppermute | solution.py:44
  16.8 14.3 %collective-permute-start.2 = (bf16[2,3,48,512]{3,2,1,0:T(8,128)(2,1)S(1)}, bf16[2,3,48,512]{3,2,1,0:T(8,128)(2,1)S(1)}, u32[]{:S(2)}, u32[]{:S(2)}) collective-permute-start(bf16[2,3,48,512]{3,2,1,0:T(8,128)(2,1)S(1)} %get-tuple-element.49), channel_id=1, source_target_pairs={{1,225},{3,227},{5,229},{7,231},{9,233},{11,235},{13,237},{15,239}... | collective-permute-start | bytes 884744 | tf_op jit(solution)/shard_map/ppermute | solution.py:44
  21.4 11.0 %collective-permute-start.4 = (bf16[4,64,256]{2,1,0:T(8,128)(2,1)S(1)}, bf16[4,64,256]{2,1,0:T(8,128)(2,1)S(1)}, u32[]{:S(2)}, u32[]{:S(2)}) collective-permute-start(bf16[4,64,256]{2,1,0:T(8,128)(2,1)S(1)} %get-tuple-element.50), channel_id=1, source_target_pairs={{0,33},{1,32},{2,35},{3,34},{4,37},{5,36},{6,39},{7,38},{8,41},{9,... | collective-permute-start | bytes 393224 | tf_op jit(solution)/shard_map/ppermute | solution.py:44
  23.0 12.3 %collective-permute-start.5 = (bf16[2,32,1024]{2,1,0:T(8,128)(2,1)S(1)}, bf16[2,32,1024]{2,1,0:T(8,128)(2,1)}, u32[]{:S(2)}, u32[]{:S(2)}) collective-permute-start(bf16[2,32,1024]{2,1,0:T(8,128)(2,1)S(1)} %get-tuple-element.51), channel_id=1, source_target_pairs={{0,33},{1,32},{2,35},{3,34},{4,37},{5,36},{6,39},{7,38},{8,41},{9,... | collective-permute-start | bytes 393224 | tf_op jit(solution)/shard_map/ppermute | solution.py:44
  35.4 9.1 %collective-permute-start.3 = (bf16[2,12,6,512]{3,2,1,0:T(8,128)(2,1)S(1)}, bf16[2,12,6,512]{3,2,1,0:T(8,128)(2,1)S(1)}, u32[]{:S(2)}, u32[]{:S(2)}) collective-permute-start(bf16[2,12,6,512]{3,2,1,0:T(8,128)(2,1)S(1)} %edge.1.refs_2_), channel_id=1, source_target_pairs={{0,30},{1,31},{2,0},{3,1},{4,2},{5,3},{6,4},{7,5},{8,6},{9,7},{10,... | collective-permute-start | bytes 442376 | tf_op jit(solution)/shard_map/ppermute | solution.py:44
  37.5 5.0 %collective-permute-start.8 = (bf16[4,64,256]{2,1,0:T(8,128)(2,1)S(1)}, bf16[4,64,256]{2,1,0:T(8,128)(2,1)S(1)}, u32[]{:S(2)}, u32[]{:S(2)}) collective-permute-start(bf16[4,64,256]{2,1,0:T(8,128)(2,1)S(1)} %get-tuple-element.52.refs_1_), channel_id=1, source_target_pairs={{0,192},{1,193},{2,194},{3,195},{4,196},{5,197},{6,198},{7,199},{8... | collective-permute-start | bytes 393224 | tf_op jit(solution)/shard_map/ppermute | solution.py:44
  38.5 5.4 %collective-permute-start.7 = (bf16[4,64,256]{2,1,0:T(8,128)(2,1)S(1)}, bf16[4,64,256]{2,1,0:T(8,128)(2,1)S(1)}, u32[]{:S(2)}, u32[]{:S(2)}) collective-permute-start(bf16[4,64,256]{2,1,0:T(8,128)(2,1)S(1)} %get-tuple-element.52.refs_1_), channel_id=1, source_target_pairs={{0,128},{1,129},{2,130},{3,131},{4,132},{5,133},{6,134},{7,135},{8... | collective-permute-start | bytes 393224 | tf_op jit(solution)/shard_map/ppermute | solution.py:44
  39.6 4.9 %collective-permute-start.6 = (bf16[4,64,256]{2,1,0:T(8,128)(2,1)S(1)}, bf16[4,64,256]{2,1,0:T(8,128)(2,1)S(1)}, u32[]{:S(2)}, u32[]{:S(2)}) collective-permute-start(bf16[4,64,256]{2,1,0:T(8,128)(2,1)S(1)} %get-tuple-element.52.refs_1_), channel_id=1, source_target_pairs={{0,64},{1,65},{2,66},{3,67},{4,68},{5,69},{6,70},{7,71},{8,72},{9,... | collective-permute-start | bytes 393224 | tf_op jit(solution)/shard_map/ppermute | solution.py:44
  45.1 7.3 %collective-permute-start.9 = (bf16[4,256,256]{2,1,0:T(8,128)(2,1)S(1)}, bf16[4,256,256]{2,1,0:T(8,128)(2,1)}, u32[]{:S(2)}, u32[]{:S(2)}) collective-permute-start(bf16[4,256,256]{2,1,0:T(8,128)(2,1)S(1)} %join.1.wqo_m), channel_id=1, source_target_pairs={{0,2},{1,3},{2,0},{3,1},{4,6},{5,7},{6,4},{7,5},{8,10},{9,11},{10,... | collective-permute-start | bytes 1572872 | tf_op jit(solution)/shard_map/ppermute | solution.py:44
  80.6 16.5 %collective-permute-start.14 = (bf16[4,2,8,16,512]{4,3,2,1,0:T(8,128)(2,1)}, bf16[4,2,8,16,512]{4,3,2,1,0:T(8,128)(2,1)S(1)}, u32[]{:S(2)}, u32[]{:S(2)}) collective-permute-start(bf16[4,2,8,16,512]{4,3,2,1,0:T(8,128)(2,1)} %get-tuple-element.64), channel_id=1, source_target_pairs={{0,2},{1,3},{2,0},{3,1},{4,6},{5,7},{6,4},{7,5},{8,10},{9,11},{10,... | collective-permute-start | bytes 3145736 | tf_op jit(solution)/shard_map/ppermute | solution.py:44
  96.9 5.9 %collective-permute-start.10 = (bf16[12,6,512]{2,1,0:T(8,128)(2,1)S(1)}, bf16[12,6,512]{2,1,0:T(8,128)(2,1)S(1)}, u32[]{:S(2)}, u32[]{:S(2)}) collective-permute-start(bf16[12,6,512]{2,1,0:T(8,128)(2,1)S(1)} %get-tuple-element.61), channel_id=1, source_target_pairs={{0,2},{1,3},{2,4},{3,5},{4,6},{5,7},{6,8},{7,9},{8,10},{9,11},{10,... | collective-permute-start | bytes 221192 | tf_op jit(solution)/shard_map/ppermute | solution.py:44
  99.9 22.4 %collective-permute-start.16 = (bf16[2,2,8,16,512]{4,3,2,1,0:T(8,128)(2,1)S(1)}, bf16[2,2,8,16,512]{4,3,2,1,0:T(8,128)(2,1)S(1)}, u32[]{:S(2)}, u32[]{:S(2)}) collective-permute-start(bf16[2,2,8,16,512]{4,3,2,1,0:T(8,128)(2,1)S(1)} %get-tuple-element.68), channel_id=1, source_target_pairs={{0,64},{1,65},{2,66},{3,67},{4,68},{5,69},{6,70},{7,71},{8,72},{9,... | collective-permute-start | bytes 1572872 | tf_op jit(solution)/shard_map/ppermute | solution.py:44
  100.9 21.5 %collective-permute-start.18 = (bf16[2,2,8,16,512]{4,3,2,1,0:T(8,128)(2,1)S(1)}, bf16[2,2,8,16,512]{4,3,2,1,0:T(8,128)(2,1)S(1)}, u32[]{:S(2)}, u32[]{:S(2)}) collective-permute-start(bf16[2,2,8,16,512]{4,3,2,1,0:T(8,128)(2,1)S(1)} %get-tuple-element.70), channel_id=1, source_target_pairs={{0,192},{1,193},{2,194},{3,195},{4,196},{5,197},{6,198},{7,199},{8... | collective-permute-start | bytes 1572872 | tf_op jit(solution)/shard_map/ppermute | solution.py:44
  103.0 12.7 %collective-permute-start.13 = (bf16[3,48,512]{2,1,0:T(8,128)(2,1)S(1)}, bf16[3,48,512]{2,1,0:T(8,128)(2,1)S(1)}, u32[]{:S(2)}, u32[]{:S(2)}) collective-permute-start(bf16[3,48,512]{2,1,0:T(8,128)(2,1)S(1)} %get-tuple-element.89), channel_id=1, source_target_pairs={{1,33},{3,35},{5,37},{7,39},{9,41},{11,43},{13,45},{15,47},{17,49}... | collective-permute-start | bytes 442376 | tf_op jit(solution)/shard_map/ppermute | solution.py:44
  103.7 18.6 %collective-permute-start.11 = (bf16[3,48,512]{2,1,0:T(8,128)(2,1)S(1)}, bf16[3,48,512]{2,1,0:T(8,128)(2,1)S(1)}, u32[]{:S(2)}, u32[]{:S(2)}) collective-permute-start(bf16[3,48,512]{2,1,0:T(8,128)(2,1)S(1)} %get-tuple-element.90), channel_id=1, source_target_pairs={{0,1},{1,32},{2,3},{3,34},{4,5},{5,36},{6,7},{7,38},{8,9},{9,40},{... | collective-permute-start | bytes 442376 | tf_op jit(solution)/shard_map/ppermute | solution.py:44
  107.3 15.0 %collective-permute-start.12 = (bf16[3,48,512]{2,1,0:T(8,128)(2,1)S(1)}, bf16[3,48,512]{2,1,0:T(8,128)(2,1)S(1)}, u32[]{:S(2)}, u32[]{:S(2)}) collective-permute-start(bf16[3,48,512]{2,1,0:T(8,128)(2,1)S(1)} %get-tuple-element.91), channel_id=1, source_target_pairs={{0,1},{1,0},{2,3},{3,2},{4,5},{5,4},{6,7},{7,6},{8,9},{9,8},{10,11... | collective-permute-start | bytes 442376 | tf_op jit(solution)/shard_map/ppermute | solution.py:44
  124.9 3.6 %collective-permute-start.19 = (bf16[4,2,2,8,16,256]{5,4,3,2,1,0:T(8,128)(2,1)S(1)}, bf16[4,2,2,8,16,256]{5,4,3,2,1,0:T(8,128)(2,1)S(1)}, u32[]{:S(2)}, u32[]{:S(2)}) collective-permute-start(bf16[4,2,2,8,16,256]{5,4,3,2,1,0:T(8,128)(2,1)S(1)} %get-tuple-element.80), channel_id=1, source_target_pairs={{0,2},{1,3},{2,0},{3,1},{4,6},{5,7},{6,4},{7,5},{8,10},{9,11},{10,... | collective-permute-start | bytes 3145736 | tf_op jit(solution)/shard_map/ppermute | solution.py:44
  126.3 15.0 %collective-permute-start.17 = (bf16[2,2,8,16,512]{4,3,2,1,0:T(8,128)(2,1)S(1)}, bf16[2,2,8,16,512]{4,3,2,1,0:T(8,128)(2,1)S(1)}, u32[]{:S(2)}, u32[]{:S(2)}) collective-permute-start(bf16[2,2,8,16,512]{4,3,2,1,0:T(8,128)(2,1)S(1)} %get-tuple-element.69), channel_id=1, source_target_pairs={{0,128},{1,129},{2,130},{3,131},{4,132},{5,133},{6,134},{7,135},{8... | collective-permute-start | bytes 1572872 | tf_op jit(solution)/shard_map/ppermute | solution.py:44
  128.8 15.8 %collective-permute-start.20 = (bf16[2,2,8,16,256]{4,3,2,1,0:T(8,128)(2,1)S(1)}, bf16[2,2,8,16,256]{4,3,2,1,0:T(8,128)(2,1)S(1)}, u32[]{:S(2)}, u32[]{:S(2)}) collective-permute-start(bf16[2,2,8,16,256]{4,3,2,1,0:T(8,128)(2,1)S(1)} %get-tuple-element.82), channel_id=1, source_target_pairs={{0,64},{1,65},{2,66},{3,67},{4,68},{5,69},{6,70},{7,71},{8,72},{9,... | collective-permute-start | bytes 786440 | tf_op jit(solution)/shard_map/ppermute | solution.py:44
  128.9 23.6 %collective-permute-start.21 = (bf16[2,2,8,16,256]{4,3,2,1,0:T(8,128)(2,1)S(1)}, bf16[2,2,8,16,256]{4,3,2,1,0:T(8,128)(2,1)S(1)}, u32[]{:S(2)}, u32[]{:S(2)}) collective-permute-start(bf16[2,2,8,16,256]{4,3,2,1,0:T(8,128)(2,1)S(1)} %get-tuple-element.83), channel_id=1, source_target_pairs={{0,128},{1,129},{2,130},{3,131},{4,132},{5,133},{6,134},{7,135},{8... | collective-permute-start | bytes 786440 | tf_op jit(solution)/shard_map/ppermute | solution.py:44
  130.3 22.3 %collective-permute-start.22 = (bf16[2,2,8,16,256]{4,3,2,1,0:T(8,128)(2,1)S(1)}, bf16[2,2,8,16,256]{4,3,2,1,0:T(8,128)(2,1)S(1)}, u32[]{:S(2)}, u32[]{:S(2)}) collective-permute-start(bf16[2,2,8,16,256]{4,3,2,1,0:T(8,128)(2,1)S(1)} %get-tuple-element.84), channel_id=1, source_target_pairs={{0,192},{1,193},{2,194},{3,195},{4,196},{5,197},{6,198},{7,199},{8... | collective-permute-start | bytes 786440 | tf_op jit(solution)/shard_map/ppermute | solution.py:44
  212.1 8.0 %collective-permute-start.23 = (bf16[8,8,16,768]{3,2,1,0:T(8,128)(2,1)S(1)}, bf16[8,8,16,768]{3,2,1,0:T(8,128)(2,1)S(1)}, u32[]{:S(2)}, u32[]{:S(2)}) collective-permute-start(bf16[8,8,16,768]{3,2,1,0:T(8,128)(2,1)S(1)} %all_to_all.17.mine), channel_id=1, source_target_pairs={{0,2},{1,3},{2,0},{3,1},{4,6},{5,7},{6,4},{7,5},{8,10},{9,11},{10,... | collective-permute-start | bytes 4718600 | tf_op jit(solution)/shard_map/ppermute | solution.py:44
  (47 other events, 234.1 us)
Sparse Core Ops, SparseCore 0:
  35.5 41.9 all-gather.2

commit v3 on v2

--- a/solution.py
+++ b/solution.py
@@ -92,25 +92,59 @@
 
 def fence(values, after):
     n = len(values)
-    anywhere = pl.BlockSpec(memory_space=pl.ANY)
+    spec = pl.BlockSpec(memory_space=pltpu.VMEM)
     return pl.pallas_call(
         lambda *refs: None,
         out_shape=tuple(jax.ShapeDtypeStruct(v.shape, v.dtype) for v in values),
-        in_specs=[anywhere] * (n + len(after)),
-        out_specs=tuple([anywhere] * n),
+        in_specs=[spec] * (n + len(after)),
+        out_specs=tuple([spec] * n),
         input_output_aliases={i: i for i in range(n)},
         compiler_params=pltpu.CompilerParams(vmem_limit_bytes=MIB),
         name="fence",
     )(*values, *after)
 
 
-def pieces_kernel(place, tile, cot, near, far, below):
-    t = place[4]
+def cut_kernel(place, tile, cot, wq, wo, w1, w2, near, far, below, attend, mlp, sems):
+    x, c, t = place[0], place[3], place[4]
+    eighth = c * 4 + x
+    copies = []
     for n, ref in enumerate((tile, cot)):
-        for i in range(3):
-            near[n, i] = ref[9 + i - 6 * t]
-            far[n, i] = ref[i + 6 * t]
-            below[n, i] = ref[i]
+        copies.append((ref.at[pl.ds(9 - 6 * t, 3)], near.at[n]))
+        copies.append((ref.at[pl.ds(6 * t, 3)], far.at[n]))
+        copies.append((ref.at[pl.ds(0, 3)], below.at[n]))
+    copies.append((wq.at[:, pl.ds(pl.multiple_of(eighth * 64, 64), 64)], attend.at[pl.ds(0, 3)]))
+    copies.append(
+        (
+            wo.at[pl.ds(pl.multiple_of(x * 64, 64), 64), pl.ds(pl.multiple_of(c * 256, 256), 256)],
+            attend.at[3],
+        )
+    )
+    copies.append(
+        (
+            w1.at[pl.ds(pl.multiple_of(x * 128, 128), 128), pl.ds(pl.multiple_of(c * 512, 512), 512)],
+            mlp.at[0],
+        )
+    )
+    copies.append((w2.at[pl.ds(pl.multiple_of(eighth * 128, 128), 128)], mlp.at[1]))
+    copies = [pltpu.make_async_copy(a, b, sems.at[i]) for i, (a, b) in enumerate(copies)]
+    for copy in copies:
+        copy.start()
+    for copy in copies:
+        copy.wait()
+
+
+def cut_parts(place, *arrays):
+    shapes = [(2, 3, 48, D)] * 3 + [(4, 64, 256), (2, 128, 512)]
+    hbm = pl.BlockSpec(memory_space=pltpu.HBM)
+    return pl.pallas_call(
+        cut_kernel,
+        out_shape=tuple(whole(shape) for shape in shapes),
+        in_specs=[pl.BlockSpec(memory_space=pltpu.SMEM)] + [hbm] * len(arrays),
+        out_specs=tuple([pl.BlockSpec(memory_space=pltpu.VMEM)] * len(shapes)),
+        scratch_shapes=[pltpu.SemaphoreType.DMA((10,))],
+        compiler_params=pltpu.CompilerParams(vmem_limit_bytes=MIB),
+        name="cut",
+    )(place, *arrays)
 
 
 def edge_kernel(place, tile, cot, near, far, below, edge):
@@ -124,40 +158,19 @@
             edge[n, 9 + i] = far[n, i, :6]
 
 
-def weight_parts(place, w_qkv, w_out, w_fc1, w_fc2):
-    def kernel(place, wq, wo, w1, w2, attend, mlp):
-        attend[0:3] = wq[...]
-        attend[3] = wo[...]
-        mlp[0] = w1[...]
-        mlp[1, :, :512] = w2[:32]
-        mlp[1, :, 512:] = w2[32:]
-
-    specs = [
-        ((3, 64, 256), lambda i, p: (0, p[3] * 4 + p[0], 0)),
-        ((64, 256), lambda i, p: (p[0], p[3])),
-        ((32, 1024), lambda i, p: (p[2] * 2 + p[3], 0)),
-        ((64, 512), lambda i, p: (p[2] * 2 + p[3], 0)),
-    ]
-    shapes = ((4, 64, 256), (2, 32, 1024))
-    return pl.pallas_call(
-        kernel,
-        out_shape=tuple(whole(shape) for shape in shapes),
-        grid_spec=pltpu.PrefetchScalarGridSpec(
-            num_scalar_prefetch=1,
-            grid=(1,),
-            in_specs=[pl.BlockSpec(block, index) for block, index in specs],
-            out_specs=tuple(pl.BlockSpec(shape, lambda i, p: (0, 0, 0)) for shape in shapes),
-        ),
-        compiler_params=pltpu.CompilerParams(vmem_limit_bytes=4 * MIB),
-        name="weight_parts",
-    )(place, w_qkv, w_out, w_fc1, w_fc2)
-
-
 def join_kernel(place, *refs):
     out = refs[4]
     rows = refs[0].shape[1]
     for k in range(4):
         out[:, pl.ds(pl.multiple_of((place[0] ^ k) * rows, rows), rows), :] = refs[k][...]
+
+
+def join(place, part, name, after=()):
+    depth, rows, width = part.shape
+    parts = [part] + [flip(part, x=k) for k in (1, 2, 3)]
+    out = whole((depth, 4 * rows, width))
+    (out,) = call(without(join_kernel, 5, len(after)), parts, [out], (), place, name=name, after=after)
+    return out
 
 
 def to_windows(band):
@@ -316,23 +329,22 @@
 
 
 def mlp_other_kernel(
-    place, mixed_ref, n2_ref, n2t, cot_ref, cott, out_acc, norm_acc, g2, gathered,
+    place, mixed_ref, n2_ref, n2t, cot_ref, cott, out_acc, norm_acc, g2, w12_m, w12_s,
     band, tail, dm_ref, keep, away,
-    hid_scr, dpre_scr, stage, wins, w1, w2,
+    hid_scr, dpre_scr, stage, wins,
 ):
     mx, c = place[0], place[3]
     n2, cot = n2_ref[...], cot_ref[...]
-    for p in range(16):
-        w1[32 * p : 32 * p + 32, :] = gathered[p, 0]
-        w2[64 * p : 64 * p + 32, :] = gathered[p, 1, :, :512]
-        w2[64 * p + 32 : 64 * p + 64, :] = gathered[p, 1, :, 512:]
-    for x in range(4):
-        cols = slice(x * 256, x * 256 + 256)
-        hidden, dpre = mlp_block(w1, w2, cols, n2, cot)
-        hid_scr[:, cols] = hidden
-        dpre_scr[:, cols] = dpre
-        store_grads(n2t, cott, hidden, dpre, (x ^ mx,), c, keep, away)
-    d_norm = norm_acc[...] + dot_nt(dpre_scr[...], w1[...])
+    for n, (pair, half) in enumerate(((w12_m, c), (w12_s, 1 - c))):
+        for i in range(2):
+            cols = slice(i * 256, i * 256 + 256)
+            hidden, dpre = mlp_block(pair.at[0], pair.at[1], cols, n2, cot)
+            hid_scr[:, n * 512 + i * 256 : n * 512 + i * 256 + 256] = hidden
+            dpre_scr[:, n * 512 + i * 256 : n * 512 + i * 256 + 256] = dpre
+            store_grads(n2t, cott, hidden, dpre, ((2 * half + i) ^ mx,), c, keep, away)
+    d_norm = norm_acc[...] + (
+        dot_nt(dpre_scr[:, :512], w12_m[0]) + dot_nt(dpre_scr[:, 512:], w12_s[0])
+    )
     gain = g2[...]
     xhat, rstd = norm(mixed_ref[...].astype(F32), gain)[1:]
     scaled = d_norm * gain
@@ -342,7 +354,7 @@
         - xhat * jnp.mean(scaled * xhat, -1, keepdims=True)
     )
     dm_ref[...] = dm.astype(BF)
-    wins[...] = out_acc[...] + dot(hid_scr[...], w2[...])
+    wins[...] = out_acc[...] + (dot(hid_scr[:, :512], w12_m[1]) + dot(hid_scr[:, 512:], w12_s[1]))
     store_windows(wins, stage, band, tail)
 
 
@@ -387,7 +399,7 @@
 
 
 def attend_grads_kernel(
-    place, dqkv, dmt, heads_ref, n1t_ref, first, second, third, fourth, fifth,
+    place, dqkv, dmt, heads_ref, n1t_ref, first, second, third, fourth,
     keep, away,
 ):
     mx, c, mt = place[0], place[3], place[4]
@@ -414,8 +426,8 @@
 
 def call(kernel, args, outs, scratch=(), place=None, flops=0, name=None, after=(), limit=8):
     spec = pl.BlockSpec(memory_space=pltpu.VMEM)
-    specs = [spec] * len(args) + [pl.BlockSpec(memory_space=pl.ANY)] * len(after)
     args = tuple(args) + tuple(after)
+    specs = [spec] * len(args)
     if place is not None:
         args = (place,) + args
         specs = [pl.BlockSpec(memory_space=pltpu.SMEM)] + specs
@@ -528,23 +540,13 @@
     place = jnp.stack([x, yl, z, c, t]).astype(jnp.int32)
     tile, cot = tokens[0], cotangent[0]
 
-    part_attend, part_mlp = weight_parts(place, w_qkv, w_out, w_fc1, w_fc2)
-    wqo = flip(part_attend, yl=1, t=1)
-    pieces = call(pieces_kernel, (tile, cot), [whole((2, 3, 48, D))] * 3, (), place, name="pieces")
-    rows = (flip(pieces[0], t=1), send(pieces[1], far_move), send(pieces[2], lat_move(-1)))
+    near, far, below, wqo, w12 = cut_parts(place, tile, cot, w_qkv, w_out, w_fc1, w_fc2)
+    wqo = flip(wqo, yl=1, t=1)
+    rows = (flip(near, t=1), send(far, far_move), send(below, lat_move(-1)))
     (edge,) = call(edge_kernel, (tile, cot, *rows), [whole((2, 12, 6, D))], (), place, name="edge")
     moved = send(edge, lon_move(-1))
-    wqo, w12 = fence((wqo, flip(part_mlp, yl=1, t=1)), (edge,))
-    w12 = lax.all_gather(w12, ("z", "c"), axis=0)
-    (wqo,) = call(
-        without(join_kernel, 5, 1),
-        [wqo] + [flip(wqo, x=k) for k in (1, 2, 3)],
-        [whole((4, 256, 256))],
-        (),
-        place,
-        name="join",
-        after=(moved,),
-    )
+    wqo, w12 = fence((wqo, flip(w12, yl=1, t=1)), (edge,))
+    wqo = join(place, wqo, "join_attend", (moved,))
     wqo_sib = flip(wqo, c=1)
 
     band = lax.dynamic_slice_in_dim(labels, t * 6, 6, 1)
@@ -580,12 +582,14 @@
         name="mlp_own",
         limit=12,
     )
+    w12 = join(place, w12, "join_mlp", (mixed, keep))
+    w12_sib = flip(w12, c=1)
     arrived = flip(away, c=1)
     out_band, tail, dm, keep_two, away_two = call(
         mlp_other_kernel,
-        (mixed, *carried, second_norm_gain[None], w12),
+        (mixed, *carried, second_norm_gain[None], w12, w12_sib),
         [whole((12, 48, D)), whole((12, 6, D)), whole((TOK, D))] + grads,
-        scratch + [pltpu.VMEM((D, 1024), BF), pltpu.VMEM((1024, D), BF)],
+        scratch,
         place,
         flops=4 * 10**9,
         name="mlp_other",
@@ -612,12 +616,13 @@
         [whole((4, 2, 2, 8, 16, 256))] * 2,
         (),
         place,
-        flops=1 * 10**9,
         name="attend_grads",
         limit=12,
-        after=(fc_parts[1], fc_parts[3], near, far, above),
-    )
-    at_cut = core_phase(*at, ())
+        after=(fc_parts[1], fc_parts[3], near, far),
+    )
+    keep, away = at
+    (away,) = fence((away,), fc_parts[2:3])
+    at_cut = core_phase(keep, away, ())
     at_parts = x_phase(at_cut)
     gq, go, g1, g2 = reduce_and_gather(place, fc_parts, at_parts, (above,))
     out = jnp.where(

time: 231 us -> 216 us (0.935)
  local copies, waits for them, and re-layouts: 30.9 us -> 14.7 us
  between operations: 14.4 us -> 0.96 us
  starting transfers between devices: 40.9 us -> 45.8 us
  waiting for transfers between devices: 45.9 us -> 50.8 us
  blocking collectives: 58.4 us -> 61.9 us
    unnamed x92 -> x32, local copies, waits for them, and re-layouts: 30.3 us -> 8.6 us
    all_to_all x1, blocking collectives: 24.7 us -> 30.2 us  [reduce_and_gather(): parts = lax.all_to_all(total.reshape(32, 16, 768), ('tp', 'yl', 'z'), 0, 0)]
    ppermute x24 -> x28, waiting for transfers between devices: 45.9 us -> 50.8 us  [send(): return lax.ppermute(value, AXES, pairs_of(move))]
    ppermute x24 -> x28, starting transfers between devices: 40.9 us -> 45.8 us  [send(): return lax.ppermute(value, AXES, pairs_of(move))]
  transfers between devices with their start and end apart: 25 -> 28, of which waited for: 13 -> 12; matrix products, arithmetic and copies ran while one was open for 1% -> 4% of each run, Pallas kernels for 13% -> 15%
where the time goes in v3:
time: 216 us
  blocking collectives  61.9 us (29%)
  waiting for transfers between devices  50.8 us (24%)
  starting transfers between devices  45.8 us (21%)
  Pallas kernels  39.5 us (18%)
  local copies, waits for them, and re-layouts  14.7 us (7%)
    ppermute x28, waiting for transfers between devices, send(): return lax.ppermute(value, AXES, pairs_of(move))  50.8 us
    ppermute x28, starting transfers between devices, send(): return lax.ppermute(value, AXES, pairs_of(move))  45.8 us
    pallas_call x14, Pallas kernels, call(): pl.pallas_call(kernel, out_shape=tuple(outs), in_specs=specs, out_specs=t...  37.5 us
    all_to_all x1, blocking collectives, reduce_and_gather(): parts = lax.all_to_all(total.reshape(32, 16, 768), ('tp', 'yl', 'z'), 0, 0)  30.2 us
    all_to_all x1, blocking collectives, reduce_and_gather(): mine = lax.all_to_all(columns, ('x', 'yl'), 0, 0)  18.1 us
    all_to_all x1, blocking collectives, reduce_and_gather(): column = lax.all_to_all(chunks, 'z', 0, 0)  13.7 us
    unnamed x32, local copies, waits for them, and re-layouts  8.6 us
  transfers between devices with their start and end apart: 28, of which 12 were waited for; matrix products, arithmetic and copies ran while one was open for 4% of the time, Pallas kernels for 15%

profile of v3, /device:TPU:1, one launch (start us, length us, event | category | flops | bytes accessed | tf_op | source)
XLA Modules:
  0.0 215.6 jit_solution(17652532834073676784)
XLA Ops:
  9.4 3.8 %collective-permute-start = (bf16[2,3,48,512]{3,2,1,0:T(8,128)(2,1)S(1)}, bf16[2,3,48,512]{3,2,1,0:T(8,128)(2,1)S(1)}, u32[]{:S(2)}, u32[]{:S(2)}) collective-permute-start(bf16[2,3,48,512]{3,2,1,0:T(8,128)(2,1)S(1)} %get-tuple-element.47), channel_id=1, source_target_pairs={{0,1},{1,0},{2,3},{3,2},{4,5},{5,4},{6,7},{7,6},{8,9},{9,8},{10,11... | collective-permute-start | bytes 884744 | tf_op jit(solution)/shard_map/ppermute | solution.py:44
  13.3 3.0 %collective-permute-start.1 = (bf16[2,3,48,512]{3,2,1,0:T(8,128)(2,1)S(1)}, bf16[2,3,48,512]{3,2,1,0:T(8,128)(2,1)S(1)}, u32[]{:S(2)}, u32[]{:S(2)}) collective-permute-start(bf16[2,3,48,512]{3,2,1,0:T(8,128)(2,1)S(1)} %get-tuple-element.48), channel_id=1, source_target_pairs={{0,225},{1,0},{2,227},{3,2},{4,229},{5,4},{6,231},{7,6},{8,233},{9... | collective-permute-start | bytes 884744 | tf_op jit(solution)/shard_map/ppermute | solution.py:44
  19.7 10.8 %collective-permute-done.1.far = bf16[2,3,48,512]{3,2,1,0:T(8,128)(2,1)S(1)} collective-permute-done((bf16[2,3,48,512]{3,2,1,0:T(8,128)(2,1)S(1)}, bf16[2,3,48,512]{3,2,1,0:T(8,128)(2,1)S(1)}, u32[]{:S(2)}, u32[]{:S(2)}) %collective-permute-start.1) | collective-permute-done | bytes 294944 | tf_op jit(solution)/shard_map/ppermute | solution.py:44
  31.1 3.5 %collective-permute-start.3 = (bf16[2,12,6,512]{3,2,1,0:T(8,128)(2,1)S(1)}, bf16[2,12,6,512]{3,2,1,0:T(8,128)(2,1)S(1)}, u32[]{:S(2)}, u32[]{:S(2)}) collective-permute-start(bf16[2,12,6,512]{3,2,1,0:T(8,128)(2,1)S(1)} %edge.1.refs_2_), channel_id=1, source_target_pairs={{0,30},{1,31},{2,0},{3,1},{4,2},{5,3},{6,4},{7,5},{8,6},{9,7},{10,... | collective-permute-start | bytes 442376 | tf_op jit(solution)/shard_map/ppermute | solution.py:44
  34.9 3.2 %collective-permute-start.8 = (bf16[4,64,256]{2,1,0:T(8,128)(2,1)S(1)}, bf16[4,64,256]{2,1,0:T(8,128)(2,1)S(1)}, u32[]{:S(2)}, u32[]{:S(2)}) collective-permute-start(bf16[4,64,256]{2,1,0:T(8,128)(2,1)S(1)} %get-tuple-element.52.refs_1_), channel_id=1, source_target_pairs={{0,192},{1,193},{2,194},{3,195},{4,196},{5,197},{6,198},{7,199},{8... | collective-permute-start | bytes 393224 | tf_op jit(solution)/shard_map/ppermute | solution.py:44
  38.7 2.7 %collective-permute-done.8.refs_4_ = bf16[4,64,256]{2,1,0:T(8,128)(2,1)S(1)} collective-permute-done((bf16[4,64,256]{2,1,0:T(8,128)(2,1)S(1)}, bf16[4,64,256]{2,1,0:T(8,128)(2,1)S(1)}, u32[]{:S(2)}, u32[]{:S(2)}) %collective-permute-start.8) | collective-permute-done | bytes 131104 | tf_op jit(solution)/shard_map/ppermute | solution.py:44
  44.0 5.0 %collective-permute-start.9 = (bf16[4,256,256]{2,1,0:T(8,128)(2,1)S(1)}, bf16[4,256,256]{2,1,0:T(8,128)(2,1)}, u32[]{:S(2)}, u32[]{:S(2)}) collective-permute-start(bf16[4,256,256]{2,1,0:T(8,128)(2,1)S(1)} %join_attend.1.wqo_m), channel_id=1, source_target_pairs={{0,2},{1,3},{2,0},{3,1},{4,6},{5,7},{6,4},{7,5},{8,10},{9,11},{10,... | collective-permute-start | bytes 1572872 | tf_op jit(solution)/shard_map/ppermute | solution.py:44
  60.9 7.4 %attend.1 = (bf16[512,576]{1,0:T(8,128)(2,1)S(1)}, bf16[576,1536]{1,0:T(8,128)(2,1)S(1)}, bf16[32,144,144]{2,1,0:T(8,128)(2,1)S(1)}, bf16[576,512]{1,0:T(8,128)(...) custom-call(s32[5]{0:T(128)S(1)} %stack.23.place.refs_0_, bf16[12,48,512]{2,1,0:T(8,128)(2,1)S(1)} %bitcast.25, ...), custom_call_target="tpu_custom_call" | custom-call | flops 3000000000 | bytes 9424916 | tf_op jit(solution)/shard_map/attend/pallas_call | solution.py:435
  68.4 6.6 %mlp_own.1 = (bf16[576,512]{1,0:T(8,128)(2,1)S(1)}, bf16[512,576]{1,0:T(8,128)(2,1)S(1)}, bf16[576,512]{1,0:T(8,128)(2,1)S(1)}, bf16[512,576]{1,0:T(8,128)(2,1)S...) custom-call(s32[5]{0:T(128)S(1)} %stack.23.place.refs_0_, ...), custom_call_target="tpu_custom_call" | custom-call | flops 4000000000 | bytes 11126804 | tf_op jit(solution)/shard_map/mlp_own/pallas_call | solution.py:435
  78.9 6.4 %mlp_other.1 = (bf16[12,48,512]{2,1,0:T(8,128)(2,1)S(1)}, bf16[12,6,512]{2,1,0:T(8,128)(2,1)S(1)}, bf16[576,512]{1,0:T(8,128)(2,1)S(1)}, bf16[4,2,8,16,512]{4,3,...) custom-call(s32[5]{0:T(128)S(1)} %stack.23.place.refs_0_, bf16[576,512]{1,0:T(8,128)(2,1)S(1)} %get-tuple-element.53.mixed_ref.refs_5_, ...), custom_call_target="tpu_custom_call" | custom-call | flops 4000000000 | bytes 10758164 | tf_op jit(solution)/shard_map/mlp_other/pallas_call | solution.py:435
  85.7 2.2 %collective-permute-done.19.arrived_two = bf16[4,2,8,16,512]{4,3,2,1,0:T(8,128)(2,1)S(1)} collective-permute-done((bf16[4,2,8,16,512]{4,3,2,1,0:T(8,128)(2,1)S(1)}, bf16[4,2,8,16,512]{4,3,2,1,0:T(8,128)(2,1)S(1)}, u32[]{:S(2)}, u32[]{:S(2)}) %collective-permute-start.19) | collective-permute-done | bytes 1048608 | tf_op jit(solution)/shard_map/ppermute | solution.py:44
  94.4 8.0 %attend_back.1 = (bf16[576,1536]{1,0:T(8,128)(2,1)S(1)}, bf16[512,576]{1,0:T(8,128)(2,1)S(1)}) custom-call(bf16[576,512]{1,0:T(8,128)(2,1)S(1)} %get-tuple-element.71.dm_ref, bf16[32,144,144]{2,1,0:T(8,128)(2,1)S(1)} %get-tuple-element.72.prob_ref, bf16[576,1536]{1,0:T(8,128)(2,1)S(1)} %get-tuple-element.73.qkv_ref, ...), custom_call_target="tpu_custom_call" | custom-call | flops 4000000000 | bytes 7168000 | tf_op jit(solution)/shard_map/attend_back/pallas_call | solution.py:435
  102.5 16.0 %collective-permute-done.15.fourth = bf16[3,48,512]{2,1,0:T(8,128)(2,1)S(1)} collective-permute-done((bf16[3,48,512]{2,1,0:T(8,128)(2,1)S(1)}, bf16[3,48,512]{2,1,0:T(8,128)(2,1)S(1)}, u32[]{:S(2)}, u32[]{:S(2)}) %collective-permute-start.15) | collective-permute-done | bytes 147488 | tf_op jit(solution)/shard_map/ppermute | solution.py:44
  118.4 2.6 %attend_grads.1 = (bf16[4,2,2,8,16,256]{5,4,3,2,1,0:T(8,128)(2,1)S(1)}, bf16[4,2,2,8,16,256]{5,4,3,2,1,0:T(8,128)(2,1)S(1)}) custom-call(s32[5]{0:T(128)S(1)} %stack.23.place.refs_0_, bf16[576,1536]{1,0:T(8,128)(2,1)S(1)} %get-tuple-element.75.dqkv, bf16[512,576]{1,0:T(8,128)(2,1)S(1)} %get-tuple-element.76.dmt, ...), custom_call_target="tpu_custom_call" | custom-call | bytes 6979604 | tf_op jit(solution)/shard_map/attend_grads/pallas_call | solution.py:435
  122.6 2.3 %collective-permute-done.23.refs_1_ = bf16[4,2,2,8,16,256]{5,4,3,2,1,0:T(8,128)(2,1)S(1)} collective-permute-done((bf16[4,2,2,8,16,256]{5,4,3,2,1,0:T(8,128)(2,1)S(1)}, bf16[4,2,2,8,16,256]{5,4,3,2,1,0:T(8,128)(2,1)S(1)}, u32[]{:S(2)}, u32[]{:S(2)}) %collective-permute-start.23) | collective-permute-done | bytes 1048608 | tf_op jit(solution)/shard_map/ppermute | solution.py:44
  126.6 2.6 %collective-permute-start.26 = (bf16[2,2,8,16,256]{4,3,2,1,0:T(8,128)(2,1)S(1)}, bf16[2,2,8,16,256]{4,3,2,1,0:T(8,128)(2,1)S(1)}, u32[]{:S(2)}, u32[]{:S(2)}) collective-permute-start(bf16[2,2,8,16,256]{4,3,2,1,0:T(8,128)(2,1)S(1)} %get-tuple-element.84), channel_id=1, source_target_pairs={{0,192},{1,193},{2,194},{3,195},{4,196},{5,197},{6,198},{7,199},{8... | collective-permute-start | bytes 786440 | tf_op jit(solution)/shard_map/ppermute | solution.py:44
  129.8 3.0 %collective-permute-done.24.refs_5_ = bf16[2,2,8,16,256]{4,3,2,1,0:T(8,128)(2,1)S(1)} collective-permute-done((bf16[2,2,8,16,256]{4,3,2,1,0:T(8,128)(2,1)S(1)}, bf16[2,2,8,16,256]{4,3,2,1,0:T(8,128)(2,1)S(1)}, u32[]{:S(2)}, u32[]{:S(2)}) %collective-permute-start.24) | collective-permute-done | bytes 262176 | tf_op jit(solution)/shard_map/ppermute | solution.py:44
  132.8 5.4 %collective-permute-done.25.refs_6_ = bf16[2,2,8,16,256]{4,3,2,1,0:T(8,128)(2,1)S(1)} collective-permute-done((bf16[2,2,8,16,256]{4,3,2,1,0:T(8,128)(2,1)S(1)}, bf16[2,2,8,16,256]{4,3,2,1,0:T(8,128)(2,1)S(1)}, u32[]{:S(2)}, u32[]{:S(2)}) %collective-permute-start.25) | collective-permute-done | bytes 262176 | tf_op jit(solution)/shard_map/ppermute | solution.py:44
  138.2 2.1 collective-permute-done.26.refs_7_
  141.3 30.2 %all_to_all.15.parts = bf16[32,16,768]{2,1,0:T(8,128)(2,1)S(1)} all-to-all(bf16[32,16,768]{2,1,0:T(8,128)(2,1)S(1)} %bitcast.22), channel_id=1, replica_groups=mesh['x'=4,'yl'=2,'z'=8,'c'=2,'tp'=2] {'tp','yl','z'}, dimensions={0} | all-to-all | bytes 1572864 | tf_op jit(solution)/shard_map/all_to_all | solution.py:527
  171.6 13.7 %all_to_all.16.part = bf16[8,16,768]{2,1,0:T(8,128)(2,1)S(1)} all-to-all(bf16[8,16,768]{2,1,0:T(8,128)(2,1)S(1)} %last_sum.1), channel_id=1, replica_groups=mesh['x'=4,'yl'=2,'z'=8,'c'=2,'tp'=2] {'z'}, dimensions={0} | all-to-all | bytes 393216 | tf_op jit(solution)/shard_map/all_to_all | solution.py:529
  185.4 18.1 %all_to_all.17.mine = bf16[8,8,16,768]{3,2,1,0:T(8,128)(2,1)S(1)} all-to-all(bf16[8,8,16,768]{3,2,1,0:T(8,128)(2,1)S(1)} %copies.1), channel_id=1, replica_groups=mesh['x'=4,'yl'=2,'z'=8,'c'=2,'tp'=2] {'x','yl'}, dimensions={0} | all-to-all | bytes 3145728 | tf_op jit(solution)/shard_map/all_to_all | solution.py:531
  203.4 6.3 %collective-permute-start.27 = (bf16[8,8,16,768]{3,2,1,0:T(8,128)(2,1)S(1)}, bf16[8,8,16,768]{3,2,1,0:T(8,128)(2,1)S(1)}, u32[]{:S(2)}, u32[]{:S(2)}) collective-permute-start(bf16[8,8,16,768]{3,2,1,0:T(8,128)(2,1)S(1)} %all_to_all.17.mine), channel_id=1, source_target_pairs={{0,2},{1,3},{2,0},{3,1},{4,6},{5,7},{6,4},{7,5},{8,10},{9,11},{10,... | collective-permute-start | bytes 4718600 | tf_op jit(solution)/shard_map/ppermute | solution.py:44
  212.8 2.8 %place.1 = (bf16[3,512,256]{2,1,0:T(8,128)(2,1)}, bf16[256,512]{1,0:T(8,128)(2,1)}, bf16[512,1024]{1,0:T(8,128)(2,1)}, bf16[1024,512]{1,0:T(8,128)(2,1)}) custom-call(s32[5]{0:T(128)S(1)} %stack.23.place.refs_0_, bf16[8,8,16,768]{3,2,1,0:T(8,128)(2,1)S(1)} %all_to_all.17.mine, bf16[8,8,16,768]{3,2,1,0:T(8,128)(2,1)S(1)} %collective-permute-done.27.sib), custom_call_target="tpu_custom_call" | custom-call | bytes 6291476 | tf_op jit(solution)/shard_map/place/pallas_call | solution.py:435
  (99 shorter events, 47.0 us)
Async XLA Ops:
  9.4 10.2 %collective-permute-start = (bf16[2,3,48,512]{3,2,1,0:T(8,128)(2,1)S(1)}, bf16[2,3,48,512]{3,2,1,0:T(8,128)(2,1)S(1)}, u32[]{:S(2)}, u32[]{:S(2)}) collective-permute-start(bf16[2,3,48,512]{3,2,1,0:T(8,128)(2,1)S(1)} %get-tuple-element.47), channel_id=1, source_target_pairs={{0,1},{1,0},{2,3},{3,2},{4,5},{5,4},{6,7},{7,6},{8,9},{9,8},{10,11... | collective-permute-start | bytes 884744 | tf_op jit(solution)/shard_map/ppermute | solution.py:44
  13.3 17.3 %collective-permute-start.1 = (bf16[2,3,48,512]{3,2,1,0:T(8,128)(2,1)S(1)}, bf16[2,3,48,512]{3,2,1,0:T(8,128)(2,1)S(1)}, u32[]{:S(2)}, u32[]{:S(2)}) collective-permute-start(bf16[2,3,48,512]{3,2,1,0:T(8,128)(2,1)S(1)} %get-tuple-element.48), channel_id=1, source_target_pairs={{0,225},{1,0},{2,227},{3,2},{4,229},{5,4},{6,231},{7,6},{8,233},{9... | collective-permute-start | bytes 884744 | tf_op jit(solution)/shard_map/ppermute | solution.py:44
  16.2 14.3 %collective-permute-start.2 = (bf16[2,3,48,512]{3,2,1,0:T(8,128)(2,1)S(1)}, bf16[2,3,48,512]{3,2,1,0:T(8,128)(2,1)S(1)}, u32[]{:S(2)}, u32[]{:S(2)}) collective-permute-start(bf16[2,3,48,512]{3,2,1,0:T(8,128)(2,1)S(1)} %get-tuple-element.49), channel_id=1, source_target_pairs={{1,225},{3,227},{5,229},{7,231},{9,233},{11,235},{13,237},{15,239}... | collective-permute-start | bytes 884744 | tf_op jit(solution)/shard_map/ppermute | solution.py:44
  16.9 17.9 %collective-permute-start.5 = (bf16[2,128,512]{2,1,0:T(8,128)(2,1)S(1)}, bf16[2,128,512]{2,1,0:T(8,128)(2,1)S(1)}, u32[]{:S(2)}, u32[]{:S(2)}) collective-permute-start(bf16[2,128,512]{2,1,0:T(8,128)(2,1)S(1)} %get-tuple-element.51), channel_id=1, source_target_pairs={{0,33},{1,32},{2,35},{3,34},{4,37},{5,36},{6,39},{7,38},{8,41},{9,... | collective-permute-start | bytes 786440 | tf_op jit(solution)/shard_map/ppermute | solution.py:44
  18.5 16.3 %collective-permute-start.4 = (bf16[4,64,256]{2,1,0:T(8,128)(2,1)S(1)}, bf16[4,64,256]{2,1,0:T(8,128)(2,1)S(1)}, u32[]{:S(2)}, u32[]{:S(2)}) collective-permute-start(bf16[4,64,256]{2,1,0:T(8,128)(2,1)S(1)} %get-tuple-element.50), channel_id=1, source_target_pairs={{0,33},{1,32},{2,35},{3,34},{4,37},{5,36},{6,39},{7,38},{8,41},{9,... | collective-permute-start | bytes 393224 | tf_op jit(solution)/shard_map/ppermute | solution.py:44
  31.1 12.2 %collective-permute-start.3 = (bf16[2,12,6,512]{3,2,1,0:T(8,128)(2,1)S(1)}, bf16[2,12,6,512]{3,2,1,0:T(8,128)(2,1)S(1)}, u32[]{:S(2)}, u32[]{:S(2)}) collective-permute-start(bf16[2,12,6,512]{3,2,1,0:T(8,128)(2,1)S(1)} %edge.1.refs_2_), channel_id=1, source_target_pairs={{0,30},{1,31},{2,0},{3,1},{4,2},{5,3},{6,4},{7,5},{8,6},{9,7},{10,... | collective-permute-start | bytes 442376 | tf_op jit(solution)/shard_map/ppermute | solution.py:44
  34.9 6.5 %collective-permute-start.8 = (bf16[4,64,256]{2,1,0:T(8,128)(2,1)S(1)}, bf16[4,64,256]{2,1,0:T(8,128)(2,1)S(1)}, u32[]{:S(2)}, u32[]{:S(2)}) collective-permute-start(bf16[4,64,256]{2,1,0:T(8,128)(2,1)S(1)} %get-tuple-element.52.refs_1_), channel_id=1, source_target_pairs={{0,192},{1,193},{2,194},{3,195},{4,196},{5,197},{6,198},{7,199},{8... | collective-permute-start | bytes 393224 | tf_op jit(solution)/shard_map/ppermute | solution.py:44
  38.0 5.3 %collective-permute-start.7 = (bf16[4,64,256]{2,1,0:T(8,128)(2,1)S(1)}, bf16[4,64,256]{2,1,0:T(8,128)(2,1)S(1)}, u32[]{:S(2)}, u32[]{:S(2)}) collective-permute-start(bf16[4,64,256]{2,1,0:T(8,128)(2,1)S(1)} %get-tuple-element.52.refs_1_), channel_id=1, source_target_pairs={{0,128},{1,129},{2,130},{3,131},{4,132},{5,133},{6,134},{7,135},{8... | collective-permute-start | bytes 393224 | tf_op jit(solution)/shard_map/ppermute | solution.py:44
  38.5 4.8 %collective-permute-start.6 = (bf16[4,64,256]{2,1,0:T(8,128)(2,1)S(1)}, bf16[4,64,256]{2,1,0:T(8,128)(2,1)S(1)}, u32[]{:S(2)}, u32[]{:S(2)}) collective-permute-start(bf16[4,64,256]{2,1,0:T(8,128)(2,1)S(1)} %get-tuple-element.52.refs_1_), channel_id=1, source_target_pairs={{0,64},{1,65},{2,66},{3,67},{4,68},{5,69},{6,70},{7,71},{8,72},{9,... | collective-permute-start | bytes 393224 | tf_op jit(solution)/shard_map/ppermute | solution.py:44
  44.0 14.8 %collective-permute-start.9 = (bf16[4,256,256]{2,1,0:T(8,128)(2,1)S(1)}, bf16[4,256,256]{2,1,0:T(8,128)(2,1)}, u32[]{:S(2)}, u32[]{:S(2)}) collective-permute-start(bf16[4,256,256]{2,1,0:T(8,128)(2,1)S(1)} %join_attend.1.wqo_m), channel_id=1, source_target_pairs={{0,2},{1,3},{2,0},{3,1},{4,6},{5,7},{6,4},{7,5},{8,10},{9,11},{10,... | collective-permute-start | bytes 1572872 | tf_op jit(solution)/shard_map/ppermute | solution.py:44
  55.5 19.5 %collective-permute-start.12 = (bf16[2,128,512]{2,1,0:T(8,128)(2,1)S(1)}, bf16[2,128,512]{2,1,0:T(8,128)(2,1)S(1)}, u32[]{:S(2)}, u32[]{:S(2)}) collective-permute-start(bf16[2,128,512]{2,1,0:T(8,128)(2,1)S(1)} %get-tuple-element.60.refs_1_), channel_id=1, source_target_pairs={{0,192},{1,193},{2,194},{3,195},{4,196},{5,197},{6,198},{7,199},{8... | collective-permute-start | bytes 786440 | tf_op jit(solution)/shard_map/ppermute | solution.py:44
  57.2 17.7 %collective-permute-start.11 = (bf16[2,128,512]{2,1,0:T(8,128)(2,1)S(1)}, bf16[2,128,512]{2,1,0:T(8,128)(2,1)S(1)}, u32[]{:S(2)}, u32[]{:S(2)}) collective-permute-start(bf16[2,128,512]{2,1,0:T(8,128)(2,1)S(1)} %get-tuple-element.60.refs_1_), channel_id=1, source_target_pairs={{0,128},{1,129},{2,130},{3,131},{4,132},{5,133},{6,134},{7,135},{8... | collective-permute-start | bytes 786440 | tf_op jit(solution)/shard_map/ppermute | solution.py:44
  57.7 17.3 %collective-permute-start.10 = (bf16[2,128,512]{2,1,0:T(8,128)(2,1)S(1)}, bf16[2,128,512]{2,1,0:T(8,128)(2,1)S(1)}, u32[]{:S(2)}, u32[]{:S(2)}) collective-permute-start(bf16[2,128,512]{2,1,0:T(8,128)(2,1)S(1)} %get-tuple-element.60.refs_1_), channel_id=1, source_target_pairs={{0,64},{1,65},{2,66},{3,67},{4,68},{5,69},{6,70},{7,71},{8,72},{9,... | collective-permute-start | bytes 786440 | tf_op jit(solution)/shard_map/ppermute | solution.py:44
  76.6 9.2 %collective-permute-start.18 = (bf16[4,2,8,16,512]{4,3,2,1,0:T(8,128)(2,1)S(1)}, bf16[4,2,8,16,512]{4,3,2,1,0:T(8,128)(2,1)S(1)}, u32[]{:S(2)}, u32[]{:S(2)}) collective-permute-start(bf16[4,2,8,16,512]{4,3,2,1,0:T(8,128)(2,1)S(1)} %get-tuple-element.64), channel_id=1, source_target_pairs={{0,2},{1,3},{2,0},{3,1},{4,6},{5,7},{6,4},{7,5},{8,10},{9,11},{10,... | collective-permute-start | bytes 3145736 | tf_op jit(solution)/shard_map/ppermute | solution.py:44
  85.7 6.3 %collective-permute-start.14 = (bf16[12,6,512]{2,1,0:T(8,128)(2,1)S(1)}, bf16[12,6,512]{2,1,0:T(8,128)(2,1)S(1)}, u32[]{:S(2)}, u32[]{:S(2)}) collective-permute-start(bf16[12,6,512]{2,1,0:T(8,128)(2,1)S(1)} %get-tuple-element.62), channel_id=1, source_target_pairs={{0,2},{1,3},{2,4},{3,5},{4,6},{5,7},{6,8},{7,9},{8,10},{9,11},{10,... | collective-permute-start | bytes 221192 | tf_op jit(solution)/shard_map/ppermute | solution.py:44
  88.5 30.0 %collective-permute-start.20 = (bf16[2,2,8,16,512]{4,3,2,1,0:T(8,128)(2,1)S(1)}, bf16[2,2,8,16,512]{4,3,2,1,0:T(8,128)(2,1)S(1)}, u32[]{:S(2)}, u32[]{:S(2)}) collective-permute-start(bf16[2,2,8,16,512]{4,3,2,1,0:T(8,128)(2,1)S(1)} %get-tuple-element.68), channel_id=1, source_target_pairs={{0,64},{1,65},{2,66},{3,67},{4,68},{5,69},{6,70},{7,71},{8,72},{9,... | collective-permute-start | bytes 1572872 | tf_op jit(solution)/shard_map/ppermute | solution.py:44
  88.9 29.5 %collective-permute-start.22 = (bf16[2,2,8,16,512]{4,3,2,1,0:T(8,128)(2,1)S(1)}, bf16[2,2,8,16,512]{4,3,2,1,0:T(8,128)(2,1)S(1)}, u32[]{:S(2)}, u32[]{:S(2)}) collective-permute-start(bf16[2,2,8,16,512]{4,3,2,1,0:T(8,128)(2,1)S(1)} %get-tuple-element.70), channel_id=1, source_target_pairs={{0,192},{1,193},{2,194},{3,195},{4,196},{5,197},{6,198},{7,199},{8... | collective-permute-start | bytes 1572872 | tf_op jit(solution)/shard_map/ppermute | solution.py:44
  90.7 30.3 %collective-permute-start.21 = (bf16[2,2,8,16,512]{4,3,2,1,0:T(8,128)(2,1)S(1)}, bf16[2,2,8,16,512]{4,3,2,1,0:T(8,128)(2,1)S(1)}, u32[]{:S(2)}, u32[]{:S(2)}) collective-permute-start(bf16[2,2,8,16,512]{4,3,2,1,0:T(8,128)(2,1)S(1)} %get-tuple-element.69), channel_id=1, source_target_pairs={{0,128},{1,129},{2,130},{3,131},{4,132},{5,133},{6,134},{7,135},{8... | collective-permute-start | bytes 1572872 | tf_op jit(solution)/shard_map/ppermute | solution.py:44
  92.1 26.3 %collective-permute-start.15 = (bf16[3,48,512]{2,1,0:T(8,128)(2,1)S(1)}, bf16[3,48,512]{2,1,0:T(8,128)(2,1)S(1)}, u32[]{:S(2)}, u32[]{:S(2)}) collective-permute-start(bf16[3,48,512]{2,1,0:T(8,128)(2,1)S(1)} %get-tuple-element.90), channel_id=1, source_target_pairs={{0,1},{1,32},{2,3},{3,34},{4,5},{5,36},{6,7},{7,38},{8,9},{9,40},{... | collective-permute-start | bytes 442376 | tf_op jit(solution)/shard_map/ppermute | solution.py:44
  94.1 24.3 %collective-permute-start.16 = (bf16[3,48,512]{2,1,0:T(8,128)(2,1)S(1)}, bf16[3,48,512]{2,1,0:T(8,128)(2,1)S(1)}, u32[]{:S(2)}, u32[]{:S(2)}) collective-permute-start(bf16[3,48,512]{2,1,0:T(8,128)(2,1)S(1)} %get-tuple-element.91), channel_id=1, source_target_pairs={{0,1},{1,0},{2,3},{3,2},{4,5},{5,4},{6,7},{7,6},{8,9},{9,8},{10,11... | collective-permute-start | bytes 442376 | tf_op jit(solution)/shard_map/ppermute | solution.py:44
  125.2 7.6 %collective-permute-start.24 = (bf16[2,2,8,16,256]{4,3,2,1,0:T(8,128)(2,1)S(1)}, bf16[2,2,8,16,256]{4,3,2,1,0:T(8,128)(2,1)S(1)}, u32[]{:S(2)}, u32[]{:S(2)}) collective-permute-start(bf16[2,2,8,16,256]{4,3,2,1,0:T(8,128)(2,1)S(1)} %get-tuple-element.82), channel_id=1, source_target_pairs={{0,64},{1,65},{2,66},{3,67},{4,68},{5,69},{6,70},{7,71},{8,72},{9,... | collective-permute-start | bytes 786440 | tf_op jit(solution)/shard_map/ppermute | solution.py:44
  125.3 12.9 %collective-permute-start.25 = (bf16[2,2,8,16,256]{4,3,2,1,0:T(8,128)(2,1)S(1)}, bf16[2,2,8,16,256]{4,3,2,1,0:T(8,128)(2,1)S(1)}, u32[]{:S(2)}, u32[]{:S(2)}) collective-permute-start(bf16[2,2,8,16,256]{4,3,2,1,0:T(8,128)(2,1)S(1)} %get-tuple-element.83), channel_id=1, source_target_pairs={{0,128},{1,129},{2,130},{3,131},{4,132},{5,133},{6,134},{7,135},{8... | collective-permute-start | bytes 786440 | tf_op jit(solution)/shard_map/ppermute | solution.py:44
  126.6 13.8 %collective-permute-start.26 = (bf16[2,2,8,16,256]{4,3,2,1,0:T(8,128)(2,1)S(1)}, bf16[2,2,8,16,256]{4,3,2,1,0:T(8,128)(2,1)S(1)}, u32[]{:S(2)}, u32[]{:S(2)}) collective-permute-start(bf16[2,2,8,16,256]{4,3,2,1,0:T(8,128)(2,1)S(1)} %get-tuple-element.84), channel_id=1, source_target_pairs={{0,192},{1,193},{2,194},{3,195},{4,196},{5,197},{6,198},{7,199},{8... | collective-permute-start | bytes 786440 | tf_op jit(solution)/shard_map/ppermute | solution.py:44
  203.4 9.3 %collective-permute-start.27 = (bf16[8,8,16,768]{3,2,1,0:T(8,128)(2,1)S(1)}, bf16[8,8,16,768]{3,2,1,0:T(8,128)(2,1)S(1)}, u32[]{:S(2)}, u32[]{:S(2)}) collective-permute-start(bf16[8,8,16,768]{3,2,1,0:T(8,128)(2,1)S(1)} %all_to_all.17.mine), channel_id=1, source_target_pairs={{0,2},{1,3},{2,0},{3,1},{4,6},{5,7},{6,4},{7,5},{8,10},{9,11},{10,... | collective-permute-start | bytes 4718600 | tf_op jit(solution)/shard_map/ppermute | solution.py:44
  (20 other events, 156.2 us)

commit v4 on v3

--- a/solution.py
+++ b/solution.py
@@ -104,28 +104,20 @@
     )(*values, *after)
 
 
-def cut_kernel(place, tile, cot, wq, wo, w1, w2, near, far, below, attend, mlp, sems):
-    x, c, t = place[0], place[3], place[4]
-    eighth = c * 4 + x
+def cut_kernel(place, tile, cot, wq, wo, w1, w2, *refs):
+    rows, attend, mlp, sems = refs[0:6], refs[6], refs[7], refs[8]
+    c, t = place[3], place[4]
+    half = pl.ds(pl.multiple_of(c * 256, 256), 256)
+    halves = pl.ds(pl.multiple_of(c * 512, 512), 512)
     copies = []
-    for n, ref in enumerate((tile, cot)):
-        copies.append((ref.at[pl.ds(9 - 6 * t, 3)], near.at[n]))
-        copies.append((ref.at[pl.ds(6 * t, 3)], far.at[n]))
-        copies.append((ref.at[pl.ds(0, 3)], below.at[n]))
-    copies.append((wq.at[:, pl.ds(pl.multiple_of(eighth * 64, 64), 64)], attend.at[pl.ds(0, 3)]))
-    copies.append(
-        (
-            wo.at[pl.ds(pl.multiple_of(x * 64, 64), 64), pl.ds(pl.multiple_of(c * 256, 256), 256)],
-            attend.at[3],
-        )
-    )
-    copies.append(
-        (
-            w1.at[pl.ds(pl.multiple_of(x * 128, 128), 128), pl.ds(pl.multiple_of(c * 512, 512), 512)],
-            mlp.at[0],
-        )
-    )
-    copies.append((w2.at[pl.ds(pl.multiple_of(eighth * 128, 128), 128)], mlp.at[1]))
+    for ref, (near, far, below) in ((tile, rows[:3]), (cot, rows[3:])):
+        copies.append((ref.at[pl.ds(9 - 6 * t, 3)], near))
+        copies.append((ref.at[pl.ds(6 * t, 3)], far))
+        copies.append((ref.at[pl.ds(0, 3)], below))
+    copies.append((wq.at[:, half], attend.at[pl.ds(0, 3)]))
+    copies.append((wo.at[:, half], attend.at[3]))
+    copies.append((w1.at[:, halves], mlp.at[0]))
+    copies.append((w2.at[halves], mlp.at[1]))
     copies = [pltpu.make_async_copy(a, b, sems.at[i]) for i, (a, b) in enumerate(copies)]
     for copy in copies:
         copy.start()
@@ -134,7 +126,7 @@
 
 
 def cut_parts(place, *arrays):
-    shapes = [(2, 3, 48, D)] * 3 + [(4, 64, 256), (2, 128, 512)]
+    shapes = [(3, 48, D)] * 6 + [(4, 256, 256), (2, 512, 512)]
     hbm = pl.BlockSpec(memory_space=pltpu.HBM)
     return pl.pallas_call(
         cut_kernel,
@@ -142,35 +134,29 @@
         in_specs=[pl.BlockSpec(memory_space=pltpu.SMEM)] + [hbm] * len(arrays),
         out_specs=tuple([pl.BlockSpec(memory_space=pltpu.VMEM)] * len(shapes)),
         scratch_shapes=[pltpu.SemaphoreType.DMA((10,))],
-        compiler_params=pltpu.CompilerParams(vmem_limit_bytes=MIB),
+        compiler_params=pltpu.CompilerParams(vmem_limit_bytes=52 * MIB),
         name="cut",
     )(place, *arrays)
 
 
-def edge_kernel(place, tile, cot, near, far, below, edge):
+def exchange_rows(near, far, below):
+    return flip(near, t=1), send(far, far_move), send(below, lat_move(-1))
+
+
+def edge_kernel(place, tile, near, far, below, edge):
     t = place[4]
-    for n, ref in enumerate((tile, cot)):
-        for i in range(3):
-            edge[n, i] = ref[3 + i + 6 * t, :6]
-            row = jnp.where(t == 0, ref[6 + i, :6].astype(F32), below[n, i, :6].astype(F32))
-            edge[n, 3 + i] = row.astype(BF)
-            edge[n, 6 + i] = near[n, i, :6]
-            edge[n, 9 + i] = far[n, i, :6]
-
-
-def join_kernel(place, *refs):
-    out = refs[4]
-    rows = refs[0].shape[1]
-    for k in range(4):
-        out[:, pl.ds(pl.multiple_of((place[0] ^ k) * rows, rows), rows), :] = refs[k][...]
-
-
-def join(place, part, name, after=()):
-    depth, rows, width = part.shape
-    parts = [part] + [flip(part, x=k) for k in (1, 2, 3)]
-    out = whole((depth, 4 * rows, width))
-    (out,) = call(without(join_kernel, 5, len(after)), parts, [out], (), place, name=name, after=after)
-    return out
+    for i in range(3):
+        edge[i] = tile[3 + i + 6 * t, :6]
+        row = jnp.where(t == 0, tile[6 + i, :6].astype(F32), below[i, :6].astype(F32))
+        edge[3 + i] = row.astype(BF)
+        edge[6 + i] = near[i, :6]
+        edge[9 + i] = far[i, :6]
+
+
+def first_columns(place, tile, rows, name, after=()):
+    kernel = without(edge_kernel, 5, len(after))
+    (edge,) = call(kernel, (tile, *rows), [whole((12, 6, D))], (), place, name=name, after=after)
+    return edge
 
 
 def to_windows(band):
@@ -178,18 +164,18 @@
     return band.reshape(12, WINS, WLON, width).transpose(1, 0, 2, 3).reshape(TOK, width)
 
 
-def load_windows(t, n, tile, near, far, below, moved, stage, wins):
+def load_windows(t, tile, near, far, below, moved, stage, wins):
     for row in range(12):
         if row < 3:
             value = tile[3 + row + 6 * t].astype(F32)
         elif row < 6:
-            value = jnp.where(t == 0, tile[3 + row].astype(F32), below[n, row - 3].astype(F32))
+            value = jnp.where(t == 0, tile[3 + row].astype(F32), below[row - 3].astype(F32))
         elif row < 9:
-            value = near[n, row - 6].astype(F32)
+            value = near[row - 6].astype(F32)
         else:
-            value = far[n, row - 9].astype(F32)
+            value = far[row - 9].astype(F32)
         stage[row, 0:48] = value
-        stage[row, 48:54] = moved[n, row].astype(F32)
+        stage[row, 48:54] = moved[row].astype(F32)
         for w in range(WINS):
             start = w * SEATS + row * WLON
             wins[start : start + WLON, :] = stage[row, 6 + 12 * w : 18 + 12 * w]
@@ -235,7 +221,7 @@
     c = place[3]
     mine = pl.ds(pl.multiple_of(c * 256, 256), 256)
     sibs = pl.ds(pl.multiple_of((1 - c) * 256, 256), 256)
-    load_windows(place[4], 0, tile, near, far, below, moved, stage, wins)
+    load_windows(place[4], tile, near, far, below, moved, stage, wins)
     x = wins[...]
     normed = norm(x, g1[...])[0]
     n1_scr[...] = normed.astype(BF)
@@ -310,7 +296,7 @@
     hid_scr, dpre_scr, stage, wins,
 ):
     mx, c = place[0], place[3]
-    load_windows(place[4], 1, tile, near, far, below, moved, stage, wins)
+    load_windows(place[4], tile, near, far, below, moved, stage, wins)
     mixed = mixed_ref[...].astype(F32)
     normed = norm(mixed, g2[...])[0]
     n2_ref[...] = normed.astype(BF)
@@ -399,7 +385,7 @@
 
 
 def attend_grads_kernel(
-    place, dqkv, dmt, heads_ref, n1t_ref, first, second, third, fourth,
+    place, dqkv, dmt, heads_ref, n1t_ref, first, second,
     keep, away,
 ):
     mx, c, mt = place[0], place[3], place[4]
@@ -520,12 +506,10 @@
     return [cut[0]] + [flip(cut[k], x=k) for k in (1, 2, 3)]
 
 
-def reduce_and_gather(place, fc, at, after):
-    (total,) = call(
-        x_sum_kernel, (*fc, *at), [whole((2, 2, 8, 16, 768))], (), place, name="x_sum", after=after
-    )
+def reduce_and_gather(place, total, after):
     parts = lax.all_to_all(total.reshape(32, 16, 768), ("tp", "yl", "z"), 0, 0)
-    (chunks,) = call(last_sum_kernel, (parts,), [whole((8, 16, 768))], name="last_sum")
+    kernel = without(last_sum_kernel, 1, len(after))
+    (chunks,) = call(kernel, (parts,), [whole((8, 16, 768))], name="last_sum", after=after)
     column = lax.all_to_all(chunks, "z", 0, 0)
     (columns,) = call(copies_kernel, (column,), [whole((8, 8, 16, 768))], name="copies")
     mine = lax.all_to_all(columns, ("x", "yl"), 0, 0)
@@ -540,14 +524,9 @@
     place = jnp.stack([x, yl, z, c, t]).astype(jnp.int32)
     tile, cot = tokens[0], cotangent[0]
 
-    near, far, below, wqo, w12 = cut_parts(place, tile, cot, w_qkv, w_out, w_fc1, w_fc2)
+    *pieces, wqo, w12 = cut_parts(place, tile, cot, w_qkv, w_out, w_fc1, w_fc2)
     wqo = flip(wqo, yl=1, t=1)
-    rows = (flip(near, t=1), send(far, far_move), send(below, lat_move(-1)))
-    (edge,) = call(edge_kernel, (tile, cot, *rows), [whole((2, 12, 6, D))], (), place, name="edge")
-    moved = send(edge, lon_move(-1))
-    wqo, w12 = fence((wqo, flip(w12, yl=1, t=1)), (edge,))
-    wqo = join(place, wqo, "join_attend", (moved,))
-    wqo_sib = flip(wqo, c=1)
+    rows = exchange_rows(*pieces[:3])
 
     band = lax.dynamic_slice_in_dim(labels, t * 6, 6, 1)
     band = jnp.where(t == 0, band, band[::-1]).reshape(12, 48, 1)
@@ -555,9 +534,18 @@
     labc = jnp.broadcast_to(lab[:, None], (TOK, 128))
     labr = jnp.broadcast_to(lab.reshape(WINS, 1, SEATS), (WINS, 8, SEATS))
 
+    edge = first_columns(place, tile, rows, "edge", (labc, labr))
+    moved = send(edge, lon_move(-1))
+    cot_rows = exchange_rows(*fence(pieces[3:], (edge,)))
+    wqo_sib = flip(wqo, c=1)
+    cot_edge = first_columns(place, cot, cot_rows, "cot_edge", (moved, wqo))
+    (w12,) = fence((w12,), (cot_edge,))
+    w12 = flip(w12, yl=1, t=1)
+    cot_moved = send(cot_edge, lon_move(-1))
+
     stage = [pltpu.VMEM((12, 56, D), F32), pltpu.VMEM((TOK, D), F32)]
     n1t, qkv, prob, heads, wo_full, mixed = call(
-        attend_kernel,
+        without(attend_kernel, 13, 1),
         (tile, *rows, moved, labc, labr, gain_one[None], w_qkv, w_out, wqo, wqo_sib),
         [
             whole((D, TOK)), whole((TOK, 3 * D)), whole((WINS * 8, SEATS, SEATS)),
@@ -568,13 +556,14 @@
         flops=3 * 10**9,
         name="attend",
         limit=12,
+        after=(cot_edge,),
     )
     grads = [whole((4, 2, 8, 16, 512))] * 2
     scratch = [pltpu.VMEM((TOK, 1024), BF), pltpu.VMEM((TOK, 1024), BF)] + stage
     tokens_like = [whole((TOK, D)), whole((D, TOK))] * 2 + [whole((TOK, D), F32)] * 2
     *carried, keep, away = call(
         mlp_own_kernel,
-        (mixed, cot, *rows, moved, second_norm_gain[None], w_fc1, w_fc2),
+        (mixed, cot, *cot_rows, cot_moved, second_norm_gain[None], w_fc1, w_fc2),
         tokens_like + grads,
         scratch,
         place,
@@ -582,7 +571,7 @@
         name="mlp_own",
         limit=12,
     )
-    w12 = join(place, w12, "join_mlp", (mixed, keep))
+    (w12,) = fence((w12,), (keep,))
     w12_sib = flip(w12, c=1)
     arrived = flip(away, c=1)
     out_band, tail, dm, keep_two, away_two = call(
@@ -599,7 +588,6 @@
     fc_parts = x_phase(fc_cut)
     out_moved = send(tail, lon_move(1))
     out = jnp.concatenate([out_moved, out_band[:, 6:]], 1)
-    near, far, above = flip(out[6:9], t=1), send(out[9:12], far_back), send(out[3:6], lat_move(1))
     dqkv, dmt = call(
         attend_back_kernel,
         (dm, prob, qkv, wo_full),
@@ -618,13 +606,18 @@
         place,
         name="attend_grads",
         limit=12,
-        after=(fc_parts[1], fc_parts[3], near, far),
+        after=(fc_parts[1], fc_parts[3]),
     )
     keep, away = at
     (away,) = fence((away,), fc_parts[2:3])
     at_cut = core_phase(keep, away, ())
     at_parts = x_phase(at_cut)
-    gq, go, g1, g2 = reduce_and_gather(place, fc_parts, at_parts, (above,))
+    (total,) = call(
+        x_sum_kernel, (*fc_parts, *at_parts), [whole((2, 2, 8, 16, 768))], (), place, name="x_sum"
+    )
+    near, far, above = fence((out[6:9], out[9:12], out[3:6]), (total,))
+    near, far, above = flip(near, t=1), send(far, far_back), send(above, lat_move(1))
+    gq, go, g1, g2 = reduce_and_gather(place, total, (near, far, above))
     out = jnp.where(
         t == 0,
         jnp.concatenate([far, out[0:6], near], 0),

time: 216 us -> 205 us (0.949)
  blocking collectives: 61.9 us -> 33.3 us
  starting transfers between devices: 45.8 us -> 69 us
  local copies, waits for them, and re-layouts: 14.7 us -> 1.68 us
  waiting for transfers between devices: 50.8 us -> 56.4 us
    all_to_all x1 -> x0, blocking collectives: 30.2 us -> none  [reduce_and_gather(): parts = lax.all_to_all(total.reshape(32, 16, 768), ('tp', 'yl', 'z'), 0, 0)]
    ppermute x28 -> x26, starting transfers between devices: 45.8 us -> 58 us  [send(): return lax.ppermute(value, AXES, pairs_of(move))]
    all_to_all x0 -> x1, starting transfers between devices: none -> 11 us  [reduce_and_gather(): parts = lax.all_to_all(total.reshape(32, 16, 768), ('tp', 'yl', 'z'), 0, 0)]
    unnamed x32 -> x22, local copies, waits for them, and re-layouts: 8.6 us -> 1 us
    ppermute x28 -> x26, waiting for transfers between devices: 50.8 us -> 54 us  [send(): return lax.ppermute(value, AXES, pairs_of(move))]
    all_to_all x0 -> x1, waiting for transfers between devices: none -> 2.39 us  [reduce_and_gather(): parts = lax.all_to_all(total.reshape(32, 16, 768), ('tp', 'yl', 'z'), 0, 0)]
    pallas_call x14 -> x13, Pallas kernels: 37.5 us -> 37.1 us  [call(): pl.pallas_call(kernel, out_shape=tuple(outs), in_specs=specs, out_specs=t...]
  transfers between devices with their start and end apart: 28 -> 27, of which waited for: 12 -> 16; matrix products, arithmetic and copies ran while one was open for 4% -> 1% of each run, Pallas kernels for 15% -> 16%
where the time goes in v4:
time: 205 us; the launch traced here: 204 us
  starting transfers between devices  69 us (34%)
  waiting for transfers between devices  56.4 us (28%)
  Pallas kernels  41.6 us (20%)
  blocking collectives  33.3 us (16%)
    ppermute x26, starting transfers between devices, send(): return lax.ppermute(value, AXES, pairs_of(move))  58 us
    ppermute x26, waiting for transfers between devices, send(): return lax.ppermute(value, AXES, pairs_of(move))  54 us
    pallas_call x13, Pallas kernels, call(): pl.pallas_call(kernel, out_shape=tuple(outs), in_specs=specs, out_specs=t...  37.1 us
    all_to_all x1, blocking collectives, reduce_and_gather(): mine = lax.all_to_all(columns, ('x', 'yl'), 0, 0)  18.9 us
    all_to_all x1, blocking collectives, reduce_and_gather(): column = lax.all_to_all(chunks, 'z', 0, 0)  14.3 us
    all_to_all x1, starting transfers between devices, reduce_and_gather(): parts = lax.all_to_all(total.reshape(32, 16, 768), ('tp', 'yl', 'z'), 0, 0)  11 us
  transfers between devices with their start and end apart: 27, of which 16 were waited for; matrix products, arithmetic and copies ran while one was open for 1% of the time, Pallas kernels for 16%

profile of v4, /device:TPU:1, one launch (start us, length us, event | category | flops | bytes accessed | tf_op | source)
XLA Modules:
  0.0 204.2 jit_solution(16383153594072733671)
XLA Ops:
  1.7 3.4 %cut.1 = (bf16[3,48,512]{2,1,0:T(8,128)(2,1)}, bf16[3,48,512]{2,1,0:T(8,128)(2,1)S(1)}, bf16[3,48,512]{2,1,0:T(8,128)(2,1)S(1)}, bf16[3,48,512]{2,1,0:T(8,128)(2...) custom-call(s32[5]{0:T(128)S(1)} %stack.23.place.refs_0_, ...), custom_call_target="tpu_custom_call" | custom-call | tf_op jit(solution)/shard_map/cut/pallas_call | solution.py:131
  5.1 3.7 %collective-permute-start.4 = (bf16[4,256,256]{2,1,0:T(8,128)(2,1)S(1)}, bf16[4,256,256]{2,1,0:T(8,128)(2,1)S(1)}, u32[]{:S(2)}, u32[]{:S(2)}) collective-permute-start(bf16[4,256,256]{2,1,0:T(8,128)(2,1)S(1)} %get-tuple-element.57), channel_id=1, source_target_pairs={{0,33},{1,32},{2,35},{3,34},{4,37},{5,36},{6,39},{7,38},{8,41},{9,... | collective-permute-start | bytes 1572872 | tf_op jit(solution)/shard_map/ppermute | solution.py:44
  9.1 4.1 %collective-permute-start.1 = (bf16[3,48,512]{2,1,0:T(8,128)(2,1)S(1)}, bf16[3,48,512]{2,1,0:T(8,128)(2,1)S(1)}, u32[]{:S(2)}, u32[]{:S(2)}) collective-permute-start(bf16[3,48,512]{2,1,0:T(8,128)(2,1)S(1)} %get-tuple-element.55), channel_id=1, source_target_pairs={{0,225},{1,0},{2,227},{3,2},{4,229},{5,4},{6,231},{7,6},{8,233},{9... | collective-permute-start | bytes 442376 | tf_op jit(solution)/shard_map/ppermute | solution.py:44
  14.9 4.8 %collective-permute-done.1.refs_3_ = bf16[3,48,512]{2,1,0:T(8,128)(2,1)S(1)} collective-permute-done((bf16[3,48,512]{2,1,0:T(8,128)(2,1)S(1)}, bf16[3,48,512]{2,1,0:T(8,128)(2,1)S(1)}, u32[]{:S(2)}, u32[]{:S(2)}) %collective-permute-start.1) | collective-permute-done | bytes 147488 | tf_op jit(solution)/shard_map/ppermute | solution.py:44
  20.4 8.4 %collective-permute-start.6 = (bf16[3,48,512]{2,1,0:T(8,128)(2,1)S(1)}, bf16[3,48,512]{2,1,0:T(8,128)(2,1)S(1)}, u32[]{:S(2)}, u32[]{:S(2)}) collective-permute-start(bf16[3,48,512]{2,1,0:T(8,128)(2,1)S(1)} %get-tuple-element.61), channel_id=1, source_target_pairs={{0,1},{1,0},{2,3},{3,2},{4,5},{5,4},{6,7},{7,6},{8,9},{9,8},{10,11... | collective-permute-start | bytes 442376 | tf_op jit(solution)/shard_map/ppermute | solution.py:44
  33.9 4.3 %collective-permute-done.3.refs_5_ = bf16[12,6,512]{2,1,0:T(8,128)(2,1)S(1)} collective-permute-done((bf16[12,6,512]{2,1,0:T(8,128)(2,1)S(1)}, bf16[12,6,512]{2,1,0:T(8,128)(2,1)S(1)}, u32[]{:S(2)}, u32[]{:S(2)}) %collective-permute-start.3) | collective-permute-done | bytes 73760 | tf_op jit(solution)/shard_map/ppermute | solution.py:44
  41.5 4.4 %collective-permute-start.9 = (bf16[12,6,512]{2,1,0:T(8,128)(2,1)S(1)}, bf16[12,6,512]{2,1,0:T(8,128)(2,1)S(1)}, u32[]{:S(2)}, u32[]{:S(2)}) collective-permute-start(bf16[12,6,512]{2,1,0:T(8,128)(2,1)S(1)} %cot_edge.1.refs_13_.refs_1_), channel_id=1, source_target_pairs={{0,30},{1,31},{2,0},{3,1},{4,2},{5,3},{6,4},{7,5},{8,6},{9,7},{10,... | collective-permute-start | bytes 221192 | tf_op jit(solution)/shard_map/ppermute | solution.py:44
  46.0 6.8 %attend.1 = (bf16[512,576]{1,0:T(8,128)(2,1)S(1)}, bf16[576,1536]{1,0:T(8,128)(2,1)S(1)}, bf16[32,144,144]{2,1,0:T(8,128)(2,1)S(1)}, bf16[576,512]{1,0:T(8,128)(...) custom-call(s32[5]{0:T(128)S(1)} %stack.23.place.refs_0_, bf16[12,48,512]{2,1,0:T(8,128)(2,1)S(1)} %bitcast.24, ...), custom_call_target="tpu_custom_call" | custom-call | flops 3000000000 | bytes 8982548 | tf_op jit(solution)/shard_map/attend/pallas_call | solution.py:421
  52.8 6.6 %mlp_own.1 = (bf16[576,512]{1,0:T(8,128)(2,1)S(1)}, bf16[512,576]{1,0:T(8,128)(2,1)S(1)}, bf16[576,512]{1,0:T(8,128)(2,1)S(1)}, bf16[512,576]{1,0:T(8,128)(2,1)S...) custom-call(s32[5]{0:T(128)S(1)} %stack.23.place.refs_0_, ...), custom_call_target="tpu_custom_call" | custom-call | flops 4000000000 | bytes 10610708 | tf_op jit(solution)/shard_map/mlp_own/pallas_call | solution.py:421
  61.1 4.8 %collective-permute-start.11 = (bf16[2,512,512]{2,1,0:T(8,128)(2,1)S(1)}, bf16[2,512,512]{2,1,0:T(8,128)(2,1)S(1)}, u32[]{:S(2)}, u32[]{:S(2)}) collective-permute-start(bf16[2,512,512]{2,1,0:T(8,128)(2,1)S(1)} %fence.7.w12_m), channel_id=1, source_target_pairs={{0,2},{1,3},{2,0},{3,1},{4,6},{5,7},{6,4},{7,5},{8,10},{9,11},{10,... | collective-permute-start | bytes 3145736 | tf_op jit(solution)/shard_map/ppermute | solution.py:44
  68.2 6.4 %mlp_other.1 = (bf16[12,48,512]{2,1,0:T(8,128)(2,1)S(1)}, bf16[12,6,512]{2,1,0:T(8,128)(2,1)S(1)}, bf16[576,512]{1,0:T(8,128)(2,1)S(1)}, bf16[4,2,8,16,512]{4,3,...) custom-call(s32[5]{0:T(128)S(1)} %stack.23.place.refs_0_, bf16[576,512]{1,0:T(8,128)(2,1)S(1)} %get-tuple-element.64.mixed_ref, ...), custom_call_target="tpu_custom_call" | custom-call | flops 4000000000 | bytes 10758164 | tf_op jit(solution)/shard_map/mlp_other/pallas_call | solution.py:421
  85.6 8.0 %attend_back.1 = (bf16[576,1536]{1,0:T(8,128)(2,1)S(1)}, bf16[512,576]{1,0:T(8,128)(2,1)S(1)}) custom-call(bf16[576,512]{1,0:T(8,128)(2,1)S(1)} %get-tuple-element.82.dm_ref, bf16[32,144,144]{2,1,0:T(8,128)(2,1)S(1)} %get-tuple-element.83.prob_ref, bf16[576,1536]{1,0:T(8,128)(2,1)S(1)} %get-tuple-element.84.qkv_ref, ...), custom_call_target="tpu_custom_call" | custom-call | flops 4000000000 | bytes 7168000 | tf_op jit(solution)/shard_map/attend_back/pallas_call | solution.py:421
  96.2 8.1 %collective-permute-done.16.refs_1_.refs_2_ = bf16[2,2,8,16,512]{4,3,2,1,0:T(8,128)(2,1)S(1)} collective-permute-done((bf16[2,2,8,16,512]{4,3,2,1,0:T(8,128)(2,1)S(1)}, bf16[2,2,8,16,512]{4,3,2,1,0:T(8,128)(2,1)S(1)}, u32[]{:S(2)}, u32[]{:S(2)}) %collective-permute-start.16) | collective-permute-done | bytes 524320 | tf_op jit(solution)/shard_map/ppermute | solution.py:44
  104.3 4.1 %collective-permute-start.18 = (bf16[4,2,2,8,16,256]{5,4,3,2,1,0:T(8,128)(2,1)S(1)}, bf16[4,2,2,8,16,256]{5,4,3,2,1,0:T(8,128)(2,1)S(1)}, u32[]{:S(2)}, u32[]{:S(2)}) collective-permute-start(bf16[4,2,2,8,16,256]{5,4,3,2,1,0:T(8,128)(2,1)S(1)} %fence.8), channel_id=1, source_target_pairs={{0,2},{1,3},{2,0},{3,1},{4,6},{5,7},{6,4},{7,5},{8,10},{9,11},{10,... | collective-permute-start | bytes 3145736 | tf_op jit(solution)/shard_map/ppermute | solution.py:44
  111.3 3.0 %collective-permute-start.20 = (bf16[2,2,8,16,256]{4,3,2,1,0:T(8,128)(2,1)S(1)}, bf16[2,2,8,16,256]{4,3,2,1,0:T(8,128)(2,1)S(1)}, u32[]{:S(2)}, u32[]{:S(2)}) collective-permute-start(bf16[2,2,8,16,256]{4,3,2,1,0:T(8,128)(2,1)S(1)} %get-tuple-element.94), channel_id=1, source_target_pairs={{0,128},{1,129},{2,130},{3,131},{4,132},{5,133},{6,134},{7,135},{8... | collective-permute-start | bytes 786440 | tf_op jit(solution)/shard_map/ppermute | solution.py:44
  115.1 3.7 %collective-permute-done.19.refs_5_ = bf16[2,2,8,16,256]{4,3,2,1,0:T(8,128)(2,1)S(1)} collective-permute-done((bf16[2,2,8,16,256]{4,3,2,1,0:T(8,128)(2,1)S(1)}, bf16[2,2,8,16,256]{4,3,2,1,0:T(8,128)(2,1)S(1)}, u32[]{:S(2)}, u32[]{:S(2)}) %collective-permute-start.19) | collective-permute-done | bytes 262176 | tf_op jit(solution)/shard_map/ppermute | solution.py:44
  118.8 7.2 %collective-permute-done.20.refs_6_ = bf16[2,2,8,16,256]{4,3,2,1,0:T(8,128)(2,1)S(1)} collective-permute-done((bf16[2,2,8,16,256]{4,3,2,1,0:T(8,128)(2,1)S(1)}, bf16[2,2,8,16,256]{4,3,2,1,0:T(8,128)(2,1)S(1)}, u32[]{:S(2)}, u32[]{:S(2)}) %collective-permute-start.20) | collective-permute-done | bytes 262176 | tf_op jit(solution)/shard_map/ppermute | solution.py:44
  129.7 11.0 %all-to-all-start = ((bf16[32,16,768]{2,1,0:T(8,128)(2,1)}), bf16[32,16,768]{2,1,0:T(8,128)(2,1)S(1)}, u32[]{:S(2)}, u32[]{:S(2)}) async-start(bf16[32,16,768]{2,1,0:T(8,128)(2,1)} %bitcast.15), calls=%async_computation | async-start | bytes 1572864 | tf_op jit(solution)/shard_map/all_to_all | solution.py:510
  145.9 4.8 %collective-permute-done.22.refs_2_ = bf16[3,48,512]{2,1,0:T(8,128)(2,1)S(1)} collective-permute-done((bf16[3,48,512]{2,1,0:T(8,128)(2,1)S(1)}, bf16[3,48,512]{2,1,0:T(8,128)(2,1)S(1)}, u32[]{:S(2)}, u32[]{:S(2)}) %collective-permute-start.22) | collective-permute-done | bytes 147488 | tf_op jit(solution)/shard_map/ppermute | solution.py:44
  150.6 6.4 %collective-permute-done.23.refs_1_ = bf16[3,48,512]{2,1,0:T(8,128)(2,1)S(1)} collective-permute-done((bf16[3,48,512]{2,1,0:T(8,128)(2,1)S(1)}, bf16[3,48,512]{2,1,0:T(8,128)(2,1)S(1)}, u32[]{:S(2)}, u32[]{:S(2)}) %collective-permute-start.23) | collective-permute-done | bytes 147488 | tf_op jit(solution)/shard_map/ppermute | solution.py:44
  159.5 14.3 %all_to_all.15.part = bf16[8,16,768]{2,1,0:T(8,128)(2,1)S(1)} all-to-all(bf16[8,16,768]{2,1,0:T(8,128)(2,1)S(1)} %last_sum.1), channel_id=1, replica_groups=mesh['x'=4,'yl'=2,'z'=8,'c'=2,'tp'=2] {'z'}, dimensions={0} | all-to-all | bytes 393216 | tf_op jit(solution)/shard_map/all_to_all | solution.py:513
  173.9 18.9 %all_to_all.16.mine = bf16[8,8,16,768]{3,2,1,0:T(8,128)(2,1)S(1)} all-to-all(bf16[8,8,16,768]{3,2,1,0:T(8,128)(2,1)S(1)} %copies.1), channel_id=1, replica_groups=mesh['x'=4,'yl'=2,'z'=8,'c'=2,'tp'=2] {'x','yl'}, dimensions={0} | all-to-all | bytes 3145728 | tf_op jit(solution)/shard_map/all_to_all | solution.py:515
  192.9 5.4 %collective-permute-start.25 = (bf16[8,8,16,768]{3,2,1,0:T(8,128)(2,1)S(1)}, bf16[8,8,16,768]{3,2,1,0:T(8,128)(2,1)S(1)}, u32[]{:S(2)}, u32[]{:S(2)}) collective-permute-start(bf16[8,8,16,768]{3,2,1,0:T(8,128)(2,1)S(1)} %all_to_all.16.mine), channel_id=1, source_target_pairs={{0,2},{1,3},{2,0},{3,1},{4,6},{5,7},{6,4},{7,5},{8,10},{9,11},{10,... | collective-permute-start | bytes 4718600 | tf_op jit(solution)/shard_map/ppermute | solution.py:44
  201.3 2.8 %place.1 = (bf16[3,512,256]{2,1,0:T(8,128)(2,1)}, bf16[256,512]{1,0:T(8,128)(2,1)}, bf16[512,1024]{1,0:T(8,128)(2,1)}, bf16[1024,512]{1,0:T(8,128)(2,1)}) custom-call(s32[5]{0:T(128)S(1)} %stack.23.place.refs_0_, bf16[8,8,16,768]{3,2,1,0:T(8,128)(2,1)S(1)} %all_to_all.16.mine, bf16[8,8,16,768]{3,2,1,0:T(8,128)(2,1)S(1)} %collective-permute-done.25.sib), custom_call_target="tpu_custom_call" | custom-call | bytes 6291476 | tf_op jit(solution)/shard_map/place/pallas_call | solution.py:421
  (88 shorter events, 47.9 us)
Async XLA Ops:
  5.1 26.6 %collective-permute-start.4 = (bf16[4,256,256]{2,1,0:T(8,128)(2,1)S(1)}, bf16[4,256,256]{2,1,0:T(8,128)(2,1)S(1)}, u32[]{:S(2)}, u32[]{:S(2)}) collective-permute-start(bf16[4,256,256]{2,1,0:T(8,128)(2,1)S(1)} %get-tuple-element.57), channel_id=1, source_target_pairs={{0,33},{1,32},{2,35},{3,34},{4,37},{5,36},{6,39},{7,38},{8,41},{9,... | collective-permute-start | bytes 1572872 | tf_op jit(solution)/shard_map/ppermute | solution.py:44
  8.7 6.2 %collective-permute-start = (bf16[3,48,512]{2,1,0:T(8,128)(2,1)}, bf16[3,48,512]{2,1,0:T(8,128)(2,1)S(1)}, u32[]{:S(2)}, u32[]{:S(2)}) collective-permute-start(bf16[3,48,512]{2,1,0:T(8,128)(2,1)} %get-tuple-element.54), channel_id=1, source_target_pairs={{0,1},{1,0},{2,3},{3,2},{4,5},{5,4},{6,7},{7,6},{8,9},{9,8},{10,11... | collective-permute-start | bytes 442376 | tf_op jit(solution)/shard_map/ppermute | solution.py:44
  9.1 10.6 %collective-permute-start.1 = (bf16[3,48,512]{2,1,0:T(8,128)(2,1)S(1)}, bf16[3,48,512]{2,1,0:T(8,128)(2,1)S(1)}, u32[]{:S(2)}, u32[]{:S(2)}) collective-permute-start(bf16[3,48,512]{2,1,0:T(8,128)(2,1)S(1)} %get-tuple-element.55), channel_id=1, source_target_pairs={{0,225},{1,0},{2,227},{3,2},{4,229},{5,4},{6,231},{7,6},{8,233},{9... | collective-permute-start | bytes 442376 | tf_op jit(solution)/shard_map/ppermute | solution.py:44
  13.2 6.5 %collective-permute-start.2 = (bf16[3,48,512]{2,1,0:T(8,128)(2,1)S(1)}, bf16[3,48,512]{2,1,0:T(8,128)(2,1)S(1)}, u32[]{:S(2)}, u32[]{:S(2)}) collective-permute-start(bf16[3,48,512]{2,1,0:T(8,128)(2,1)S(1)} %get-tuple-element.56), channel_id=1, source_target_pairs={{1,225},{3,227},{5,229},{7,231},{9,233},{11,235},{13,237},{15,239}... | collective-permute-start | bytes 442376 | tf_op jit(solution)/shard_map/ppermute | solution.py:44
  20.4 17.8 %collective-permute-start.6 = (bf16[3,48,512]{2,1,0:T(8,128)(2,1)S(1)}, bf16[3,48,512]{2,1,0:T(8,128)(2,1)S(1)}, u32[]{:S(2)}, u32[]{:S(2)}) collective-permute-start(bf16[3,48,512]{2,1,0:T(8,128)(2,1)S(1)} %get-tuple-element.61), channel_id=1, source_target_pairs={{0,1},{1,0},{2,3},{3,2},{4,5},{5,4},{6,7},{7,6},{8,9},{9,8},{10,11... | collective-permute-start | bytes 442376 | tf_op jit(solution)/shard_map/ppermute | solution.py:44
  28.8 9.4 %collective-permute-start.7 = (bf16[3,48,512]{2,1,0:T(8,128)(2,1)S(1)}, bf16[3,48,512]{2,1,0:T(8,128)(2,1)S(1)}, u32[]{:S(2)}, u32[]{:S(2)}) collective-permute-start(bf16[3,48,512]{2,1,0:T(8,128)(2,1)S(1)} %get-tuple-element.62), channel_id=1, source_target_pairs={{0,225},{1,0},{2,227},{3,2},{4,229},{5,4},{6,231},{7,6},{8,233},{9... | collective-permute-start | bytes 442376 | tf_op jit(solution)/shard_map/ppermute | solution.py:44
  30.9 7.3 %collective-permute-start.8 = (bf16[3,48,512]{2,1,0:T(8,128)(2,1)S(1)}, bf16[3,48,512]{2,1,0:T(8,128)(2,1)S(1)}, u32[]{:S(2)}, u32[]{:S(2)}) collective-permute-start(bf16[3,48,512]{2,1,0:T(8,128)(2,1)S(1)} %get-tuple-element.63), channel_id=1, source_target_pairs={{1,225},{3,227},{5,229},{7,231},{9,233},{11,235},{13,237},{15,239}... | collective-permute-start | bytes 442376 | tf_op jit(solution)/shard_map/ppermute | solution.py:44
  31.7 14.2 %collective-permute-start.5 = (bf16[4,256,256]{2,1,0:T(8,128)(2,1)S(1)}, bf16[4,256,256]{2,1,0:T(8,128)(2,1)S(1)}, u32[]{:S(2)}, u32[]{:S(2)}) collective-permute-start(bf16[4,256,256]{2,1,0:T(8,128)(2,1)S(1)} %collective-permute-done.4.refs_6_.refs_11_), channel_id=1, source_target_pairs={{0,2},{1,3},{2,0},{3,1},{4,6},{5,7},{6,4},{7,5},{8,10},{9,11},{10,... | collective-permute-start | bytes 1572872 | tf_op jit(solution)/shard_map/ppermute | solution.py:44
  38.8 22.3 %collective-permute-start.10 = (bf16[2,512,512]{2,1,0:T(8,128)(2,1)S(1)}, bf16[2,512,512]{2,1,0:T(8,128)(2,1)S(1)}, u32[]{:S(2)}, u32[]{:S(2)}) collective-permute-start(bf16[2,512,512]{2,1,0:T(8,128)(2,1)S(1)} %fence.6), channel_id=1, source_target_pairs={{0,33},{1,32},{2,35},{3,34},{4,37},{5,36},{6,39},{7,38},{8,41},{9,... | collective-permute-start | bytes 3145736 | tf_op jit(solution)/shard_map/ppermute | solution.py:44
  41.5 11.3 %collective-permute-start.9 = (bf16[12,6,512]{2,1,0:T(8,128)(2,1)S(1)}, bf16[12,6,512]{2,1,0:T(8,128)(2,1)S(1)}, u32[]{:S(2)}, u32[]{:S(2)}) collective-permute-start(bf16[12,6,512]{2,1,0:T(8,128)(2,1)S(1)} %cot_edge.1.refs_13_.refs_1_), channel_id=1, source_target_pairs={{0,30},{1,31},{2,0},{3,1},{4,2},{5,3},{6,4},{7,5},{8,6},{9,7},{10,... | collective-permute-start | bytes 221192 | tf_op jit(solution)/shard_map/ppermute | solution.py:44
  61.1 7.1 %collective-permute-start.11 = (bf16[2,512,512]{2,1,0:T(8,128)(2,1)S(1)}, bf16[2,512,512]{2,1,0:T(8,128)(2,1)S(1)}, u32[]{:S(2)}, u32[]{:S(2)}) collective-permute-start(bf16[2,512,512]{2,1,0:T(8,128)(2,1)S(1)} %fence.7.w12_m), channel_id=1, source_target_pairs={{0,2},{1,3},{2,0},{3,1},{4,6},{5,7},{6,4},{7,5},{8,10},{9,11},{10,... | collective-permute-start | bytes 3145736 | tf_op jit(solution)/shard_map/ppermute | solution.py:44
  65.9 9.2 %collective-permute-start.13 = (bf16[4,2,8,16,512]{4,3,2,1,0:T(8,128)(2,1)S(1)}, bf16[4,2,8,16,512]{4,3,2,1,0:T(8,128)(2,1)S(1)}, u32[]{:S(2)}, u32[]{:S(2)}) collective-permute-start(bf16[4,2,8,16,512]{4,3,2,1,0:T(8,128)(2,1)S(1)} %get-tuple-element.75), channel_id=1, source_target_pairs={{0,2},{1,3},{2,0},{3,1},{4,6},{5,7},{6,4},{7,5},{8,10},{9,11},{10,... | collective-permute-start | bytes 3145736 | tf_op jit(solution)/shard_map/ppermute | solution.py:44
  77.8 15.8 %collective-permute-start.15 = (bf16[2,2,8,16,512]{4,3,2,1,0:T(8,128)(2,1)S(1)}, bf16[2,2,8,16,512]{4,3,2,1,0:T(8,128)(2,1)S(1)}, u32[]{:S(2)}, u32[]{:S(2)}) collective-permute-start(bf16[2,2,8,16,512]{4,3,2,1,0:T(8,128)(2,1)S(1)} %get-tuple-element.79), channel_id=1, source_target_pairs={{0,64},{1,65},{2,66},{3,67},{4,68},{5,69},{6,70},{7,71},{8,72},{9,... | collective-permute-start | bytes 1572872 | tf_op jit(solution)/shard_map/ppermute | solution.py:44
  78.9 14.7 %collective-permute-start.17 = (bf16[2,2,8,16,512]{4,3,2,1,0:T(8,128)(2,1)S(1)}, bf16[2,2,8,16,512]{4,3,2,1,0:T(8,128)(2,1)S(1)}, u32[]{:S(2)}, u32[]{:S(2)}) collective-permute-start(bf16[2,2,8,16,512]{4,3,2,1,0:T(8,128)(2,1)S(1)} %get-tuple-element.81), channel_id=1, source_target_pairs={{0,192},{1,193},{2,194},{3,195},{4,196},{5,197},{6,198},{7,199},{8... | collective-permute-start | bytes 1572872 | tf_op jit(solution)/shard_map/ppermute | solution.py:44
  80.7 23.6 %collective-permute-start.16 = (bf16[2,2,8,16,512]{4,3,2,1,0:T(8,128)(2,1)S(1)}, bf16[2,2,8,16,512]{4,3,2,1,0:T(8,128)(2,1)S(1)}, u32[]{:S(2)}, u32[]{:S(2)}) collective-permute-start(bf16[2,2,8,16,512]{4,3,2,1,0:T(8,128)(2,1)S(1)} %get-tuple-element.80), channel_id=1, source_target_pairs={{0,128},{1,129},{2,130},{3,131},{4,132},{5,133},{6,134},{7,135},{8... | collective-permute-start | bytes 1572872 | tf_op jit(solution)/shard_map/ppermute | solution.py:44
  104.3 6.4 %collective-permute-start.18 = (bf16[4,2,2,8,16,256]{5,4,3,2,1,0:T(8,128)(2,1)S(1)}, bf16[4,2,2,8,16,256]{5,4,3,2,1,0:T(8,128)(2,1)S(1)}, u32[]{:S(2)}, u32[]{:S(2)}) collective-permute-start(bf16[4,2,2,8,16,256]{5,4,3,2,1,0:T(8,128)(2,1)S(1)} %fence.8), channel_id=1, source_target_pairs={{0,2},{1,3},{2,0},{3,1},{4,6},{5,7},{6,4},{7,5},{8,10},{9,11},{10,... | collective-permute-start | bytes 3145736 | tf_op jit(solution)/shard_map/ppermute | solution.py:44
  110.9 7.9 %collective-permute-start.19 = (bf16[2,2,8,16,256]{4,3,2,1,0:T(8,128)(2,1)S(1)}, bf16[2,2,8,16,256]{4,3,2,1,0:T(8,128)(2,1)S(1)}, u32[]{:S(2)}, u32[]{:S(2)}) collective-permute-start(bf16[2,2,8,16,256]{4,3,2,1,0:T(8,128)(2,1)S(1)} %get-tuple-element.93), channel_id=1, source_target_pairs={{0,64},{1,65},{2,66},{3,67},{4,68},{5,69},{6,70},{7,71},{8,72},{9,... | collective-permute-start | bytes 786440 | tf_op jit(solution)/shard_map/ppermute | solution.py:44
  111.3 14.7 %collective-permute-start.20 = (bf16[2,2,8,16,256]{4,3,2,1,0:T(8,128)(2,1)S(1)}, bf16[2,2,8,16,256]{4,3,2,1,0:T(8,128)(2,1)S(1)}, u32[]{:S(2)}, u32[]{:S(2)}) collective-permute-start(bf16[2,2,8,16,256]{4,3,2,1,0:T(8,128)(2,1)S(1)} %get-tuple-element.94), channel_id=1, source_target_pairs={{0,128},{1,129},{2,130},{3,131},{4,132},{5,133},{6,134},{7,135},{8... | collective-permute-start | bytes 786440 | tf_op jit(solution)/shard_map/ppermute | solution.py:44
  114.2 13.7 %collective-permute-start.21 = (bf16[2,2,8,16,256]{4,3,2,1,0:T(8,128)(2,1)S(1)}, bf16[2,2,8,16,256]{4,3,2,1,0:T(8,128)(2,1)S(1)}, u32[]{:S(2)}, u32[]{:S(2)}) collective-permute-start(bf16[2,2,8,16,256]{4,3,2,1,0:T(8,128)(2,1)S(1)} %get-tuple-element.95), channel_id=1, source_target_pairs={{0,192},{1,193},{2,194},{3,195},{4,196},{5,197},{6,198},{7,199},{8... | collective-permute-start | bytes 786440 | tf_op jit(solution)/shard_map/ppermute | solution.py:44
  129.7 29.7 %all-to-all-start = ((bf16[32,16,768]{2,1,0:T(8,128)(2,1)}), bf16[32,16,768]{2,1,0:T(8,128)(2,1)S(1)}, u32[]{:S(2)}, u32[]{:S(2)}) async-start(bf16[32,16,768]{2,1,0:T(8,128)(2,1)} %bitcast.15), calls=%async_computation | async-start | bytes 1572864 | tf_op jit(solution)/shard_map/all_to_all | solution.py:510
  142.2 8.4 %collective-permute-start.22 = (bf16[3,48,512]{2,1,0:T(8,128)(2,1)S(1)}, bf16[3,48,512]{2,1,0:T(8,128)(2,1)S(1)}, u32[]{:S(2)}, u32[]{:S(2)}) collective-permute-start(bf16[3,48,512]{2,1,0:T(8,128)(2,1)S(1)} %get-tuple-element.96), channel_id=1, source_target_pairs={{0,1},{1,32},{2,3},{3,34},{4,5},{5,36},{6,7},{7,38},{8,9},{9,40},{... | collective-permute-start | bytes 442376 | tf_op jit(solution)/shard_map/ppermute | solution.py:44
  144.9 12.1 %collective-permute-start.23 = (bf16[3,48,512]{2,1,0:T(8,128)(2,1)S(1)}, bf16[3,48,512]{2,1,0:T(8,128)(2,1)S(1)}, u32[]{:S(2)}, u32[]{:S(2)}) collective-permute-start(bf16[3,48,512]{2,1,0:T(8,128)(2,1)S(1)} %get-tuple-element.97), channel_id=1, source_target_pairs={{0,1},{1,0},{2,3},{3,2},{4,5},{5,4},{6,7},{7,6},{8,9},{9,8},{10,11... | collective-permute-start | bytes 442376 | tf_op jit(solution)/shard_map/ppermute | solution.py:44
  145.2 11.8 %collective-permute-start.24 = (bf16[3,48,512]{2,1,0:T(8,128)(2,1)S(1)}, bf16[3,48,512]{2,1,0:T(8,128)(2,1)S(1)}, u32[]{:S(2)}, u32[]{:S(2)}) collective-permute-start(bf16[3,48,512]{2,1,0:T(8,128)(2,1)S(1)} %get-tuple-element.98), channel_id=1, source_target_pairs={{1,33},{3,35},{5,37},{7,39},{9,41},{11,43},{13,45},{15,47},{17,49}... | collective-permute-start | bytes 442376 | tf_op jit(solution)/shard_map/ppermute | solution.py:44
  192.9 8.5 %collective-permute-start.25 = (bf16[8,8,16,768]{3,2,1,0:T(8,128)(2,1)S(1)}, bf16[8,8,16,768]{3,2,1,0:T(8,128)(2,1)S(1)}, u32[]{:S(2)}, u32[]{:S(2)}) collective-permute-start(bf16[8,8,16,768]{3,2,1,0:T(8,128)(2,1)S(1)} %all_to_all.16.mine), channel_id=1, source_target_pairs={{0,2},{1,3},{2,0},{3,1},{4,6},{5,7},{6,4},{7,5},{8,10},{9,11},{10,... | collective-permute-start | bytes 4718600 | tf_op jit(solution)/shard_map/ppermute | solution.py:44
  (14 other events, 160.5 us)

commit v5 on v4

--- a/solution.py
+++ b/solution.py
@@ -99,7 +99,7 @@
         in_specs=[spec] * (n + len(after)),
         out_specs=tuple([spec] * n),
         input_output_aliases={i: i for i in range(n)},
-        compiler_params=pltpu.CompilerParams(vmem_limit_bytes=MIB),
+        compiler_params=pltpu.CompilerParams(vmem_limit_bytes=8 * MIB),
         name="fence",
     )(*values, *after)
 
@@ -116,8 +116,9 @@
         copies.append((ref.at[pl.ds(0, 3)], below))
     copies.append((wq.at[:, half], attend.at[pl.ds(0, 3)]))
     copies.append((wo.at[:, half], attend.at[3]))
-    copies.append((w1.at[:, halves], mlp.at[0]))
-    copies.append((w2.at[halves], mlp.at[1]))
+    x = place[0]
+    copies.append((w1.at[pl.ds(pl.multiple_of(x * 128, 128), 128), halves], mlp.at[0]))
+    copies.append((w2.at[pl.ds(pl.multiple_of((c * 4 + x) * 128, 128), 128)], mlp.at[1]))
     copies = [pltpu.make_async_copy(a, b, sems.at[i]) for i, (a, b) in enumerate(copies)]
     for copy in copies:
         copy.start()
@@ -126,7 +127,7 @@
 
 
 def cut_parts(place, *arrays):
-    shapes = [(3, 48, D)] * 6 + [(4, 256, 256), (2, 512, 512)]
+    shapes = [(3, 48, D)] * 6 + [(4, 256, 256), (2, 128, 512)]
     hbm = pl.BlockSpec(memory_space=pltpu.HBM)
     return pl.pallas_call(
         cut_kernel,
@@ -151,6 +152,21 @@
         edge[3 + i] = row.astype(BF)
         edge[6 + i] = near[i, :6]
         edge[9 + i] = far[i, :6]
+
+
+def join_kernel(place, *refs):
+    out = refs[4]
+    rows = refs[0].shape[1]
+    for k in range(4):
+        out[:, pl.ds(pl.multiple_of((place[0] ^ k) * rows, rows), rows), :] = refs[k][...]
+
+
+def join(place, part, name, after=()):
+    depth, rows, width = part.shape
+    parts = [part] + [flip(part, x=k) for k in (1, 2, 3)]
+    out = whole((depth, 4 * rows, width))
+    (out,) = call(without(join_kernel, 5, len(after)), parts, [out], (), place, name=name, after=after)
+    return out
 
 
 def first_columns(place, tile, rows, name, after=()):
@@ -270,11 +286,11 @@
     return v * half, slope
 
 
-def store_rows(out, block, lead, cols):
+def store_rows(out, block, lead, cols, my=0):
     for yl in range(2):
         for z in range(8):
             rows = slice(z * 32 + yl * 16, z * 32 + yl * 16 + 16)
-            out[lead + (yl, z, slice(None), cols)] = block[rows].astype(BF)
+            out[lead + (yl ^ my, z, slice(None), cols)] = block[rows].astype(BF)
 
 
 def mlp_block(w1, w2, cols, n2, cot):
@@ -282,12 +298,13 @@
     return hidden.astype(BF), (dot_nt(cot, w2[cols, :]) * slope).astype(BF)
 
 
-def store_grads(n2t, cott, hidden, dpre, lead, c, keep, away):
+def store_grads(place, n2t, cott, hidden, dpre, x, keep, away):
+    c, my, lead = place[3], place[1], (x ^ place[0],)
     mine = pl.ds(pl.multiple_of(c * 256, 256), 256)
     sibs = pl.ds(pl.multiple_of((1 - c) * 256, 256), 256)
     for rows, out in ((sibs, away), (mine, keep)):
-        store_rows(out, dot(n2t[rows, :], dpre), lead, slice(0, 256))
-        store_rows(out, dot(cott[rows, :], hidden), lead, slice(256, 512))
+        store_rows(out, dot(n2t[rows, :], dpre), lead, slice(0, 256), my)
+        store_rows(out, dot(cott[rows, :], hidden), lead, slice(256, 512), my)
 
 
 def mlp_own_kernel(
@@ -295,7 +312,6 @@
     n2_ref, n2t, cot_ref, cott, out_acc, norm_acc, keep, away,
     hid_scr, dpre_scr, stage, wins,
 ):
-    mx, c = place[0], place[3]
     load_windows(place[4], tile, near, far, below, moved, stage, wins)
     mixed = mixed_ref[...].astype(F32)
     normed = norm(mixed, g2[...])[0]
@@ -309,7 +325,7 @@
         hidden, dpre = mlp_block(w1_own, w2_own, cols, n2, cot)
         hid_scr[:, cols] = hidden
         dpre_scr[:, cols] = dpre
-        store_grads(n2t, cott, hidden, dpre, (x ^ mx,), c, keep, away)
+        store_grads(place, n2t, cott, hidden, dpre, x, keep, away)
     out_acc[...] = mixed + dot(hid_scr[...], w2_own[...])
     norm_acc[...] = dot_nt(dpre_scr[...], w1_own[...])
 
@@ -319,7 +335,7 @@
     band, tail, dm_ref, keep, away,
     hid_scr, dpre_scr, stage, wins,
 ):
-    mx, c = place[0], place[3]
+    c = place[3]
     n2, cot = n2_ref[...], cot_ref[...]
     for n, (pair, half) in enumerate(((w12_m, c), (w12_s, 1 - c))):
         for i in range(2):
@@ -327,7 +343,7 @@
             hidden, dpre = mlp_block(pair.at[0], pair.at[1], cols, n2, cot)
             hid_scr[:, n * 512 + i * 256 : n * 512 + i * 256 + 256] = hidden
             dpre_scr[:, n * 512 + i * 256 : n * 512 + i * 256 + 256] = dpre
-            store_grads(n2t, cott, hidden, dpre, ((2 * half + i) ^ mx,), c, keep, away)
+            store_grads(place, n2t, cott, hidden, dpre, 2 * half + i, keep, away)
     d_norm = norm_acc[...] + (
         dot_nt(dpre_scr[:, :512], w12_m[0]) + dot_nt(dpre_scr[:, 512:], w12_s[0])
     )
@@ -345,7 +361,7 @@
 
 
 def attend_back_kernel(
-    dm_ref, prob_ref, qkv_ref, wo_full, first, second,
+    dm_ref, prob_ref, qkv_ref, wo_full, first,
     dqkv, dmt,
     dheads,
 ):
@@ -385,10 +401,10 @@
 
 
 def attend_grads_kernel(
-    place, dqkv, dmt, heads_ref, n1t_ref, first, second,
+    place, dqkv, dmt, heads_ref, n1t_ref, first, second, third,
     keep, away,
 ):
-    mx, c, mt = place[0], place[3], place[4]
+    c, mt = place[3], place[4]
     mine = pl.ds(pl.multiple_of(c * 256, 256), 256)
     sibs = pl.ds(pl.multiple_of((1 - c) * 256, 256), 256)
     for rows, out in ((sibs, away), (mine, keep)):
@@ -401,7 +417,7 @@
                     else:
                         grad = dot(dmt[rows, :], heads_ref[:, t * 256 : t * 256 + 256])
                     for sub in range(2):
-                        lead = ((half * 2 + sub) ^ mx, t ^ mt)
+                        lead = (half * 2 + sub, t ^ mt)
                         cols = slice(which * 128, which * 128 + 128)
                         store_rows(out, grad[:, sub * 128 : sub * 128 + 128], lead, cols)
 
@@ -437,28 +453,44 @@
     return total.astype(BF)
 
 
-def core_sum_kernel(keep, arrived, *outs):
-    for x in range(4):
-        outs[x][...] = add(keep[x], arrived[x])
+def core_sum_kernel(keep, arrived, out):
+    out[...] = add(keep[...], arrived[...])
 
 
 def core_sum_two_kernel(keep, arrived, keep_two, arrived_two, *outs):
-    for x in range(4):
-        outs[x][0] = add(keep[x], arrived[x])
-        outs[x][1] = add(keep_two[x], arrived_two[x])
-
-
-def x_sum_kernel(place, *refs):
-    fc, at, out = refs[0:4], refs[4:8], refs[-1]
-    t = place[4]
-    out[t, :, :, :, :512] = add(*[r[0] for r in fc])
-    out[1 - t, :, :, :, :512] = add(*[r[1] for r in fc])
-    out[:, :, :, :, 512:] = add(*[r[...] for r in at])
+    for refs, near, far, kept, sent in (
+        ((keep, arrived), 1, 3, outs[0], outs[1]),
+        ((keep_two, arrived_two), 3, 1, outs[2], outs[3]),
+    ):
+        for out, order in ((kept, (0, far)), (sent, (near, 2))):
+            for i, x in enumerate(order):
+                out[i] = add(*[r[x] for r in refs])
+
+
+def half_sum_kernel(kept, arrived, kept_two, arrived_two, *outs):
+    for i in range(2):
+        outs[i][...] = add(kept[i], arrived[i])
+        outs[2 + i][...] = add(kept_two[i], arrived_two[i])
+
+
+def x_sum_kernel(own, arrived, other, arrived_two, *outs):
+    for yl in range(2):
+        outs[yl][...] = add(own[yl], arrived[yl])
+        outs[2 + yl][...] = add(other[yl], arrived_two[yl])
+
+
+def xy_sum_kernel(*refs):
+    fc, at, out = refs[0:4], refs[4], refs[5]
+    out[:, :, :512] = add(*[r[...] for r in fc])
+    total = at[0].astype(F32)
+    for i in range(1, 16):
+        total = total + at[i].astype(F32)
+    out[:, :, 512:] = total.astype(BF)
 
 
 def last_sum_kernel(parts, out):
     total = parts[0].astype(F32)
-    for i in range(1, 32):
+    for i in range(1, 8):
         total = total + parts[i].astype(F32)
     for z in range(8):
         out[z] = total.astype(BF)
@@ -491,28 +523,25 @@
     go[...] = scro[...].astype(F32).T.astype(BF)
 
 
-def core_phase(keep, away, after):
-    outs = [whole(keep.shape[1:])] * 4
-    kernel = without(core_sum_kernel, 2, len(after))
-    return call(kernel, (keep, flip(away, c=1)), outs, name="core_sum", after=after)
-
-
 def core_phase_two(keep, arrived, keep_two, arrived_two):
     outs = [whole((2,) + keep.shape[1:])] * 4
     return call(core_sum_two_kernel, (keep, arrived, keep_two, arrived_two), outs, name="core_sum_two")
 
 
-def x_phase(cut):
-    return [cut[0]] + [flip(cut[k], x=k) for k in (1, 2, 3)]
-
-
-def reduce_and_gather(place, total, after):
-    parts = lax.all_to_all(total.reshape(32, 16, 768), ("tp", "yl", "z"), 0, 0)
-    kernel = without(last_sum_kernel, 1, len(after))
-    (chunks,) = call(kernel, (parts,), [whole((8, 16, 768))], name="last_sum", after=after)
+def y_phase(cut):
+    return [cut[0]] + [flip(cut[k], t=k // 2, yl=k % 2) for k in (1, 2, 3)]
+
+
+def reduce_over_z(total):
+    parts = lax.all_to_all(total, "z", 0, 0)
+    (chunks,) = call(last_sum_kernel, (parts,), [whole((8, 16, 768))], name="last_sum")
     column = lax.all_to_all(chunks, "z", 0, 0)
     (columns,) = call(copies_kernel, (column,), [whole((8, 8, 16, 768))], name="copies")
-    mine = lax.all_to_all(columns, ("x", "yl"), 0, 0)
+    return columns
+
+
+def gather_grads(place, columns, after):
+    (mine,) = fence((lax.all_to_all(columns, ("x", "yl"), 0, 0),), after)
     sib = flip(mine, c=1)
     outs = [whole((3, 512, 256)), whole((256, 512)), whole((512, 1024)), whole((1024, 512))]
     scratch = [pltpu.VMEM((512, 1024), BF), pltpu.VMEM((512, 256), BF)]
@@ -537,11 +566,13 @@
     edge = first_columns(place, tile, rows, "edge", (labc, labr))
     moved = send(edge, lon_move(-1))
     cot_rows = exchange_rows(*fence(pieces[3:], (edge,)))
+    (wqo,) = fence((wqo,), (edge,))
     wqo_sib = flip(wqo, c=1)
+    (w12,) = fence((w12,), (wqo,))
+    w12 = flip(w12, yl=1, t=1)
     cot_edge = first_columns(place, cot, cot_rows, "cot_edge", (moved, wqo))
+    cot_moved = send(cot_edge, lon_move(-1))
     (w12,) = fence((w12,), (cot_edge,))
-    w12 = flip(w12, yl=1, t=1)
-    cot_moved = send(cot_edge, lon_move(-1))
 
     stage = [pltpu.VMEM((12, 56, D), F32), pltpu.VMEM((TOK, D), F32)]
     n1t, qkv, prob, heads, wo_full, mixed = call(
@@ -571,7 +602,7 @@
         name="mlp_own",
         limit=12,
     )
-    (w12,) = fence((w12,), (keep,))
+    w12 = join(place, w12, "join_mlp", (keep,))
     w12_sib = flip(w12, c=1)
     arrived = flip(away, c=1)
     out_band, tail, dm, keep_two, away_two = call(
@@ -585,7 +616,8 @@
         limit=12,
     )
     fc_cut = core_phase_two(keep, arrived, keep_two, flip(away_two, c=1))
-    fc_parts = x_phase(fc_cut)
+    kept, sent, kept_two, sent_two = fc_cut
+    first, second = flip(sent, x=1), flip(sent_two, x=3)
     out_moved = send(tail, lon_move(1))
     out = jnp.concatenate([out_moved, out_band[:, 6:]], 1)
     dqkv, dmt = call(
@@ -596,7 +628,11 @@
         flops=4 * 10**9,
         name="attend_back",
         limit=12,
-        after=(fc_cut[0], out_moved),
+        after=(kept,),
+    )
+    halves = [whole((2, 8, 16, 512))] * 4
+    own, own_sent, other, other_sent = call(
+        half_sum_kernel, (kept, first, kept_two, second), halves, name="half_sum"
     )
     at = call(
         attend_grads_kernel,
@@ -606,18 +642,23 @@
         place,
         name="attend_grads",
         limit=12,
-        after=(fc_parts[1], fc_parts[3]),
+        after=(own_sent, other_sent, out_moved),
     )
     keep, away = at
-    (away,) = fence((away,), fc_parts[2:3])
-    at_cut = core_phase(keep, away, ())
-    at_parts = x_phase(at_cut)
-    (total,) = call(
-        x_sum_kernel, (*fc_parts, *at_parts), [whole((2, 2, 8, 16, 768))], (), place, name="x_sum"
-    )
-    near, far, above = fence((out[6:9], out[9:12], out[3:6]), (total,))
+    arrived, arrived_two = flip(own_sent, x=3), flip(other_sent, x=1)
+    fc_cut = call(
+        x_sum_kernel, (own, arrived, other, arrived_two), [whole((8, 16, 512))] * 4, name="x_sum"
+    )
+    fc_parts = y_phase(fc_cut)
+    (at_total,) = call(
+        without(core_sum_kernel, 2, 1), (keep, flip(away, c=1)), [whole(keep.shape)], name="core_sum", after=fc_cut[:1]
+    )
+    at_parts = lax.all_to_all(at_total.reshape(16, 8, 16, 256), ("x", "tp", "yl"), 0, 0)
+    (total,) = call(xy_sum_kernel, (*fc_parts, at_parts), [whole((8, 16, 768))], name="xy_sum")
+    columns = reduce_over_z(total)
+    near, far, above = fence((out[6:9], out[9:12], out[3:6]), (columns,))
     near, far, above = flip(near, t=1), send(far, far_back), send(above, lat_move(1))
-    gq, go, g1, g2 = reduce_and_gather(place, total, (near, far, above))
+    gq, go, g1, g2 = gather_grads(place, columns, (near, far, above))
     out = jnp.where(
         t == 0,
         jnp.concatenate([far, out[0:6], near], 0),

time: 205 us -> 196 us (0.956)
  blocking collectives: 33.3 us -> 23.2 us
  waiting for transfers between devices: 56.4 us -> 62.7 us
  starting transfers between devices: 69 us -> 64.1 us
    all_to_all x2, blocking collectives: 33.3 us -> 23.2 us  [the longest x1 12.2 us: reduce_over_z(): parts = lax.all_to_all(total, 'z', 0, 0)]
    ppermute x26 -> x30, waiting for transfers between devices: 54 us -> 62.7 us  [send(): return lax.ppermute(value, AXES, pairs_of(move))]
    ppermute x26 -> x30, starting transfers between devices: 58 us -> 51 us  [send(): return lax.ppermute(value, AXES, pairs_of(move))]
    all_to_all x1 -> x2, waiting for transfers between devices: 2.39 us -> 0.01 us  [the longest x1 0.01 us: per_device(): lax.all_to_all(at_total.reshape(16, 8, 16, 256), ('x', 'tp', 'yl'), 0, 0)]
    all_to_all x1 -> x2, starting transfers between devices: 11 us -> 13.2 us  [the longest x1 7.13 us: per_device(): lax.all_to_all(at_total.reshape(16, 8, 16, 256), ('x', 'tp', 'yl'), 0, 0)]
    pallas_call x13 -> x16, Pallas kernels: 37.1 us -> 38.4 us  [call(): pl.pallas_call(kernel, out_shape=tuple(outs), in_specs=specs, out_specs=t...]
  transfers between devices with their start and end apart: 27 -> 32, of which waited for: 16 -> 16; matrix products, arithmetic and copies ran while one was open for 1% -> 1% of each run, Pallas kernels for 16% -> 16%
where the time goes in v5:
time: 196 us
  starting transfers between devices  64.1 us (33%)
  waiting for transfers between devices  62.7 us (32%)
  Pallas kernels  41.9 us (21%)
  blocking collectives  23.2 us (12%)
    ppermute x30, waiting for transfers between devices, send(): return lax.ppermute(value, AXES, pairs_of(move))  62.7 us
    ppermute x30, starting transfers between devices, send(): return lax.ppermute(value, AXES, pairs_of(move))  51 us
    pallas_call x16, Pallas kernels, call(): pl.pallas_call(kernel, out_shape=tuple(outs), in_specs=specs, out_specs=t...  38.4 us
    all_to_all x1, blocking collectives, reduce_over_z(): parts = lax.all_to_all(total, 'z', 0, 0)  12.2 us
    all_to_all x1, blocking collectives, reduce_over_z(): column = lax.all_to_all(chunks, 'z', 0, 0)  11 us
    all_to_all x1, starting transfers between devices, per_device(): lax.all_to_all(at_total.reshape(16, 8, 16, 256), ('x', 'tp', 'yl'), 0, 0)  7.13 us
    all_to_all x1, starting transfers between devices, gather_grads(): mine, = fence((lax.all_to_all(columns, ('x', 'yl'), 0, 0),), after)  6.04 us
  transfers between devices with their start and end apart: 32, of which 16 were waited for; matrix products, arithmetic and copies ran while one was open for 1% of the time, Pallas kernels for 16%

profile of v5, /device:TPU:1, one launch (start us, length us, event | category | flops | bytes accessed | tf_op | source)
XLA Modules:
  0.0 195.8 jit_solution(9669711151801458444)
XLA Ops:
  3.8 3.7 %collective-permute-start.4 = (bf16[4,256,256]{2,1,0:T(8,128)(2,1)S(1)}, bf16[4,256,256]{2,1,0:T(8,128)(2,1)S(1)}, u32[]{:S(2)}, u32[]{:S(2)}) collective-permute-start(bf16[4,256,256]{2,1,0:T(8,128)(2,1)S(1)} %get-tuple-element.61), channel_id=1, source_target_pairs={{0,33},{1,32},{2,35},{3,34},{4,37},{5,36},{6,39},{7,38},{8,41},{9,... | collective-permute-start | bytes 1572872 | tf_op jit(solution)/shard_map/ppermute | solution.py:44
  7.8 4.1 %collective-permute-start.1 = (bf16[3,48,512]{2,1,0:T(8,128)(2,1)S(1)}, bf16[3,48,512]{2,1,0:T(8,128)(2,1)S(1)}, u32[]{:S(2)}, u32[]{:S(2)}) collective-permute-start(bf16[3,48,512]{2,1,0:T(8,128)(2,1)S(1)} %get-tuple-element.59), channel_id=1, source_target_pairs={{0,225},{1,0},{2,227},{3,2},{4,229},{5,4},{6,231},{7,6},{8,233},{9... | collective-permute-start | bytes 442376 | tf_op jit(solution)/shard_map/ppermute | solution.py:44
  13.4 4.7 %collective-permute-done.1.refs_3_ = bf16[3,48,512]{2,1,0:T(8,128)(2,1)S(1)} collective-permute-done((bf16[3,48,512]{2,1,0:T(8,128)(2,1)S(1)}, bf16[3,48,512]{2,1,0:T(8,128)(2,1)S(1)}, u32[]{:S(2)}, u32[]{:S(2)}) %collective-permute-start.1) | collective-permute-done | bytes 147488 | tf_op jit(solution)/shard_map/ppermute | solution.py:44
  18.9 6.1 %collective-permute-done.4.refs_0_ = bf16[4,256,256]{2,1,0:T(8,128)(2,1)S(1)} collective-permute-done((bf16[4,256,256]{2,1,0:T(8,128)(2,1)S(1)}, bf16[4,256,256]{2,1,0:T(8,128)(2,1)S(1)}, u32[]{:S(2)}, u32[]{:S(2)}) %collective-permute-start.4) | collective-permute-done | bytes 524320 | tf_op jit(solution)/shard_map/ppermute | solution.py:44
  26.6 2.7 %collective-permute-start.10 = (bf16[2,128,512]{2,1,0:T(8,128)(2,1)S(1)}, bf16[2,128,512]{2,1,0:T(8,128)(2,1)S(1)}, u32[]{:S(2)}, u32[]{:S(2)}) collective-permute-start(bf16[2,128,512]{2,1,0:T(8,128)(2,1)S(1)} %fence.8), channel_id=1, source_target_pairs={{0,33},{1,32},{2,35},{3,34},{4,37},{5,36},{6,39},{7,38},{8,41},{9,... | collective-permute-start | bytes 786440 | tf_op jit(solution)/shard_map/ppermute | solution.py:44
  29.7 4.1 %collective-permute-start.7 = (bf16[3,48,512]{2,1,0:T(8,128)(2,1)S(1)}, bf16[3,48,512]{2,1,0:T(8,128)(2,1)S(1)}, u32[]{:S(2)}, u32[]{:S(2)}) collective-permute-start(bf16[3,48,512]{2,1,0:T(8,128)(2,1)S(1)} %get-tuple-element.66), channel_id=1, source_target_pairs={{0,225},{1,0},{2,227},{3,2},{4,229},{5,4},{6,231},{7,6},{8,233},{9... | collective-permute-start | bytes 442376 | tf_op jit(solution)/shard_map/ppermute | solution.py:44
  37.4 7.3 %collective-permute-start.9 = (bf16[12,6,512]{2,1,0:T(8,128)(2,1)S(1)}, bf16[12,6,512]{2,1,0:T(8,128)(2,1)S(1)}, u32[]{:S(2)}, u32[]{:S(2)}) collective-permute-start(bf16[12,6,512]{2,1,0:T(8,128)(2,1)S(1)} %cot_edge.1.refs_13_.refs_1_), channel_id=1, source_target_pairs={{0,30},{1,31},{2,0},{3,1},{4,2},{5,3},{6,4},{7,5},{8,6},{9,7},{10,... | collective-permute-start | bytes 221192 | tf_op jit(solution)/shard_map/ppermute | solution.py:44
  44.7 3.4 %collective-permute-start.13 = (bf16[2,128,512]{2,1,0:T(8,128)(2,1)S(1)}, bf16[2,128,512]{2,1,0:T(8,128)(2,1)S(1)}, u32[]{:S(2)}, u32[]{:S(2)}) collective-permute-start(bf16[2,128,512]{2,1,0:T(8,128)(2,1)S(1)} %fence.9.refs_1_), channel_id=1, source_target_pairs={{0,192},{1,193},{2,194},{3,195},{4,196},{5,197},{6,198},{7,199},{8... | collective-permute-start | bytes 786440 | tf_op jit(solution)/shard_map/ppermute | solution.py:44
  48.8 6.8 %attend.1 = (bf16[512,576]{1,0:T(8,128)(2,1)S(1)}, bf16[576,1536]{1,0:T(8,128)(2,1)S(1)}, bf16[32,144,144]{2,1,0:T(8,128)(2,1)S(1)}, bf16[576,512]{1,0:T(8,128)(...) custom-call(s32[5]{0:T(128)S(1)} %stack.23.place.refs_0_, bf16[12,48,512]{2,1,0:T(8,128)(2,1)S(1)} %bitcast.24, ...), custom_call_target="tpu_custom_call" | custom-call | flops 3000000000 | bytes 8982548 | tf_op jit(solution)/shard_map/attend/pallas_call | solution.py:437
  55.6 6.7 %mlp_own.1 = (bf16[576,512]{1,0:T(8,128)(2,1)S(1)}, bf16[512,576]{1,0:T(8,128)(2,1)S(1)}, bf16[576,512]{1,0:T(8,128)(2,1)S(1)}, bf16[512,576]{1,0:T(8,128)(2,1)S...) custom-call(s32[5]{0:T(128)S(1)} %stack.23.place.refs_0_, ...), custom_call_target="tpu_custom_call" | custom-call | flops 4000000000 | bytes 10610708 | tf_op jit(solution)/shard_map/mlp_own/pallas_call | solution.py:437
  66.3 6.5 %mlp_other.1 = (bf16[12,48,512]{2,1,0:T(8,128)(2,1)S(1)}, bf16[12,6,512]{2,1,0:T(8,128)(2,1)S(1)}, bf16[576,512]{1,0:T(8,128)(2,1)S(1)}, bf16[4,2,8,16,512]{4,3,...) custom-call(s32[5]{0:T(128)S(1)} %stack.23.place.refs_0_, bf16[576,512]{1,0:T(8,128)(2,1)S(1)} %get-tuple-element.68.mixed_ref, ...), custom_call_target="tpu_custom_call" | custom-call | flops 4000000000 | bytes 10758164 | tf_op jit(solution)/shard_map/mlp_other/pallas_call | solution.py:437
  80.5 8.0 %attend_back.1 = (bf16[576,1536]{1,0:T(8,128)(2,1)S(1)}, bf16[512,576]{1,0:T(8,128)(2,1)S(1)}) custom-call(bf16[576,512]{1,0:T(8,128)(2,1)S(1)} %get-tuple-element.94.dm_ref, bf16[32,144,144]{2,1,0:T(8,128)(2,1)S(1)} %get-tuple-element.95.prob_ref, bf16[576,1536]{1,0:T(8,128)(2,1)S(1)} %get-tuple-element.96.qkv_ref, ...), custom_call_target="tpu_custom_call" | custom-call | flops 4000000000 | bytes 7094272 | tf_op jit(solution)/shard_map/attend_back/pallas_call | solution.py:437
  97.4 7.2 %collective-permute-done.20.arrived = bf16[2,8,16,512]{3,2,1,0:T(8,128)(2,1)S(1)} collective-permute-done((bf16[2,8,16,512]{3,2,1,0:T(8,128)(2,1)S(1)}, bf16[2,8,16,512]{3,2,1,0:T(8,128)(2,1)S(1)}, u32[]{:S(2)}, u32[]{:S(2)}) %collective-permute-start.20) | collective-permute-done | bytes 262176 | tf_op jit(solution)/shard_map/ppermute | solution.py:44
  106.3 7.1 %all-to-all-start = ((bf16[16,8,16,256]{3,2,1,0:T(8,128)(2,1)}), bf16[16,8,16,256]{3,2,1,0:T(8,128)(2,1)S(1)}, u32[]{:S(2)}, u32[]{:S(2)}) async-start(bf16[16,8,16,256]{3,2,1,0:T(8,128)(2,1)} %bitcast.10), calls=%async_computation | async-start | bytes 2097152 | tf_op jit(solution)/shard_map/all_to_all | solution.py:656
  117.3 6.0 %collective-permute-done.22.refs_1_ = bf16[8,16,512]{2,1,0:T(8,128)(2,1)S(1)} collective-permute-done((bf16[8,16,512]{2,1,0:T(8,128)(2,1)S(1)}, bf16[8,16,512]{2,1,0:T(8,128)(2,1)S(1)}, u32[]{:S(2)}, u32[]{:S(2)}) %collective-permute-start.22) | collective-permute-done | bytes 131104 | tf_op jit(solution)/shard_map/ppermute | solution.py:44
  123.3 9.5 %collective-permute-done.23.refs_2_ = bf16[8,16,512]{2,1,0:T(8,128)(2,1)S(1)} collective-permute-done((bf16[8,16,512]{2,1,0:T(8,128)(2,1)S(1)}, bf16[8,16,512]{2,1,0:T(8,128)(2,1)S(1)}, u32[]{:S(2)}, u32[]{:S(2)}) %collective-permute-start.23) | collective-permute-done | bytes 131104 | tf_op jit(solution)/shard_map/ppermute | solution.py:44
  133.0 12.2 %all_to_all.20.parts = bf16[8,16,768]{2,1,0:T(8,128)(2,1)S(1)} all-to-all(bf16[8,16,768]{2,1,0:T(8,128)(2,1)S(1)} %xy_sum.1), channel_id=1, replica_groups=mesh['x'=4,'yl'=2,'z'=8,'c'=2,'tp'=2] {'z'}, dimensions={0} | all-to-all | bytes 393216 | tf_op jit(solution)/shard_map/all_to_all | solution.py:536
  145.2 11.0 %all_to_all.21.part = bf16[8,16,768]{2,1,0:T(8,128)(2,1)S(1)} all-to-all(bf16[8,16,768]{2,1,0:T(8,128)(2,1)S(1)} %last_sum.1), channel_id=1, replica_groups=mesh['x'=4,'yl'=2,'z'=8,'c'=2,'tp'=2] {'z'}, dimensions={0} | all-to-all | bytes 393216 | tf_op jit(solution)/shard_map/all_to_all | solution.py:538
  157.6 6.0 %all-to-all-start.3 = ((bf16[8,8,16,768]{3,2,1,0:T(8,128)(2,1)}), bf16[8,8,16,768]{3,2,1,0:T(8,128)(2,1)S(1)}, u32[]{:S(2)}, u32[]{:S(2)}) async-start(bf16[8,8,16,768]{3,2,1,0:T(8,128)(2,1)} %copies.1.refs_3_), calls=%async_computation.3 | async-start | bytes 3145728 | tf_op jit(solution)/shard_map/all_to_all | solution.py:544
  165.8 2.8 %collective-permute-start.27 = (bf16[3,48,512]{2,1,0:T(8,128)(2,1)S(1)}, bf16[3,48,512]{2,1,0:T(8,128)(2,1)S(1)}, u32[]{:S(2)}, u32[]{:S(2)}) collective-permute-start(bf16[3,48,512]{2,1,0:T(8,128)(2,1)S(1)} %get-tuple-element.105), channel_id=1, source_target_pairs={{0,1},{1,0},{2,3},{3,2},{4,5},{5,4},{6,7},{7,6},{8,9},{9,8},{10,11... | collective-permute-start | bytes 442376 | tf_op jit(solution)/shard_map/ppermute | solution.py:44
  169.3 13.5 %collective-permute-done.26.refs_2_ = bf16[3,48,512]{2,1,0:T(8,128)(2,1)S(1)} collective-permute-done((bf16[3,48,512]{2,1,0:T(8,128)(2,1)S(1)}, bf16[3,48,512]{2,1,0:T(8,128)(2,1)S(1)}, u32[]{:S(2)}, u32[]{:S(2)}) %collective-permute-start.26) | collective-permute-done | bytes 147488 | tf_op jit(solution)/shard_map/ppermute | solution.py:44
  182.8 3.4 %collective-permute-done.27.refs_1_ = bf16[3,48,512]{2,1,0:T(8,128)(2,1)S(1)} collective-permute-done((bf16[3,48,512]{2,1,0:T(8,128)(2,1)S(1)}, bf16[3,48,512]{2,1,0:T(8,128)(2,1)S(1)}, u32[]{:S(2)}, u32[]{:S(2)}) %collective-permute-start.27) | collective-permute-done | bytes 147488 | tf_op jit(solution)/shard_map/ppermute | solution.py:44
  186.2 3.8 %collective-permute-start.29 = (bf16[8,8,16,768]{3,2,1,0:T(8,128)(2,1)S(1)}, bf16[8,8,16,768]{3,2,1,0:T(8,128)(2,1)S(1)}, u32[]{:S(2)}, u32[]{:S(2)}) collective-permute-start(bf16[8,8,16,768]{3,2,1,0:T(8,128)(2,1)S(1)} %fence.11.mine), channel_id=1, source_target_pairs={{0,2},{1,3},{2,0},{3,1},{4,6},{5,7},{6,4},{7,5},{8,10},{9,11},{10,... | collective-permute-start | bytes 4718600 | tf_op jit(solution)/shard_map/ppermute | solution.py:44
  193.0 2.8 %place.1 = (bf16[3,512,256]{2,1,0:T(8,128)(2,1)}, bf16[256,512]{1,0:T(8,128)(2,1)}, bf16[512,1024]{1,0:T(8,128)(2,1)}, bf16[1024,512]{1,0:T(8,128)(2,1)}) custom-call(s32[5]{0:T(128)S(1)} %stack.23.place.refs_0_, bf16[8,8,16,768]{3,2,1,0:T(8,128)(2,1)S(1)} %fence.11.mine, bf16[8,8,16,768]{3,2,1,0:T(8,128)(2,1)S(1)} %collective-permute-done.29.sib), custom_call_target="tpu_custom_call" | custom-call | bytes 6291476 | tf_op jit(solution)/shard_map/place/pallas_call | solution.py:437
  (100 shorter events, 45.3 us)
Async XLA Ops:
  3.8 21.2 %collective-permute-start.4 = (bf16[4,256,256]{2,1,0:T(8,128)(2,1)S(1)}, bf16[4,256,256]{2,1,0:T(8,128)(2,1)S(1)}, u32[]{:S(2)}, u32[]{:S(2)}) collective-permute-start(bf16[4,256,256]{2,1,0:T(8,128)(2,1)S(1)} %get-tuple-element.61), channel_id=1, source_target_pairs={{0,33},{1,32},{2,35},{3,34},{4,37},{5,36},{6,39},{7,38},{8,41},{9,... | collective-permute-start | bytes 1572872 | tf_op jit(solution)/shard_map/ppermute | solution.py:44
  7.8 10.4 %collective-permute-start.1 = (bf16[3,48,512]{2,1,0:T(8,128)(2,1)S(1)}, bf16[3,48,512]{2,1,0:T(8,128)(2,1)S(1)}, u32[]{:S(2)}, u32[]{:S(2)}) collective-permute-start(bf16[3,48,512]{2,1,0:T(8,128)(2,1)S(1)} %get-tuple-element.59), channel_id=1, source_target_pairs={{0,225},{1,0},{2,227},{3,2},{4,229},{5,4},{6,231},{7,6},{8,233},{9... | collective-permute-start | bytes 442376 | tf_op jit(solution)/shard_map/ppermute | solution.py:44
  25.0 23.8 %collective-permute-start.5 = (bf16[4,256,256]{2,1,0:T(8,128)(2,1)S(1)}, bf16[4,256,256]{2,1,0:T(8,128)(2,1)S(1)}, u32[]{:S(2)}, u32[]{:S(2)}) collective-permute-start(bf16[4,256,256]{2,1,0:T(8,128)(2,1)S(1)} %fence.6.refs_6_.refs_11_.refs_1_), channel_id=1, source_target_pairs={{0,2},{1,3},{2,0},{3,1},{4,6},{5,7},{6,4},{7,5},{8,10},{9,11},{10,... | collective-permute-start | bytes 1572872 | tf_op jit(solution)/shard_map/ppermute | solution.py:44
  26.6 18.1 %collective-permute-start.10 = (bf16[2,128,512]{2,1,0:T(8,128)(2,1)S(1)}, bf16[2,128,512]{2,1,0:T(8,128)(2,1)S(1)}, u32[]{:S(2)}, u32[]{:S(2)}) collective-permute-start(bf16[2,128,512]{2,1,0:T(8,128)(2,1)S(1)} %fence.8), channel_id=1, source_target_pairs={{0,33},{1,32},{2,35},{3,34},{4,37},{5,36},{6,39},{7,38},{8,41},{9,... | collective-permute-start | bytes 786440 | tf_op jit(solution)/shard_map/ppermute | solution.py:44
  29.7 7.2 %collective-permute-start.7 = (bf16[3,48,512]{2,1,0:T(8,128)(2,1)S(1)}, bf16[3,48,512]{2,1,0:T(8,128)(2,1)S(1)}, u32[]{:S(2)}, u32[]{:S(2)}) collective-permute-start(bf16[3,48,512]{2,1,0:T(8,128)(2,1)S(1)} %get-tuple-element.66), channel_id=1, source_target_pairs={{0,225},{1,0},{2,227},{3,2},{4,229},{5,4},{6,231},{7,6},{8,233},{9... | collective-permute-start | bytes 442376 | tf_op jit(solution)/shard_map/ppermute | solution.py:44
  37.4 18.2 %collective-permute-start.9 = (bf16[12,6,512]{2,1,0:T(8,128)(2,1)S(1)}, bf16[12,6,512]{2,1,0:T(8,128)(2,1)S(1)}, u32[]{:S(2)}, u32[]{:S(2)}) collective-permute-start(bf16[12,6,512]{2,1,0:T(8,128)(2,1)S(1)} %cot_edge.1.refs_13_.refs_1_), channel_id=1, source_target_pairs={{0,30},{1,31},{2,0},{3,1},{4,2},{5,3},{6,4},{7,5},{8,6},{9,7},{10,... | collective-permute-start | bytes 221192 | tf_op jit(solution)/shard_map/ppermute | solution.py:44
  44.7 17.6 %collective-permute-start.13 = (bf16[2,128,512]{2,1,0:T(8,128)(2,1)S(1)}, bf16[2,128,512]{2,1,0:T(8,128)(2,1)S(1)}, u32[]{:S(2)}, u32[]{:S(2)}) collective-permute-start(bf16[2,128,512]{2,1,0:T(8,128)(2,1)S(1)} %fence.9.refs_1_), channel_id=1, source_target_pairs={{0,192},{1,193},{2,194},{3,195},{4,196},{5,197},{6,198},{7,199},{8... | collective-permute-start | bytes 786440 | tf_op jit(solution)/shard_map/ppermute | solution.py:44
  48.2 14.2 %collective-permute-start.12 = (bf16[2,128,512]{2,1,0:T(8,128)(2,1)S(1)}, bf16[2,128,512]{2,1,0:T(8,128)(2,1)S(1)}, u32[]{:S(2)}, u32[]{:S(2)}) collective-permute-start(bf16[2,128,512]{2,1,0:T(8,128)(2,1)S(1)} %fence.9.refs_1_), channel_id=1, source_target_pairs={{0,128},{1,129},{2,130},{3,131},{4,132},{5,133},{6,134},{7,135},{8... | collective-permute-start | bytes 786440 | tf_op jit(solution)/shard_map/ppermute | solution.py:44
  48.2 14.2 %collective-permute-start.11 = (bf16[2,128,512]{2,1,0:T(8,128)(2,1)S(1)}, bf16[2,128,512]{2,1,0:T(8,128)(2,1)S(1)}, u32[]{:S(2)}, u32[]{:S(2)}) collective-permute-start(bf16[2,128,512]{2,1,0:T(8,128)(2,1)S(1)} %fence.9.refs_1_), channel_id=1, source_target_pairs={{0,64},{1,65},{2,66},{3,67},{4,68},{5,69},{6,70},{7,71},{8,72},{9,... | collective-permute-start | bytes 786440 | tf_op jit(solution)/shard_map/ppermute | solution.py:44
  64.0 9.2 %collective-permute-start.16 = (bf16[4,2,8,16,512]{4,3,2,1,0:T(8,128)(2,1)S(1)}, bf16[4,2,8,16,512]{4,3,2,1,0:T(8,128)(2,1)S(1)}, u32[]{:S(2)}, u32[]{:S(2)}) collective-permute-start(bf16[4,2,8,16,512]{4,3,2,1,0:T(8,128)(2,1)S(1)} %get-tuple-element.79), channel_id=1, source_target_pairs={{0,2},{1,3},{2,0},{3,1},{4,6},{5,7},{6,4},{7,5},{8,10},{9,11},{10,... | collective-permute-start | bytes 3145736 | tf_op jit(solution)/shard_map/ppermute | solution.py:44
  76.0 13.2 %collective-permute-start.18 = (bf16[2,2,8,16,512]{4,3,2,1,0:T(8,128)(2,1)S(1)}, bf16[2,2,8,16,512]{4,3,2,1,0:T(8,128)(2,1)S(1)}, u32[]{:S(2)}, u32[]{:S(2)}) collective-permute-start(bf16[2,2,8,16,512]{4,3,2,1,0:T(8,128)(2,1)S(1)} %get-tuple-element.83), channel_id=1, source_target_pairs={{0,64},{1,65},{2,66},{3,67},{4,68},{5,69},{6,70},{7,71},{8,72},{9,... | collective-permute-start | bytes 1572872 | tf_op jit(solution)/shard_map/ppermute | solution.py:44
  77.3 14.0 %collective-permute-start.19 = (bf16[2,2,8,16,512]{4,3,2,1,0:T(8,128)(2,1)S(1)}, bf16[2,2,8,16,512]{4,3,2,1,0:T(8,128)(2,1)S(1)}, u32[]{:S(2)}, u32[]{:S(2)}) collective-permute-start(bf16[2,2,8,16,512]{4,3,2,1,0:T(8,128)(2,1)S(1)} %get-tuple-element.85), channel_id=1, source_target_pairs={{0,192},{1,193},{2,194},{3,195},{4,196},{5,197},{6,198},{7,199},{8... | collective-permute-start | bytes 1572872 | tf_op jit(solution)/shard_map/ppermute | solution.py:44
  79.1 12.5 %collective-permute-start.15 = (bf16[12,6,512]{2,1,0:T(8,128)(2,1)S(1)}, bf16[12,6,512]{2,1,0:T(8,128)(2,1)S(1)}, u32[]{:S(2)}, u32[]{:S(2)}) collective-permute-start(bf16[12,6,512]{2,1,0:T(8,128)(2,1)S(1)} %get-tuple-element.77), channel_id=1, source_target_pairs={{0,2},{1,3},{2,4},{3,5},{4,6},{5,7},{6,8},{7,9},{8,10},{9,11},{10,... | collective-permute-start | bytes 221192 | tf_op jit(solution)/shard_map/ppermute | solution.py:44
  93.9 11.1 %collective-permute-start.25 = (bf16[4,2,2,8,16,256]{5,4,3,2,1,0:T(8,128)(2,1)S(1)}, bf16[4,2,2,8,16,256]{5,4,3,2,1,0:T(8,128)(2,1)S(1)}, u32[]{:S(2)}, u32[]{:S(2)}) collective-permute-start(bf16[4,2,2,8,16,256]{5,4,3,2,1,0:T(8,128)(2,1)S(1)} %get-tuple-element.103), channel_id=1, source_target_pairs={{0,2},{1,3},{2,0},{3,1},{4,6},{5,7},{6,4},{7,5},{8,10},{9,11},{10,... | collective-permute-start | bytes 3145736 | tf_op jit(solution)/shard_map/ppermute | solution.py:44
  95.5 9.1 %collective-permute-start.20 = (bf16[2,8,16,512]{3,2,1,0:T(8,128)(2,1)S(1)}, bf16[2,8,16,512]{3,2,1,0:T(8,128)(2,1)S(1)}, u32[]{:S(2)}, u32[]{:S(2)}) collective-permute-start(bf16[2,8,16,512]{3,2,1,0:T(8,128)(2,1)S(1)} %get-tuple-element.87.first), channel_id=1, source_target_pairs={{0,192},{1,193},{2,194},{3,195},{4,196},{5,197},{6,198},{7,199},{8... | collective-permute-start | bytes 786440 | tf_op jit(solution)/shard_map/ppermute | solution.py:44
  97.4 7.5 %collective-permute-start.21 = (bf16[2,8,16,512]{3,2,1,0:T(8,128)(2,1)S(1)}, bf16[2,8,16,512]{3,2,1,0:T(8,128)(2,1)S(1)}, u32[]{:S(2)}, u32[]{:S(2)}) collective-permute-start(bf16[2,8,16,512]{3,2,1,0:T(8,128)(2,1)S(1)} %get-tuple-element.89.second), channel_id=1, source_target_pairs={{0,64},{1,65},{2,66},{3,67},{4,68},{5,69},{6,70},{7,71},{8,72},{9,... | collective-permute-start | bytes 786440 | tf_op jit(solution)/shard_map/ppermute | solution.py:44
  106.3 26.6 %all-to-all-start = ((bf16[16,8,16,256]{3,2,1,0:T(8,128)(2,1)}), bf16[16,8,16,256]{3,2,1,0:T(8,128)(2,1)S(1)}, u32[]{:S(2)}, u32[]{:S(2)}) async-start(bf16[16,8,16,256]{3,2,1,0:T(8,128)(2,1)} %bitcast.10), calls=%async_computation | async-start | bytes 2097152 | tf_op jit(solution)/shard_map/all_to_all | solution.py:656
  113.4 9.9 %collective-permute-start.22 = (bf16[8,16,512]{2,1,0:T(8,128)(2,1)S(1)}, bf16[8,16,512]{2,1,0:T(8,128)(2,1)S(1)}, u32[]{:S(2)}, u32[]{:S(2)}) collective-permute-start(bf16[8,16,512]{2,1,0:T(8,128)(2,1)S(1)} %get-tuple-element.91), channel_id=1, source_target_pairs={{0,32},{1,33},{2,34},{3,35},{4,36},{5,37},{6,38},{7,39},{8,40},{9,... | collective-permute-start | bytes 393224 | tf_op jit(solution)/shard_map/ppermute | solution.py:44
  114.8 18.1 %collective-permute-start.23 = (bf16[8,16,512]{2,1,0:T(8,128)(2,1)S(1)}, bf16[8,16,512]{2,1,0:T(8,128)(2,1)S(1)}, u32[]{:S(2)}, u32[]{:S(2)}) collective-permute-start(bf16[8,16,512]{2,1,0:T(8,128)(2,1)S(1)} %get-tuple-element.92), channel_id=1, source_target_pairs={{0,1},{1,0},{2,3},{3,2},{4,5},{5,4},{6,7},{7,6},{8,9},{9,8},{10,11... | collective-permute-start | bytes 393224 | tf_op jit(solution)/shard_map/ppermute | solution.py:44
  117.2 15.7 %collective-permute-start.24 = (bf16[8,16,512]{2,1,0:T(8,128)(2,1)S(1)}, bf16[8,16,512]{2,1,0:T(8,128)(2,1)S(1)}, u32[]{:S(2)}, u32[]{:S(2)}) collective-permute-start(bf16[8,16,512]{2,1,0:T(8,128)(2,1)S(1)} %get-tuple-element.93), channel_id=1, source_target_pairs={{0,33},{1,32},{2,35},{3,34},{4,37},{5,36},{6,39},{7,38},{8,41},{9,... | collective-permute-start | bytes 393224 | tf_op jit(solution)/shard_map/ppermute | solution.py:44
  157.6 28.6 %all-to-all-start.3 = ((bf16[8,8,16,768]{3,2,1,0:T(8,128)(2,1)}), bf16[8,8,16,768]{3,2,1,0:T(8,128)(2,1)S(1)}, u32[]{:S(2)}, u32[]{:S(2)}) async-start(bf16[8,8,16,768]{3,2,1,0:T(8,128)(2,1)} %copies.1.refs_3_), calls=%async_computation.3 | async-start | bytes 3145728 | tf_op jit(solution)/shard_map/all_to_all | solution.py:544
  165.4 17.4 %collective-permute-start.26 = (bf16[3,48,512]{2,1,0:T(8,128)(2,1)S(1)}, bf16[3,48,512]{2,1,0:T(8,128)(2,1)S(1)}, u32[]{:S(2)}, u32[]{:S(2)}) collective-permute-start(bf16[3,48,512]{2,1,0:T(8,128)(2,1)S(1)} %get-tuple-element.104), channel_id=1, source_target_pairs={{0,1},{1,32},{2,3},{3,34},{4,5},{5,36},{6,7},{7,38},{8,9},{9,40},{... | collective-permute-start | bytes 442376 | tf_op jit(solution)/shard_map/ppermute | solution.py:44
  165.8 20.4 %collective-permute-start.27 = (bf16[3,48,512]{2,1,0:T(8,128)(2,1)S(1)}, bf16[3,48,512]{2,1,0:T(8,128)(2,1)S(1)}, u32[]{:S(2)}, u32[]{:S(2)}) collective-permute-start(bf16[3,48,512]{2,1,0:T(8,128)(2,1)S(1)} %get-tuple-element.105), channel_id=1, source_target_pairs={{0,1},{1,0},{2,3},{3,2},{4,5},{5,4},{6,7},{7,6},{8,9},{9,8},{10,11... | collective-permute-start | bytes 442376 | tf_op jit(solution)/shard_map/ppermute | solution.py:44
  168.6 17.6 %collective-permute-start.28 = (bf16[3,48,512]{2,1,0:T(8,128)(2,1)S(1)}, bf16[3,48,512]{2,1,0:T(8,128)(2,1)S(1)}, u32[]{:S(2)}, u32[]{:S(2)}) collective-permute-start(bf16[3,48,512]{2,1,0:T(8,128)(2,1)S(1)} %get-tuple-element.106), channel_id=1, source_target_pairs={{1,33},{3,35},{5,37},{7,39},{9,41},{11,43},{13,45},{15,47},{17,49}... | collective-permute-start | bytes 442376 | tf_op jit(solution)/shard_map/ppermute | solution.py:44
  (18 other events, 171.7 us)
